TPU v7x, 32 devices: a whole 2x2x4 slice. The times are simulated.
32 devices in a mesh: groups: 2 (over x), lon: 8 (over z, y), lat: 2 (over core).
Axes of the slice: x: 2, y: 2, z: 4, core: 2. Of those that a mesh axis runs over, the one named last changes fastest.
Arguments:
- lam_in: float32 [2048, 1024], P(('groups', 'lat'), 'lon'), parts along dimension 0, may hold values from -6 to 6
- flux_east: float32 [2048, 1024], P(('groups', 'lat'), 'lon'), parts along dimension 0, may hold values from -6 to 6
- flux_north: float32 [2048, 1024], P(('groups', 'lat'), 'lon'), parts along dimension 0, may hold values from -6 to 6
- depth: float32 [2048, 1024], P(('groups', 'lat'), 'lon'), parts along dimension 0, may hold values from 0.2 to 2
- drag: float32 [2048, 1024], P(('groups', 'lat'), 'lon'), parts along dimension 0, may hold values from 0.05 to 1
- ocean: int32 [2048, 1024], P(('groups', 'lat'), 'lon'), parts along dimension 0, may hold values 0 or 1
- coarse_of: int32 [1024, 1024], P('lat', 'lon'), may hold values from 0 to 8191, as said below
- green: float32 [8192, 8192], P(('lon', 'lat')), may hold values from -3 to 3
Outputs:
- lam_out: float32 [2048, 1024], P(('groups', 'lat'), 'lon'), parts along dimension 0
- east_out: float32 [2048, 1024], P(('groups', 'lat'), 'lon'), parts along dimension 0
- north_out: float32 [2048, 1024], P(('groups', 'lat'), 'lon'), parts along dimension 0
- bands: float32 [3, 4, 512, 1024], P(None, ('groups', 'lat'), 'lon'), parts along dimension 1
There are 2 independent parts, one for each index of `groups`. A program takes and returns all parts, laid end to end along the dimension named above; an argument that names none is the same for every part. Nothing has to cross between parts.
Inputs may be any that keep to these rules, and one draw needn't show every extreme that they name: `coarse_of`: block (latitude band b, longitude band a) of 512 x 128 cells holds only the coarse points (a * 2 + b) * 512 to that plus 512 - 1; the first 512 cells of each block in row-major order hold these points in order, so that every point has a cell.
All inputs are finite; a program needn't handle non-finite values. No bound on the sum of `ocean` on one device may be relied on, other than what follows from the above.
Results may differ from a plain program's by a relative error of at most 0.0001.
Values sent between devices are 32-bit elements; how exact they have to be, the bound alone decides.
No kernel may reach another device: no remote copies, remote signals or barrier semaphores. Data moves between devices by JAX's collectives and lax.ppermute only.
A program may use at most 64 MiB of HBM per device.

v0:
```python
import math

import jax
import jax.numpy as jnp
from jax import lax
from jax.sharding import PartitionSpec as P

ITERS = 2


flux_ratio = 0.25
slope_ratio = 0.25
drag_step = 1.0
attract_coef = 0.5


def extended(block, sides, width, periodic):
    for axis, dim in sides:
        count = lax.axis_size(axis)
        forward = [(i, i + 1) for i in range(count - 1)]
        if periodic:
            forward.append((count - 1, 0))
        backward = [(target, source) for source, target in forward]
        low = lax.ppermute(
            lax.slice_in_dim(block, block.shape[dim] - width, None, axis=dim), axis, forward
        )
        high = lax.ppermute(lax.slice_in_dim(block, 0, width, axis=dim), axis, backward)
        block = jnp.concatenate([low, block, high], axis=dim)
    return block


def rim_lon(stack):
    return extended(stack, (("lon", 2),), 1, True)


def rim_lat(stack):
    return extended(stack, (("lat", 1),), 1, False)


def one_hot(ids, point_iota):
    return (ids[:, None] == point_iota).astype(jnp.float32)


def body(lam_in, flux_east, flux_north, depth, drag, ocean, coarse_of, green):
    ocean_f = ocean.astype(jnp.float32)
    rows, cols = lam_in.shape
    points = green.shape[0]
    statics = jnp.stack([depth, drag, ocean_f])
    wide = rim_lon(statics)
    tall = rim_lat(statics)
    west_side = wide[:, :, :-1]
    east_side = wide[:, :, 1:]
    depth_u = 0.5 * (west_side[0] + east_side[0])
    damp_u = west_side[2] * east_side[2] / (1.0 + drag_step * 0.5 * (west_side[1] + east_side[1]))
    south_side = tall[:, :-1]
    north_side = tall[:, 1:]
    depth_v = 0.5 * (south_side[0] + north_side[0])
    damp_v = (
        south_side[2] * north_side[2] / (1.0 + drag_step * 0.5 * (south_side[1] + north_side[1]))
    )
    block_rows = math.gcd(rows, 64)
    block_count = rows // block_rows
    local_ids = (coarse_of % points).reshape(block_count, block_rows * cols)
    point_iota = lax.broadcasted_iota(jnp.int32, (1, points), 1)

    def count_block(total, ids):
        return (total + jnp.sum(one_hot(ids, point_iota), axis=0), None)

    counts, _ = lax.scan(count_block, jnp.zeros((points,), jnp.float32), local_ids)

    def load_block(total, pair):
        ids, values = pair
        return (
            total + jnp.dot(values, one_hot(ids, point_iota), precision=lax.Precision.HIGHEST),
            None,
        )

    lam, east, north = (lam_in, flux_east, flux_north)
    for step in range(ITERS):
        wide_state = rim_lon(jnp.stack([lam, east]))
        tall_state = rim_lat(jnp.stack([lam, north]))
        lam_wide = wide_state[0]
        lam_tall = tall_state[0]
        adj_u = damp_u * (
            wide_state[1][:, :-1] + flux_ratio * depth_u * (lam_wide[:, 1:] - lam_wide[:, :-1])
        )
        adj_v = damp_v * (
            tall_state[1][:-1] + flux_ratio * depth_v * (lam_tall[1:] - lam_tall[:-1])
        )
        source = slope_ratio * (adj_u[:, :-1] - adj_u[:, 1:] + adj_v[:-1] - adj_v[1:])
        source_blocks = source.reshape(block_count, block_rows * cols)
        sums, _ = lax.scan(
            load_block, jnp.zeros((points,), jnp.float32), (local_ids, source_blocks)
        )
        loads = sums / counts
        potential = jnp.dot(
            green,
            lax.all_gather(loads, ("lon", "lat"), axis=0, tiled=True),
            precision=lax.Precision.HIGHEST,
        )
        spread = lax.map(
            lambda ids: jnp.dot(
                one_hot(ids, point_iota), potential, precision=lax.Precision.HIGHEST
            ),
            local_ids,
        )
        lam = ocean_f * (lam + source - attract_coef * spread.reshape(rows, cols))
        east = adj_u[:, 1:]
        north = adj_v[1:]
    tall_last = rim_lat(lam[None])[0]
    slope_y = tall_last[2:] - lam
    wide_last = rim_lon(lam[None])[0]
    slope_x = wide_last[:, 2:] - lam
    payload = jnp.stack([lam, slope_x, slope_y])
    banded = lax.all_to_all(payload, "lon", split_axis=1, concat_axis=2, tiled=True)
    bands = banded.reshape(3, 1, banded.shape[1], banded.shape[2])
    return (lam, east, north, bands)


def solution(mesh):
    in_specs = (
        P(("groups", "lat"), "lon"),
        P(("groups", "lat"), "lon"),
        P(("groups", "lat"), "lon"),
        P(("groups", "lat"), "lon"),
        P(("groups", "lat"), "lon"),
        P(("groups", "lat"), "lon"),
        P("lat", "lon"),
        P(("lon", "lat"), None),
    )
    out_specs = (
        P(("groups", "lat"), "lon"),
        P(("groups", "lat"), "lon"),
        P(("groups", "lat"), "lon"),
        P(None, ("groups", "lat"), "lon", None),
    )
    return jax.shard_map(body, mesh=mesh, in_specs=in_specs, out_specs=out_specs, check_vma=False)
```

profile of v0, /device:TPU:0, one launch (start us, length us, event | category | flops | bytes accessed | tf_op | source)
XLA Modules:
  0.0 508.4 jit_solution(10006310712397546343)
XLA Ops:
  18.2 16.1 %while.58 = (s32[]{:T(128)}, f32[512]{0:T(512)S(1)}, s32[8,8192]{1,0:T(8,128)S(1)}, s32[]{:T(128)}, s32[]{:T(128)}) while((s32[]{:T(128)}, f32[512]{0:T(512)S(1)}, s32[8,8192]{1,0:T(8,128)S(1)}, s32[]{:T(128)}, s32[]{:T(128)}) %tuple.113), condition=%wide.region_4.5_spmd.clone, body=%wide.region_2.4_spmd.clone.sunk | while | flops 12583427 | bytes 106579 | solution.py:69
  42.5 17.0 %collective-permute-done.2 = f32[2,512,1]{2,1,0:T(8,128)S(1)} collective-permute-done((f32[2,512,1]{2,1,0:T(8,128)}, f32[2,512,1]{2,1,0:T(8,128)S(1)}, u32[]{:S(2)}, u32[]{:S(2)}) %collective-permute-start.2) | collective-permute-done | bytes 4128 | tf_op jit(solution)/shard_map/ppermute | solution.py:24
  72.1 57.6 %while.57 = (s32[]{:T(128)}, f32[512]{0:T(512)S(1)}, f32[8,8192]{1,0:T(8,128)}, s32[8,8192]{1,0:T(8,128)}, s32[]{:T(128)}, /*index=5*/s32[]{:T(128)}) while((s32[]{:T(128)}, f32[512]{0:T(512)S(1)}, f32[8,8192]{1,0:T(8,128)}, s32[8,8192]{1,0:T(8,128)}, s32[]{:T(128)}, /*index=5*/s32[]{:T(128)}) %tuple.125), condition=%wide.region_1.2_spmd.clone, body=%wide.region_0.1_spmd.clone.sunk | while | flops 54526976 | bytes 139359 | solution.py:92
  129.7 21.8 %all-gather = f32[16,1,512]{2,1,0:T(1,128)S(1)} all-gather(f32[1,1,512]{2,1,0:T(1,128)S(1)} %bitcast.162), channel_id=1, replica_groups=mesh['groups'=2,'lon'=8,'lat'=2] {'lon','lat'}, dimensions={0}, use_global_device_ids=true | all-gather | bytes 34816 | tf_op jit(solution)/shard_map/all_gather | solution.py:98
  151.5 17.1 %fusion.66 = f32[1,512]{1,0:T(1,128)S(1)} fusion(f32[8192,1]{0,1:T(1,128)S(1)} %bitcast.157, f32[512,8192]{1,0:T(8,128)} %param.25), kind=kOutput, calls=%fused_computation.130 | convolution fusion | flops 50331648 | bytes 16812032 | tf_op jit(solution)/shard_map/dot_general | solution.py:96
  169.3 91.7 %while.55 = (s32[]{:T(128)}, f32[8,8192]{1,0:T(8,128)}, s32[8,8192]{1,0:T(8,128)}, f32[512]{0:T(512)S(1)}, s32[]{:T(128)}, /*index=5*/s32[]{:T(128)}) while((s32[]{:T(128)}, f32[8,8192]{1,0:T(8,128)}, s32[8,8192]{1,0:T(8,128)}, f32[512]{0:T(512)S(1)}, s32[]{:T(128)}, /*index=5*/s32[]{:T(128)}) %tuple.130), condition=%wide.region_6.7_spmd.clone, body=%wide.region_5.6_spmd.clone.sunk | while | flops 54525952 | bytes 198741 | solution.py:101
  170.2 8.7 %fusion.83 = f32[1,8192]{1,0:T(1,128)S(1)} fusion(f32[512,1]{0,1:T(1,128)S(1)} %bitcast.166, s32[8192]{0:T(1024)S(1)} %bitcast.155), kind=kOutput, calls=%fused_computation.6.clone.1 | convolution fusion | flops 54525952 | bytes 67584 | tf_op jit(solution)/shard_map/while/body/eval_jaxpr/dot_general | solution.py:102
  181.7 8.7 %fusion.83 = f32[1,8192]{1,0:T(1,128)S(1)} fusion(f32[512,1]{0,1:T(1,128)S(1)} %bitcast.166, s32[8192]{0:T(1024)S(1)} %bitcast.155), kind=kOutput, calls=%fused_computation.6.clone.1 | convolution fusion | flops 54525952 | bytes 67584 | tf_op jit(solution)/shard_map/while/body/eval_jaxpr/dot_general | solution.py:102
  193.2 8.7 %fusion.83 = f32[1,8192]{1,0:T(1,128)S(1)} fusion(f32[512,1]{0,1:T(1,128)S(1)} %bitcast.166, s32[8192]{0:T(1024)S(1)} %bitcast.155), kind=kOutput, calls=%fused_computation.6.clone.1 | convolution fusion | flops 54525952 | bytes 67584 | tf_op jit(solution)/shard_map/while/body/eval_jaxpr/dot_general | solution.py:102
  204.6 8.7 %fusion.83 = f32[1,8192]{1,0:T(1,128)S(1)} fusion(f32[512,1]{0,1:T(1,128)S(1)} %bitcast.166, s32[8192]{0:T(1024)S(1)} %bitcast.155), kind=kOutput, calls=%fused_computation.6.clone.1 | convolution fusion | flops 54525952 | bytes 67584 | tf_op jit(solution)/shard_map/while/body/eval_jaxpr/dot_general | solution.py:102
  216.1 8.7 %fusion.83 = f32[1,8192]{1,0:T(1,128)S(1)} fusion(f32[512,1]{0,1:T(1,128)S(1)} %bitcast.166, s32[8192]{0:T(1024)S(1)} %bitcast.155), kind=kOutput, calls=%fused_computation.6.clone.1 | convolution fusion | flops 54525952 | bytes 67584 | tf_op jit(solution)/shard_map/while/body/eval_jaxpr/dot_general | solution.py:102
  227.5 8.7 %fusion.83 = f32[1,8192]{1,0:T(1,128)S(1)} fusion(f32[512,1]{0,1:T(1,128)S(1)} %bitcast.166, s32[8192]{0:T(1024)S(1)} %bitcast.155), kind=kOutput, calls=%fused_computation.6.clone.1 | convolution fusion | flops 54525952 | bytes 67584 | tf_op jit(solution)/shard_map/while/body/eval_jaxpr/dot_general | solution.py:102
  239.0 8.7 %fusion.83 = f32[1,8192]{1,0:T(1,128)S(1)} fusion(f32[512,1]{0,1:T(1,128)S(1)} %bitcast.166, s32[8192]{0:T(1024)S(1)} %bitcast.155), kind=kOutput, calls=%fused_computation.6.clone.1 | convolution fusion | flops 54525952 | bytes 67584 | tf_op jit(solution)/shard_map/while/body/eval_jaxpr/dot_general | solution.py:102
  250.5 8.7 %fusion.83 = f32[1,8192]{1,0:T(1,128)S(1)} fusion(f32[512,1]{0,1:T(1,128)S(1)} %bitcast.166, s32[8192]{0:T(1024)S(1)} %bitcast.155), kind=kOutput, calls=%fused_computation.6.clone.1 | convolution fusion | flops 54525952 | bytes 67584 | tf_op jit(solution)/shard_map/while/body/eval_jaxpr/dot_general | solution.py:102
  278.8 15.4 %collective-permute-done.8 = f32[2,512,1]{2,1,0:T(8,128)S(1)} collective-permute-done((f32[2,512,1]{2,1,0:T(8,128)S(1)}, f32[2,512,1]{2,1,0:T(8,128)S(1)}, u32[]{:S(2)}, u32[]{:S(2)}) %collective-permute-start.8) | collective-permute-done | bytes 4128 | tf_op jit(solution)/shard_map/ppermute | solution.py:24
  298.2 50.0 %while.59 = (s32[]{:T(128)}, f32[512]{0:T(512)S(1)}, f32[8,8192]{1,0:T(8,128)S(1)}, s32[8,8192]{1,0:T(8,128)}, s32[]{:T(128)}, /*index=5*/s32[]{:T(128)}) while((s32[]{:T(128)}, f32[512]{0:T(512)S(1)}, f32[8,8192]{1,0:T(8,128)S(1)}, s32[8,8192]{1,0:T(8,128)}, s32[]{:T(128)}, /*index=5*/s32[]{:T(128)}) %tuple.127), condition=%wide.region_8.9_spmd.clone, body=%wide.region_7.8_spmd.clone.sunk | while | flops 54526976 | bytes 139359 | solution.py:92
  348.2 17.6 %all-gather.1 = f32[16,1,512]{2,1,0:T(1,128)S(1)} all-gather(f32[1,1,512]{2,1,0:T(1,128)S(1)} %bitcast.161), channel_id=1, replica_groups=mesh['groups'=2,'lon'=8,'lat'=2] {'lon','lat'}, dimensions={0}, use_global_device_ids=true | all-gather | bytes 34816 | tf_op jit(solution)/shard_map/all_gather | solution.py:98
  365.8 17.1 %fusion.67 = f32[1,512]{1,0:T(1,128)S(1)} fusion(f32[8192,1]{0,1:T(1,128)S(1)} %bitcast.158, f32[512,8192]{1,0:T(8,128)} %param.25), kind=kOutput, calls=%fused_computation.131 | convolution fusion | flops 50331648 | bytes 16812032 | tf_op jit(solution)/shard_map/dot_general | solution.py:96
  382.9 79.0 %while.56 = (s32[]{:T(128)}, f32[8,8192]{1,0:T(8,128)S(1)}, s32[8,8192]{1,0:T(8,128)}, f32[512]{0:T(512)S(1)}, s32[]{:T(128)}, /*index=5*/s32[]{:T(128)}) while((s32[]{:T(128)}, f32[8,8192]{1,0:T(8,128)S(1)}, s32[8,8192]{1,0:T(8,128)}, f32[512]{0:T(512)S(1)}, s32[]{:T(128)}, /*index=5*/s32[]{:T(128)}) %tuple.129), condition=%wide.region_10.11_spmd.clone, body=%wide.region_9.10_spmd.clone.sunk | while | flops 54525952 | bytes 198741 | solution.py:101
  384.0 8.7 %fusion.85 = f32[1,8192]{1,0:T(1,128)S(1)} fusion(f32[512,1]{0,1:T(1,128)S(1)} %bitcast.164, s32[8192]{0:T(1024)S(1)} %bitcast.156), kind=kOutput, calls=%fused_computation.10.clone.1 | convolution fusion | flops 54525952 | bytes 67584 | tf_op jit(solution)/shard_map/while/body/eval_jaxpr/dot_general | solution.py:102
  393.8 8.7 %fusion.85 = f32[1,8192]{1,0:T(1,128)S(1)} fusion(f32[512,1]{0,1:T(1,128)S(1)} %bitcast.164, s32[8192]{0:T(1024)S(1)} %bitcast.156), kind=kOutput, calls=%fused_computation.10.clone.1 | convolution fusion | flops 54525952 | bytes 67584 | tf_op jit(solution)/shard_map/while/body/eval_jaxpr/dot_general | solution.py:102
  403.7 8.7 %fusion.85 = f32[1,8192]{1,0:T(1,128)S(1)} fusion(f32[512,1]{0,1:T(1,128)S(1)} %bitcast.164, s32[8192]{0:T(1024)S(1)} %bitcast.156), kind=kOutput, calls=%fused_computation.10.clone.1 | convolution fusion | flops 54525952 | bytes 67584 | tf_op jit(solution)/shard_map/while/body/eval_jaxpr/dot_general | solution.py:102
  443.2 8.7 %fusion.85 = f32[1,8192]{1,0:T(1,128)S(1)} fusion(f32[512,1]{0,1:T(1,128)S(1)} %bitcast.164, s32[8192]{0:T(1024)S(1)} %bitcast.156), kind=kOutput, calls=%fused_computation.10.clone.1 | convolution fusion | flops 54525952 | bytes 67584 | tf_op jit(solution)/shard_map/while/body/eval_jaxpr/dot_general | solution.py:102
  479.0 27.9 %all_to_all.15 = f32[3,512,128]{2,0,1:T(4,128)S(1)} all-to-all(f32[3,512,128]{2,0,1:T(4,128)S(1)} %copy.35), channel_id=1, replica_groups=mesh['groups'=2,'lon'=8,'lat'=2] {'lon'}, dimensions={1} | all-to-all | bytes 1572864 | tf_op jit(solution)/shard_map/all_to_all | solution.py:115
  (232 shorter events, 268.3 us)
Async XLA Ops:
  1.4 39.2 %collective-permute-start.7 = (f32[2,1,128]{2,1,0:T(1,128)S(1)}, f32[2,1,128]{2,1,0:T(1,128)S(1)}, u32[]{:S(2)}, u32[]{:S(2)}) collective-permute-start(f32[2,1,128]{2,1,0:T(1,128)S(1)} %get-tuple-element.276), channel_id=1, source_target_pairs={{1,0},{3,2},{5,4},{7,6},{9,8},{11,10},{13,12},{15,14},{17,16},{19,... | collective-permute-start | bytes 3080 | tf_op jit(solution)/shard_map/ppermute | solution.py:27
  2.7 31.6 %copy-start = (f32[512,128]{1,0:T(8,128)S(1)}, f32[512,128]{1,0:T(8,128)}, u32[]{:S(2)}) copy-start(f32[512,128]{1,0:T(8,128)} %param.18) | copy-start | bytes 786436
  2.7 31.6 %copy-start.20 = (f32[512,128]{1,0:T(8,128)S(1)}, f32[512,128]{1,0:T(8,128)}, u32[]{:S(2)}) copy-start(f32[512,128]{1,0:T(8,128)} %param.19) | copy-start | bytes 786436
  2.7 32.8 %collective-permute-start.6 = (f32[2,1,128]{2,1,0:T(1,128)S(1)}, f32[2,1,128]{2,1,0:T(1,128)S(1)}, u32[]{:S(2)}, u32[]{:S(2)}) collective-permute-start(f32[2,1,128]{2,1,0:T(1,128)S(1)} %get-tuple-element.277), channel_id=1, source_target_pairs={{0,1},{2,3},{4,5},{6,7},{8,9},{10,11},{12,13},{14,15},{16,17},{18,... | collective-permute-start | bytes 3080 | tf_op jit(solution)/shard_map/ppermute | solution.py:24
  6.9 33.6 %copy-start.2 = (f32[1,512,128]{2,1,0:T(8,128)}, f32[1,512,128]{2,1,0:T(8,128)S(1)}, u32[]{:S(2)}) copy-start(f32[1,512,128]{2,1,0:T(8,128)S(1)} %convert_bitcast_fusion) | copy-start | bytes 786436
  7.7 27.9 %collective-permute-start.4 = (f32[3,1,128]{2,1,0:T(1,128)S(1)}, f32[3,1,128]{2,1,0:T(1,128)S(1)}, u32[]{:S(2)}, u32[]{:S(2)}) collective-permute-start(f32[3,1,128]{2,1,0:T(1,128)S(1)} %get-tuple-element.266), channel_id=1, source_target_pairs={{0,1},{2,3},{4,5},{6,7},{8,9},{10,11},{12,13},{14,15},{16,17},{18,... | collective-permute-start | bytes 4616 | tf_op jit(solution)/shard_map/ppermute | solution.py:24
  9.0 26.7 %collective-permute-start.5 = (f32[3,1,128]{2,1,0:T(1,128)S(1)}, f32[3,1,128]{2,1,0:T(1,128)S(1)}, u32[]{:S(2)}, u32[]{:S(2)}) collective-permute-start(f32[3,1,128]{2,1,0:T(1,128)S(1)} %get-tuple-element.267), channel_id=1, source_target_pairs={{1,0},{3,2},{5,4},{7,6},{9,8},{11,10},{13,12},{15,14},{17,16},{19,... | collective-permute-start | bytes 4616 | tf_op jit(solution)/shard_map/ppermute | solution.py:27
  11.4 29.1 %copy-start.9 = (f32[512,128]{1,0:T(8,128)S(1)}, f32[512,128]{1,0:T(8,128)}, u32[]{:S(2)}) copy-start(f32[512,128]{1,0:T(8,128)} %param.22) | copy-start | bytes 786436
  12.0 52.6 %collective-permute-start.1 = (f32[3,512,1]{1,2,0:T(1,128)S(1)}, f32[3,512,1]{1,2,0:T(1,128)S(1)}, u32[]{:S(2)}, u32[]{:S(2)}) collective-permute-start(f32[3,512,1]{1,2,0:T(1,128)S(1)} %copy.33), channel_id=1, source_target_pairs={{2,0},{4,2},{6,4},{8,6},{10,8},{12,10},{14,12},{0,14},{3,1},{5,3},... | collective-permute-start | bytes 18440 | tf_op jit(solution)/shard_map/ppermute | solution.py:27
  35.6 27.8 %collective-permute-start = (f32[3,512,1]{1,2,0:T(1,128)S(1)}, f32[3,512,1]{1,2,0:T(1,128)S(1)}, u32[]{:S(2)}, u32[]{:S(2)}) collective-permute-start(f32[3,512,1]{1,2,0:T(1,128)S(1)} %copy.31), channel_id=1, source_target_pairs={{0,2},{2,4},{4,6},{6,8},{8,10},{10,12},{12,14},{14,0},{1,3},{3,5},... | collective-permute-start | bytes 18440 | tf_op jit(solution)/shard_map/ppermute | solution.py:24
  35.7 23.8 %collective-permute-start.2 = (f32[2,512,1]{2,1,0:T(8,128)}, f32[2,512,1]{2,1,0:T(8,128)S(1)}, u32[]{:S(2)}, u32[]{:S(2)}) collective-permute-start(f32[2,512,1]{2,1,0:T(8,128)} %get-tuple-element.274), channel_id=1, source_target_pairs={{0,2},{2,4},{4,6},{6,8},{8,10},{10,12},{12,14},{14,0},{1,3},{3,5},... | collective-permute-start | bytes 12296 | tf_op jit(solution)/shard_map/ppermute | solution.py:24
  35.8 26.1 %collective-permute-start.3 = (f32[2,512,1]{2,1,0:T(8,128)S(1)}, f32[2,512,1]{2,1,0:T(8,128)S(1)}, u32[]{:S(2)}, u32[]{:S(2)}) collective-permute-start(f32[2,512,1]{2,1,0:T(8,128)S(1)} %get-tuple-element.275), channel_id=1, source_target_pairs={{2,0},{4,2},{6,4},{8,6},{10,8},{12,10},{14,12},{0,14},{3,1},{5,3},... | collective-permute-start | bytes 12296 | tf_op jit(solution)/shard_map/ppermute | solution.py:27
  264.3 32.1 %copy-start.16 = (f32[1,512,128]{2,1,0:T(8,128)S(1)}, f32[1,512,128]{2,1,0:T(8,128)}, u32[]{:S(2)}) copy-start(f32[1,512,128]{2,1,0:T(8,128)} %get-tuple-element.270) | copy-start | bytes 786436
  266.3 11.3 %collective-permute-start.11 = (f32[2,1,128]{2,1,0:T(1,128)S(1)}, f32[2,1,128]{2,1,0:T(1,128)S(1)}, u32[]{:S(2)}, u32[]{:S(2)}) collective-permute-start(f32[2,1,128]{2,1,0:T(1,128)S(1)} %get-tuple-element.272), channel_id=1, source_target_pairs={{1,0},{3,2},{5,4},{7,6},{9,8},{11,10},{13,12},{15,14},{17,16},{19,... | collective-permute-start | bytes 3080 | tf_op jit(solution)/shard_map/ppermute | solution.py:27
  267.6 9.1 %collective-permute-start.10 = (f32[2,1,128]{2,1,0:T(1,128)S(1)}, f32[2,1,128]{2,1,0:T(1,128)S(1)}, u32[]{:S(2)}, u32[]{:S(2)}) collective-permute-start(f32[2,1,128]{2,1,0:T(1,128)S(1)} %get-tuple-element.273), channel_id=1, source_target_pairs={{0,1},{2,3},{4,5},{6,7},{8,9},{10,11},{12,13},{14,15},{16,17},{18,... | collective-permute-start | bytes 3080 | tf_op jit(solution)/shard_map/ppermute | solution.py:24
  271.8 22.3 %collective-permute-start.8 = (f32[2,512,1]{2,1,0:T(8,128)S(1)}, f32[2,512,1]{2,1,0:T(8,128)S(1)}, u32[]{:S(2)}, u32[]{:S(2)}) collective-permute-start(f32[2,512,1]{2,1,0:T(8,128)S(1)} %get-tuple-element.268), channel_id=1, source_target_pairs={{0,2},{2,4},{4,6},{6,8},{8,10},{10,12},{12,14},{14,0},{1,3},{3,5},... | collective-permute-start | bytes 12296 | tf_op jit(solution)/shard_map/ppermute | solution.py:24
  271.9 24.5 %collective-permute-start.9 = (f32[2,512,1]{2,1,0:T(8,128)S(1)}, f32[2,512,1]{2,1,0:T(8,128)S(1)}, u32[]{:S(2)}, u32[]{:S(2)}) collective-permute-start(f32[2,512,1]{2,1,0:T(8,128)S(1)} %get-tuple-element.269), channel_id=1, source_target_pairs={{2,0},{4,2},{6,4},{8,6},{10,8},{12,10},{14,12},{0,14},{3,1},{5,3},... | collective-permute-start | bytes 12296 | tf_op jit(solution)/shard_map/ppermute | solution.py:27
  382.9 79.1 %copy-start.7 = (f32[512,128]{1,0:T(8,128)S(1)}, f32[512,128]{1,0:T(8,128)}, u32[]{:S(2)}) copy-start(f32[512,128]{1,0:T(8,128)} %get-tuple-element.271) | copy-start | bytes 786436
  382.9 79.1 %copy-start.14 = (s32[512,128]{1,0:T(8,128)S(1)}, s32[512,128]{1,0:T(8,128)}, u32[]{:S(2)}) copy-start(s32[512,128]{1,0:T(8,128)} %param.23) | copy-start | bytes 786436
  382.9 79.1 %copy-start.15 = (f32[512,128]{1,0:T(8,128)S(1)}, f32[512,128]{1,0:T(8,128)}, u32[]{:S(2)}) copy-start(f32[512,128]{1,0:T(8,128)} %mul.99) | copy-start | bytes 786436
  462.1 44.8 %copy-start.1 = (f32[512,128]{1,0:T(8,128)}, f32[512,128]{1,0:T(8,128)S(1)}, u32[]{:S(2)}) copy-start(f32[512,128]{1,0:T(8,128)S(1)} %subtract_multiply_fusion) | copy-start | bytes 786436
  462.2 13.5 %collective-permute-start.12 = (f32[1,512,1]{2,1,0:T(8,128)S(1)}, f32[1,512,1]{2,1,0:T(8,128)S(1)}, u32[]{:S(2)}, u32[]{:S(2)}) collective-permute-start(f32[1,512,1]{2,1,0:T(8,128)S(1)} %get-tuple-element.280), channel_id=1, source_target_pairs={{0,2},{2,4},{4,6},{6,8},{8,10},{10,12},{12,14},{14,0},{1,3},{3,5},... | collective-permute-start | bytes 6152 | tf_op jit(solution)/shard_map/ppermute | solution.py:24
  464.1 13.9 %collective-permute-start.13 = (f32[1,512,1]{2,1,0:T(8,128)S(1)}, f32[1,512,1]{2,1,0:T(8,128)S(1)}, u32[]{:S(2)}, u32[]{:S(2)}) collective-permute-start(f32[1,512,1]{2,1,0:T(8,128)S(1)} %get-tuple-element.281), channel_id=1, source_target_pairs={{2,0},{4,2},{6,4},{8,6},{10,8},{12,10},{14,12},{0,14},{3,1},{5,3},... | collective-permute-start | bytes 6152 | tf_op jit(solution)/shard_map/ppermute | solution.py:27
  467.0 11.2 %collective-permute-start.14 = (f32[1,1,128]{2,1,0:T(1,128)S(1)}, f32[1,1,128]{2,1,0:T(1,128)S(1)}, u32[]{:S(2)}, u32[]{:S(2)}) collective-permute-start(f32[1,1,128]{2,1,0:T(1,128)S(1)} %slice.307), channel_id=1, source_target_pairs={{1,0},{3,2},{5,4},{7,6},{9,8},{11,10},{13,12},{15,14},{17,16},{19,... | collective-permute-start | bytes 1544 | tf_op jit(solution)/shard_map/ppermute | solution.py:27
  (13 other events, 203.2 us)
where the time goes:
time: 511 us; the launch traced here: 508 us
  matrix products  265 us (52%)
  blocking collectives  67.3 us (13%)
  local copies, waits for them, and re-layouts  58.7 us (11%)
  waiting for transfers between devices  46.8 us (9%)
  other arithmetic  35.9 us (7%)
  starting transfers between devices  33 us (6%)
    dot_general x16, matrix products, body(): jnp.dot(one_hot(ids, point_iota), potential, precision=lax.Precision.HIGH...  139 us
    dot_general x16, matrix products, load_block(): jnp.dot(values, one_hot(ids, point_iota), precision=lax.Precision.HIGHEST)  91.5 us
    ppermute x7, waiting for transfers between devices, extended(): lax.ppermute(lax.slice_in_dim(block, block.shape[dim] - width, None, axis...  39.9 us
    all_gather x2, blocking collectives, body(): lax.all_gather(loads, ('lon', 'lat'), axis=0, tiled=True)  39.4 us
    dot_general x2, matrix products, body(): jnp.dot(green, lax.all_gather(loads, ('lon', 'lat'), axis=0, tiled=True),...  34.2 us
    dynamic_slice x40, local copies, waits for them, and re-layouts, body(): lax.scan(count_block, jnp.zeros((points,), jnp.float32), local_ids)  31.7 us
    all_to_all x1, blocking collectives, body(): lax.all_to_all(payload, 'lon', split_axis=1, concat_axis=2, tiled=True)  27.9 us
    ppermute x8, starting transfers between devices, extended(): lax.ppermute(lax.slice_in_dim(block, 0, width, axis=dim), axis, backward)  23.5 us
  transfers between devices with their start and end apart: 15, of which 6 were waited for; matrix products, arithmetic and copies ran while one was open for 6% of the time, Pallas kernels for 0%

commit v1 on v0

v1 whole, which is shorter than its diff:
```python
import functools

import jax
import jax.numpy as jnp
from jax import lax
from jax.experimental import pallas as pl
from jax.experimental.pallas import tpu as pltpu
from jax.sharding import PartitionSpec as P

f32 = jnp.float32
bf16 = jnp.bfloat16
i32 = jnp.int32

LANES = 128
LOW = 32
HIGH = 16
PIECES = 2
SEG_ROWS = 128
STEP_ROWS = 64
HIGHEST = lax.Precision.HIGHEST

flux_ratio = 0.25
slope_ratio = 0.25
drag_step = 1.0
attract_coef = 0.5

LAM, DEPTH, DRAG, OCEAN, POINT, FLUX = range(6)
ADJ_W, ADJ_E, C_W, C_E, G_W, G_E, ID_W, ID_E = range(8)
ADJ_L, C_L, G_L, ID_L = range(4)


def iota(shape, dim):
    return lax.broadcasted_iota(i32, shape, dim)


def roll_east(x):
    return pltpu.roll(x, LANES - 1, 1)


def roll_west(x):
    return pltpu.roll(x, 1, 1)


def local_ids(ids, points):
    return lax.bitwise_and(ids, points - 1)


def bf16_pieces(values):
    out = []
    for piece in range(PIECES):
        top = values.astype(bf16).astype(f32)
        out.append(top)
        if piece < PIECES - 1:
            values = values - top
    return out


def segment_part(values, ids, points, with_counts=False):
    blocks = points // LANES
    high = lax.shift_right_logical(ids, 5)
    high = lax.bitwise_and(high, 3) * blocks + lax.shift_right_logical(high, 2)
    low = lax.bitwise_and(ids, LOW - 1)
    high_iota = iota((HIGH, LANES), 0)
    low_iota = iota((LOW, LANES), 0)
    pieces = bf16_pieces(values)
    left, right = [], []
    for row in range(values.shape[0]):
        mask = jnp.broadcast_to(high[row : row + 1], (HIGH, LANES)) == high_iota
        parts = [
            jnp.where(mask, jnp.broadcast_to(piece[row : row + 1], (HIGH, LANES)), 0.0)
            for piece in pieces
        ]
        if with_counts:
            parts.append(jnp.where(mask, 1.0, 0.0))
        left.append(jnp.concatenate(parts, 0).astype(bf16))
        mask = jnp.broadcast_to(low[row : row + 1], (LOW, LANES)) == low_iota
        right.append(jnp.where(mask, 1.0, 0.0).astype(bf16))
    return lax.dot_general(
        jnp.concatenate(left, 1),
        jnp.concatenate(right, 1),
        (((1,), (1,)), ((), ())),
        preferred_element_type=f32,
    )


def segment_all(value_ref, id_ref, points, with_counts=False):
    rows = value_ref.shape[0]
    parts = PIECES + int(with_counts)

    def step(index, total):
        at = pl.ds(pl.multiple_of(index * SEG_ROWS, SEG_ROWS), SEG_ROWS)
        return total + segment_part(
            value_ref[at, :], local_ids(id_ref[at, :], points), points, with_counts
        )

    return lax.fori_loop(0, rows // SEG_ROWS, step, jnp.zeros((parts * HIGH, LOW), f32))


def sum_pieces(parts):
    total = parts[:HIGH]
    for piece in range(1, PIECES):
        total = total + parts[piece * HIGH : (piece + 1) * HIGH]
    return total


def as_points(table, points):
    blocks = points // LANES
    return jnp.concatenate([table[q * blocks : (q + 1) * blocks] for q in range(4)], 1)


def fold(line):
    return jnp.concatenate(
        [line[:, k * LANES : (k + 1) * LANES] for k in range(line.shape[1] // LANES)], 0
    )


def unfold(block):
    return jnp.concatenate([block[k : k + 1] for k in range(block.shape[0])], 1)


def take_sides(block):
    sub, lane = iota((8, LANES), 0), iota((8, LANES), 1)
    pick = ((sub == 0) & (lane == 0)) | ((sub == 1) & (lane == LANES - 1))
    return lax.dot_general(
        pick.astype(f32), block, (((1,), (1,)), ((), ())), precision=HIGHEST,
        preferred_element_type=f32,
    )


def put_sides(lines, entries):
    sub, lane = iota((8, LANES), 0), iota((8, LANES), 1)
    parts = []
    for first, last in entries:
        part = jnp.zeros((8, LANES), f32)
        if first is not None:
            part = jnp.where((sub == first[0]) & (lane == 0), first[1], part)
        if last is not None:
            part = jnp.where((sub == last[0]) & (lane == LANES - 1), last[1], part)
        parts.append(part)
    return lax.dot_general(
        lines, jnp.concatenate(parts, 1), (((0,), (0,)), ((), ())), precision=HIGHEST,
        preferred_element_type=f32,
    )


def green_product(green_ref, load_row, acc_ref):
    points, total = green_ref.shape
    tall = 32

    def step(index, carry):
        at = pl.ds(pl.multiple_of(index * tall, tall), tall)
        acc = jnp.zeros((tall, LANES), f32)
        for k in range(total // LANES):
            acc = acc + green_ref[at, k * LANES : (k + 1) * LANES] * jnp.broadcast_to(
                load_row(k), (tall, LANES)
            )
        acc_ref[at, :] = acc
        return carry

    lax.fori_loop(0, points // tall, step, 0)
    return lax.dot_general(
        jnp.ones((8, LANES), f32), acc_ref[...], (((1,), (1,)), ((), ())), precision=HIGHEST,
        preferred_element_type=f32,
    )


def spread(potential, ids):
    points = potential.shape[1]
    rows = ids.shape[0]
    low = lax.bitwise_and(ids, LANES - 1)
    block = lax.shift_right_logical(ids, 7)
    out = None
    for k in range(points // LANES):
        table = potential[:, k * LANES : (k + 1) * LANES]
        table = jnp.broadcast_to(table[None], (rows // 8, 8, LANES)).reshape(rows, LANES)
        value = jnp.take_along_axis(table, low, axis=1, mode="promise_in_bounds")
        out = value if out is None else jnp.where(block == k, value, out)
    return out


def next_rows(ref, start, count, last=None):
    if start + count < ref.shape[0]:
        return ref[start + 1 : start + count + 1, :]
    return jnp.concatenate([ref[start + 1 :, :], jnp.zeros((1, LANES), ref.dtype)], 0)


def south_rows(first, block):
    return jnp.concatenate([first, block[:-1]], 0)


def pack_kernel(lam, east, north, depth, drag, ocean, coarse, to_east, to_west, to_lat, *, points):
    rows = lam.shape[0]
    lat = lax.axis_index("lat")
    sides = take_sides(
        jnp.concatenate(
            [
                lam[...],
                depth[...],
                drag[...],
                ocean[...].astype(f32),
                local_ids(coarse[...], points).astype(f32),
                east[...],
            ],
            0,
        )
    )
    zero = jnp.zeros((2, rows), f32)
    to_west[...] = jnp.concatenate(
        [sides[0:1, k * rows : (k + 1) * rows] for k in range(6)] + [zero], 0
    )
    to_east[...] = jnp.concatenate(
        [sides[1:2, k * rows : (k + 1) * rows] for k in range(6)] + [zero], 0
    )

    def border(row):
        return jnp.concatenate(
            [
                lam[row : row + 1, :],
                depth[row : row + 1, :],
                drag[row : row + 1, :],
                ocean[row : row + 1, :].astype(f32),
                local_ids(coarse[row : row + 1, :], points).astype(f32),
                north[row : row + 1, :],
                jnp.zeros((2, LANES), f32),
            ],
            0,
        )

    to_lat[...] = jnp.where(lat == 0, border(rows - 1), border(0))


def inner_kernel(
    lam, east, north, depth, drag, ocean, coarse,
    held, gu, cu, gv, cv, sums, source, *, points,
):
    rows = lam.shape[0]
    inner = iota((STEP_ROWS, LANES), 1) < LANES - 1
    carry = jnp.zeros((1, LANES), f32)
    for start in range(0, rows, STEP_ROWS):
        at = slice(start, start + STEP_ROWS)
        lam_c, depth_c, drag_c = lam[at, :], depth[at, :], drag[at, :]
        ocean_c = ocean[at, :].astype(f32)
        damp = jnp.where(
            inner,
            ocean_c * roll_east(ocean_c) / (1.0 + drag_step * 0.5 * (drag_c + roll_east(drag_c))),
            0.0,
        )
        ratio = damp * (flux_ratio * 0.5) * (depth_c + roll_east(depth_c))
        adj_u = damp * east[at, :] + ratio * (roll_east(lam_c) - lam_c)
        cu[at, :] = ratio
        gu[at, :] = damp * adj_u
        ocean_n = next_rows(ocean, start, STEP_ROWS).astype(f32)
        damp = (
            ocean_c
            * ocean_n
            / (1.0 + drag_step * 0.5 * (drag_c + next_rows(drag, start, STEP_ROWS)))
        )
        ratio = damp * (flux_ratio * 0.5) * (depth_c + next_rows(depth, start, STEP_ROWS))
        adj_v = damp * north[at, :] + ratio * (next_rows(lam, start, STEP_ROWS) - lam_c)
        cv[at, :] = ratio
        gv[at, :] = damp * adj_v
        src = slope_ratio * (roll_west(adj_u) - adj_u + south_rows(carry, adj_v) - adj_v)
        carry = adj_v[STEP_ROWS - 1 :]
        source[at, :] = src
        held[at, :] = lam_c + src
    sums[...] = segment_all(source, coarse, points, True)


def face(low, high, flux):
    damp = (
        low[OCEAN : OCEAN + 1]
        * high[OCEAN : OCEAN + 1]
        / (1.0 + drag_step * 0.5 * (low[DRAG : DRAG + 1] + high[DRAG : DRAG + 1]))
    )
    ratio = damp * (flux_ratio * 0.5) * (low[DEPTH : DEPTH + 1] + high[DEPTH : DEPTH + 1])
    adj = damp * flux + ratio * (high[LAM : LAM + 1] - low[LAM : LAM + 1])
    return adj, ratio, damp * adj


def rim_kernel(
    own_east, own_west, own_lat, from_west, from_east, from_lat, sums,
    payload, lines, lat_lines, *, points,
):
    lat = lax.axis_index("lat")
    blocks = points // LANES
    west, east = own_west[...], own_east[...]
    far_west, far_east = from_west[...], from_east[...]
    mine, other = own_lat[...], from_lat[...]
    adj_w, c_w, g_w = face(far_west, west, far_west[FLUX : FLUX + 1])
    adj_e, c_e, g_e = face(east, far_east, east[FLUX : FLUX + 1])
    lower = jnp.where(lat == 0, mine, other)
    upper = jnp.where(lat == 0, other, mine)
    adj_l, c_l, g_l = face(lower, upper, lower[FLUX : FLUX + 1])
    lines[...] = jnp.concatenate(
        [adj_w, adj_e, c_w, c_e, g_w, g_e, far_west[POINT : POINT + 1], far_east[POINT : POINT + 1]],
        0,
    )
    lat_lines[...] = jnp.concatenate(
        [adj_l, c_l, g_l, other[POINT : POINT + 1], jnp.zeros((4, LANES), f32)], 0
    )
    sign = jnp.where(lat == 0, -slope_ratio, slope_ratio)
    pad = jnp.zeros((1, LANES), f32)
    values = jnp.concatenate(
        [fold(slope_ratio * adj_w), fold(-slope_ratio * adj_e), sign * adj_l, pad], 0
    )
    ids = jnp.concatenate(
        [
            fold(west[POINT : POINT + 1]),
            fold(east[POINT : POINT + 1]),
            mine[POINT : POINT + 1],
            pad,
        ],
        0,
    ).astype(i32)
    total = sum_pieces(sums[...]) + sum_pieces(segment_part(values, ids, points))
    counts = as_points(sums[PIECES * HIGH : (PIECES + 1) * HIGH, :], points)
    inverse = 1.0 / counts
    loads = as_points(total, points) * inverse
    part = jnp.concatenate([loads, inverse], 0)
    if part.shape[0] < 8:
        part = jnp.concatenate([part, jnp.zeros((8 - part.shape[0], LANES), f32)], 0)
    for target in range(payload.shape[0]):
        payload[target] = part


def neighbours(n_lon, n_lat):
    lon, lat = lax.axis_index("lon"), lax.axis_index("lat")
    west = lax.rem(lon + n_lon - 1, n_lon) * n_lat + lat
    east = lax.rem(lon + 1, n_lon) * n_lat + lat
    other = lon * n_lat + (1 - lat)
    return west, east, other


def second_kernel(
    first, green, coarse, ocean, held_in, gu, cu, gv, cv, lines, lat_lines,
    payload, held, adj_u_out, adj_v_out, acc, lam, source, sides, *, points, n_lon, n_lat,
):
    rows = coarse.shape[0]
    blocks = points // LANES
    lat = lax.axis_index("lat")
    south_end = jnp.where(lat == 1, 1.0, 0.0)
    north_end = jnp.where(lat == 0, 1.0, 0.0)
    potential = green_product(
        green, lambda k: first[k // blocks, k % blocks : k % blocks + 1, :], acc
    )
    put = put_sides(
        lines[...],
        [
            ((ADJ_W, slope_ratio), (ADJ_E, -slope_ratio)),
            ((C_W, 1.0), (C_E, 1.0)),
            (None, (G_E, 1.0)),
        ],
    )
    adj_l = lat_lines[ADJ_L : ADJ_L + 1, :]
    c_l = lat_lines[C_L : C_L + 1, :]
    g_l = lat_lines[G_L : G_L + 1, :]
    row = iota((STEP_ROWS, LANES), 0)
    lane = iota((STEP_ROWS, LANES), 1)
    lam[rows : rows + 8, :] = jnp.zeros((8, LANES), f32)
    for start in range(0, rows, STEP_ROWS):
        at = slice(start, start + STEP_ROWS)
        pot = spread(potential, local_ids(coarse[at, :], points))
        value = held_in[at, :] + put[at, :LANES] - attract_coef * pot
        if start == 0:
            value = value + jnp.where(row == 0, south_end * slope_ratio * adj_l, 0.0)
        if start == rows - STEP_ROWS:
            value = value - jnp.where(row == STEP_ROWS - 1, north_end * slope_ratio * adj_l, 0.0)
        value = ocean[at, :].astype(f32) * value
        lam[at, :] = value
        sides[rows + start : rows + start + STEP_ROWS, :] = value
    carry = south_end * c_l * lam[0:1, :]
    to_lat_south = -slope_ratio * carry
    for start in range(0, rows, STEP_ROWS):
        at = slice(start, start + STEP_ROWS)
        lam_c = lam[at, :]
        c_side = put[at, LANES : 2 * LANES]
        east_c = jnp.where(lane == LANES - 1, c_side, cu[at, :])
        adj_u = (
            gu[at, :]
            + put[at, 2 * LANES :]
            + east_c * (jnp.where(lane == LANES - 1, 0.0, roll_east(lam_c)) - lam_c)
        )
        west_part = c_side * lam_c
        g_c, c_c = gv[at, :], cv[at, :]
        if start == rows - STEP_ROWS:
            last = row == STEP_ROWS - 1
            g_c = g_c + jnp.where(last, north_end * g_l, 0.0)
            c_c = c_c + jnp.where(last, north_end * c_l, 0.0)
        adj_v = g_c + c_c * (lam[start + 1 : start + STEP_ROWS + 1, :] - lam_c)
        src = slope_ratio * (
            jnp.where(lane == 0, west_part, roll_west(adj_u))
            - adj_u
            + south_rows(carry, adj_v)
            - adj_v
        )
        carry = adj_v[STEP_ROWS - 1 :]
        adj_u_out[at, :] = adj_u
        adj_v_out[at, :] = adj_v
        source[at, :] = src
        held[at, :] = lam_c + src
        sides[at, :] = jnp.where(lane == 0, -slope_ratio * west_part, slope_ratio * adj_u)
    to_lat = jnp.where(lat == 0, slope_ratio * carry, to_lat_south)
    edge = jnp.where(lat == 0, lam[rows - 1 : rows, :], lam[0:1, :])
    taken = take_sides(sides[...])
    own = as_points(sum_pieces(segment_all(source, coarse, points)), points)

    def away(line, ids):
        return as_points(sum_pieces(segment_part(line, ids.astype(i32), points)), points)

    east_part = away(fold(taken[1:2, :rows]), fold(lines[ID_E : ID_E + 1, :]))
    west_part = away(fold(taken[0:1, :rows]), fold(lines[ID_W : ID_W + 1, :]))
    pad = jnp.zeros((1, LANES), f32)
    lat_part = away(
        jnp.concatenate([to_lat, pad], 0),
        jnp.concatenate([lat_lines[ID_L : ID_L + 1, :], pad], 0),
    )
    part = jnp.concatenate([own, east_part, west_part, lat_part], 0)
    spare = payload.shape[1] - part.shape[0]
    part = jnp.concatenate([part, jnp.zeros((spare, LANES), f32)], 0)
    for target in range(payload.shape[0]):
        payload[target] = part
    west, east, other = neighbours(n_lon, n_lat)
    begin = 4 * blocks
    tall = rows // LANES
    payload[west, begin : begin + tall, :] = fold(taken[0:1, rows:])
    payload[east, begin : begin + tall, :] = fold(taken[1:2, rows:])
    payload[other, begin + tall : begin + tall + 1, :] = edge


def last_kernel(
    first, second, green, coarse, ocean, held, adj_u_in, adj_v_in, lines, lat_lines,
    lam_out, east_out, north_out, payload, edge, acc, loads, *, points, n_lon, n_lat,
):
    rows = coarse.shape[0]
    blocks = points // LANES
    tall = rows // LANES
    lat = lax.axis_index("lat")
    for lon in range(n_lon):
        for band in range(n_lat):
            here = lon * n_lat + band
            west = (lon - 1) % n_lon * n_lat + band
            east = (lon + 1) % n_lon * n_lat + band
            other = lon * n_lat + 1 - band
            total = (
                second[here, :blocks, :]
                + second[west, blocks : 2 * blocks, :]
                + second[east, 2 * blocks : 3 * blocks, :]
                + second[other, 3 * blocks : 4 * blocks, :]
            )
            loads[here * blocks : (here + 1) * blocks, :] = (
                total * first[here, blocks : 2 * blocks, :]
            )
    potential = green_product(green, lambda k: loads[k : k + 1, :], acc)
    west, east, other = neighbours(n_lon, n_lat)
    begin = 4 * blocks
    lam_w = unfold(second[west, begin : begin + tall, :])
    lam_e = unfold(second[east, begin : begin + tall, :])
    lam_l = second[other, begin + tall : begin + tall + 1, :]
    add_e = lines[C_E : C_E + 1, :] * lam_e
    add_w = lines[G_W : G_W + 1, :] - lines[C_W : C_W + 1, :] * lam_w
    put = put_sides(
        jnp.concatenate([add_w, add_e, jnp.zeros((6, rows), f32)], 0),
        [((0, slope_ratio), (1, -slope_ratio)), (None, (1, 1.0))],
    )
    c_l = lat_lines[C_L : C_L + 1, :]
    g_l = lat_lines[G_L : G_L + 1, :]
    from_north = jnp.where(lat == 0, c_l * lam_l, 0.0)
    from_south = jnp.where(lat == 1, g_l - c_l * lam_l, 0.0)
    row = iota((STEP_ROWS, LANES), 0)
    for start in range(0, rows, STEP_ROWS):
        at = slice(start, start + STEP_ROWS)
        pot = spread(potential, local_ids(coarse[at, :], points))
        value = held[at, :] + put[at, :LANES] - attract_coef * pot
        north = adj_v_in[at, :]
        if start == 0:
            value = value + jnp.where(row == 0, slope_ratio * from_south, 0.0)
        if start == rows - STEP_ROWS:
            last = row == STEP_ROWS - 1
            value = value - jnp.where(last, slope_ratio * from_north, 0.0)
            north = north + jnp.where(last, from_north, 0.0)
        lam_out[at, :] = ocean[at, :].astype(f32) * value
        east_out[at, :] = adj_u_in[at, :] + put[at, LANES:]
        north_out[at, :] = north
    edge[...] = lam_out[0:1, :]
    span = rows // n_lon
    for target in range(n_lon):
        stop = (target + 1) * span
        payload[target, :span, :] = lam_out[target * span : stop, :]
        if target < n_lon - 1:
            payload[target, span : span + 8, :] = lam_out[stop : stop + 8, :]
        else:
            payload[target, span : span + 8, :] = jnp.zeros((8, LANES), f32)


def bands_kernel(parts, bands):
    count, tall, _ = parts.shape
    span = tall - 8
    lane = iota((span, LANES), 1)
    for k in range(count):
        here = parts[k, :span, :]
        east = parts[(k + 1) % count, :span, :]
        at = slice(k * LANES, (k + 1) * LANES)
        bands[0, 0, :, at] = here
        bands[1, 0, :, at] = jnp.where(lane == LANES - 1, roll_east(east), roll_east(here)) - here
        bands[2, 0, :, at] = parts[k, 1 : span + 1, :] - here


def call(kernel, shapes, scratch, args, name):
    vmem = pl.BlockSpec(memory_space=pltpu.VMEM)
    return pl.pallas_call(
        kernel,
        out_shape=[jax.ShapeDtypeStruct(shape, f32) for shape in shapes],
        in_specs=[vmem] * len(args),
        out_specs=[vmem] * len(shapes),
        scratch_shapes=scratch,
        compiler_params=pltpu.CompilerParams(vmem_limit_bytes=16 << 20),
        name=name,
    )(*args)


def body(n_lon, n_lat, lam_in, flux_east, flux_north, depth, drag, ocean, coarse_of, green):
    rows, cols = lam_in.shape
    points = green.shape[0]
    blocks = points // LANES
    owners = n_lon * n_lat
    grid = (rows, cols)
    fields = (lam_in, flux_east, flux_north, depth, drag, ocean, coarse_of)
    to_east, to_west, to_lat = call(
        functools.partial(pack_kernel, points=points),
        [(8, rows), (8, rows), (8, cols)], [], fields, "pack",
    )
    forward = [(k, (k + 1) % n_lon) for k in range(n_lon)]
    backward = [(target, source) for source, target in forward]
    from_west = lax.ppermute(to_east, "lon", forward)
    from_east = lax.ppermute(to_west, "lon", backward)
    from_lat = lax.ppermute(to_lat, "lat", [(0, 1), (1, 0)])
    held, gu, cu, gv, cv, sums = call(
        functools.partial(inner_kernel, points=points),
        [grid] * 5 + [((PIECES + 1) * HIGH, LOW)],
        [pltpu.VMEM(grid, f32)], fields, "inner",
    )
    payload, lines, lat_lines = call(
        functools.partial(rim_kernel, points=points),
        [(owners, 8, LANES), (8, rows), (8, LANES)], [],
        (to_east, to_west, to_lat, from_west, from_east, from_lat, sums), "rim",
    )
    first = lax.all_to_all(payload, ("lon", "lat"), 0, 0, tiled=True)
    tall = -(-(4 * blocks + rows // LANES + 1) // 8) * 8
    payload, held, adj_u, adj_v = call(
        functools.partial(second_kernel, points=points, n_lon=n_lon, n_lat=n_lat),
        [(owners, tall, LANES), grid, grid, grid],
        [
            pltpu.VMEM((points, LANES), f32),
            pltpu.VMEM((rows + 8, cols), f32),
            pltpu.VMEM(grid, f32),
            pltpu.VMEM((2 * rows, cols), f32),
        ],
        (first, green, coarse_of, ocean, held, gu, cu, gv, cv, lines, lat_lines), "second",
    )
    second = lax.all_to_all(payload, ("lon", "lat"), 0, 0, tiled=True)
    span = rows // n_lon
    lam, east, north, payload, edge = call(
        functools.partial(last_kernel, points=points, n_lon=n_lon, n_lat=n_lat),
        [grid, grid, grid, (n_lon, span + 8, cols), (1, cols)],
        [pltpu.VMEM((points, LANES), f32), pltpu.VMEM((owners * blocks, LANES), f32)],
        (first, second, green, coarse_of, ocean, held, adj_u, adj_v, lines, lat_lines), "last",
    )
    edge = lax.ppermute(edge, "lat", [(1, 0)])
    payload = lax.dynamic_update_slice(payload, edge[None], (n_lon - 1, span, 0))
    parts = lax.all_to_all(payload, "lon", 0, 0, tiled=True)
    (bands,) = call(bands_kernel, [(3, 1, span, n_lon * cols)], [], (parts,), "bands")
    return lam, east, north, bands


def solution(mesh):
    cells = P(("groups", "lat"), "lon")
    n_lon, n_lat = mesh.shape["lon"], mesh.shape["lat"]
    return jax.shard_map(
        functools.partial(body, n_lon, n_lat),
        mesh=mesh,
        in_specs=(cells,) * 6 + (P("lat", "lon"), P(("lon", "lat"), None)),
        out_specs=(cells,) * 3 + (P(None, ("groups", "lat"), "lon", None),),
        check_vma=False,
    )
```

time: 511 us -> 77.5 us (0.15)
  matrix products: 265 us -> 0 us
  waiting for transfers between devices: 46.8 us -> 1.72 us
  local copies, waits for them, and re-layouts: 58.7 us -> 14.3 us
  other arithmetic: 35.9 us -> 0 us
  blocking collectives: 67.3 us -> 36.4 us
  starting transfers between devices: 33 us -> 7.33 us
  Pallas kernels: 0 us -> 16.5 us
    dot_general x34 -> x0, matrix products: 265 us -> none  [the longest x16 139 us: body(): jnp.dot(one_hot(ids, point_iota), potential, precision=lax.Precision.HIGH...]
    ppermute x15 -> x4, waiting for transfers between devices: 46.8 us -> 1.72 us  [the longest x1 1.72 us: body(): edge = lax.ppermute(edge, 'lat', [(1, 0)])]
    all_gather x2 -> x0, blocking collectives: 39.4 us -> none  [body(): lax.all_gather(loads, ('lon', 'lat'), axis=0, tiled=True)]
    dynamic_slice x40 -> x0, local copies, waits for them, and re-layouts: 31.7 us -> none  [body(): lax.scan(count_block, jnp.zeros((points,), jnp.float32), local_ids)]
    ppermute x15 -> x4, starting transfers between devices: 33 us -> 7.33 us  [the longest x1 3.07 us: body(): from_east = lax.ppermute(to_west, 'lon', backward)]
    pallas_call x0 -> x6, Pallas kernels: none -> 16.5 us  [call(): pl.pallas_call(kernel, out_shape=[jax.ShapeDtypeStruct(shape, f32) for sh...]
    reduce_sum x8 -> x0, other arithmetic: 15.6 us -> none  [count_block(): return (total + jnp.sum(one_hot(ids, point_iota), axis=0), None)]
    dynamic_update_slice x16 -> x1, local copies, waits for them, and re-layouts: 15.4 us -> 0.03 us  [body(): lax.dynamic_update_slice(payload, edge[None], (n_lon - 1, span, 0))]
  transfers between devices with their start and end apart: 15 -> 4, of which waited for: 6 -> 1; matrix products, arithmetic and copies ran while one was open for 6% -> 0% of each run, Pallas kernels for 0% -> 4%
where the time goes in v1:
time: 77.5 us; the launch traced here: 77 us
  blocking collectives  36.4 us (47%)
  Pallas kernels  16.5 us (21%)
  local copies, waits for them, and re-layouts  14.3 us (18%)
  starting transfers between devices  7.33 us (9%)
  waiting for transfers between devices  1.72 us (2%)
    pallas_call x6, Pallas kernels, call(): pl.pallas_call(kernel, out_shape=[jax.ShapeDtypeStruct(shape, f32) for sh...  16.5 us
    unnamed x22, local copies, waits for them, and re-layouts  14.3 us
    all_to_all x1, blocking collectives, body(): parts = lax.all_to_all(payload, 'lon', 0, 0, tiled=True)  13.4 us
    all_to_all x1, blocking collectives, body(): second = lax.all_to_all(payload, ('lon', 'lat'), 0, 0, tiled=True)  11.6 us
    all_to_all x1, blocking collectives, body(): first = lax.all_to_all(payload, ('lon', 'lat'), 0, 0, tiled=True)  11.4 us
    ppermute x1, starting transfers between devices, body(): from_east = lax.ppermute(to_west, 'lon', backward)  3.07 us
    ppermute x1, starting transfers between devices, body(): from_west = lax.ppermute(to_east, 'lon', forward)  2.98 us
    ppermute x1, waiting for transfers between devices, body(): edge = lax.ppermute(edge, 'lat', [(1, 0)])  1.72 us
  transfers between devices with their start and end apart: 4, of which 1 were waited for; matrix products, arithmetic and copies ran while one was open for 0% of the time, Pallas kernels for 4%

profile of v1, /device:TPU:0, one launch (start us, length us, event | category | flops | bytes accessed | tf_op | source)
XLA Modules:
  0.0 77.0 jit_solution(5639869910206677896)
XLA Ops:
  0.6 0.0 copy-start.2
  0.6 0.9 %copy-done.2 = s32[512,128]{1,0:T(8,128)S(1)} copy-done((s32[512,128]{1,0:T(8,128)S(1)}, s32[512,128]{1,0:T(8,128)}, u32[]{:S(2)}) %copy-start.2) | copy-done | bytes 262168
  1.6 0.9 %copy-done.4 = s32[512,128]{1,0:T(8,128)S(1)} copy-done((s32[512,128]{1,0:T(8,128)S(1)}, s32[512,128]{1,0:T(8,128)}, u32[]{:S(2)}) %copy-start.4) | copy-done | bytes 262168
  2.5 0.9 %copy-done.6 = f32[512,128]{1,0:T(8,128)S(1)} copy-done((f32[512,128]{1,0:T(8,128)S(1)}, f32[512,128]{1,0:T(8,128)}, u32[]{:S(2)}) %copy-start.6) | copy-done | bytes 262168
  3.5 0.9 %copy-done.7 = f32[512,128]{1,0:T(8,128)S(1)} copy-done((f32[512,128]{1,0:T(8,128)S(1)}, f32[512,128]{1,0:T(8,128)}, u32[]{:S(2)}) %copy-start.7) | copy-done | bytes 262168
  4.4 0.9 %copy-done.8 = f32[512,128]{1,0:T(8,128)S(1)} copy-done((f32[512,128]{1,0:T(8,128)S(1)}, f32[512,128]{1,0:T(8,128)}, u32[]{:S(2)}) %copy-start.8) | copy-done | bytes 262168
  5.4 0.9 %copy-done.9 = f32[512,128]{1,0:T(8,128)S(1)} copy-done((f32[512,128]{1,0:T(8,128)S(1)}, f32[512,128]{1,0:T(8,128)}, u32[]{:S(2)}) %copy-start.9) | copy-done | bytes 262168
  6.3 0.9 %copy-done.10 = f32[512,128]{1,0:T(8,128)S(1)} copy-done((f32[512,128]{1,0:T(8,128)S(1)}, f32[512,128]{1,0:T(8,128)}, u32[]{:S(2)}) %copy-start.10) | copy-done | bytes 262168
  7.3 1.4 %pack.1 = (f32[8,512]{1,0:T(8,128)S(1)}, f32[8,512]{1,0:T(8,128)S(1)}, f32[8,128]{1,0:T(8,128)S(1)}) custom-call(f32[512,128]{1,0:T(8,128)S(1)} %copy-done.6, f32[512,128]{1,0:T(8,128)S(1)} %copy-done.7, f32[512,128]{1,0:T(8,128)S(1)} %copy-done.8, f32[512,128]{1,0:T(8,128)S(1)} %copy-done.9, f32[512,128]{1,0:T(8,128)S(1)} %copy-done.10, ...), custom_call_target="tpu_custom_call" | custom-call | tf_op jit(solution)/shard_map/pack/pallas_call | solution.py:510
  8.6 3.0 %collective-permute-start = (f32[8,512]{1,0:T(8,128)S(1)}, f32[8,512]{1,0:T(8,128)S(1)}, u32[]{:S(2)}, u32[]{:S(2)}) collective-permute-start(f32[8,512]{1,0:T(8,128)S(1)} %get-tuple-element.25.own_east), channel_id=1, source_target_pairs={{0,2},{2,4},{4,6},{6,8},{8,10},{10,12},{12,14},{14,0},{1,3},{3,5},... | collective-permute-start | bytes 49160 | tf_op jit(solution)/shard_map/ppermute | solution.py:534
  11.6 3.1 %collective-permute-start.1 = (f32[8,512]{1,0:T(8,128)S(1)}, f32[8,512]{1,0:T(8,128)S(1)}, u32[]{:S(2)}, u32[]{:S(2)}) collective-permute-start(f32[8,512]{1,0:T(8,128)S(1)} %get-tuple-element.26.own_west), channel_id=1, source_target_pairs={{2,0},{4,2},{6,4},{8,6},{10,8},{12,10},{14,12},{0,14},{3,1},{5,3},... | collective-permute-start | bytes 49160 | tf_op jit(solution)/shard_map/ppermute | solution.py:535
  14.7 3.0 %inner.1 = (f32[512,128]{1,0:T(8,128)S(1)}, f32[512,128]{1,0:T(8,128)S(1)}, f32[512,128]{1,0:T(8,128)S(1)}, f32[512,128]{1,0:T(8,128)S(1)}, f32[512,128]{1,0:T(8,128)S(1)}, /*index=5*/f32[48,32]{1,0:T(8,128)S(1)}) custom-call(f32[512,128]{1,0:T(8,128)S(1)} %copy-done.6, f32[512,128]{1,0:T(8,128)S(1)} %copy-done.7, f32[512,128]{1,0:T(8,128)S(1)} %copy-done.8, ...), custom_call_target="tpu_custom_call" | custom-call | tf_op jit(solution)/shard_map/inner/pallas_call | solution.py:510
  17.8 0.3 rim.1
  18.0 11.4 %all_to_all.15.first = f32[16,8,128]{2,1,0:T(8,128)S(1)} all-to-all(f32[16,8,128]{2,1,0:T(8,128)S(1)} %get-tuple-element.29), channel_id=1, replica_groups=mesh['groups'=2,'lon'=8,'lat'=2] {'lon','lat'}, dimensions={0} | all-to-all | bytes 131072 | tf_op jit(solution)/shard_map/all_to_all | solution.py:547
  29.5 5.8 %copy-done = f32[512,8192]{1,0:T(8,128)S(1)} copy-done((f32[512,8192]{1,0:T(8,128)S(1)}, f32[512,8192]{1,0:T(8,128)}, u32[]{:S(2)}) %copy-start) | copy-done | bytes 16777240
  35.2 0.9 %copy-done.3 = s32[512,128]{1,0:T(8,128)S(1)} copy-done((s32[512,128]{1,0:T(8,128)S(1)}, s32[512,128]{1,0:T(8,128)}, u32[]{:S(2)}) %copy-start.3) | copy-done | bytes 262168
  36.2 0.9 %copy-done.5 = s32[512,128]{1,0:T(8,128)S(1)} copy-done((s32[512,128]{1,0:T(8,128)S(1)}, s32[512,128]{1,0:T(8,128)}, u32[]{:S(2)}) %copy-start.5) | copy-done | bytes 262168
  37.1 6.6 %second.1 = (f32[16,24,128]{2,1,0:T(8,128)S(1)}, f32[512,128]{1,0:T(8,128)S(1)}, f32[512,128]{1,0:T(8,128)S(1)}, f32[512,128]{1,0:T(8,128)S(1)}) custom-call(f32[16,8,128]{2,1,0:T(8,128)S(1)} %all_to_all.15.first, f32[512,8192]{1,0:T(8,128)S(1)} %copy-done, s32[512,128]{1,0:T(8,128)S(1)} %copy-done.5, s32[512,128]{1,0:T(8,128)S(1)} %copy-done.3, ...), custom_call_target="tpu_custom_call" | custom-call | tf_op jit(solution)/shard_map/second/pallas_call | solution.py:510
  43.7 11.6 %all_to_all.16.second = f32[16,24,128]{2,1,0:T(8,128)S(1)} all-to-all(f32[16,24,128]{2,1,0:T(8,128)S(1)} %get-tuple-element.37), channel_id=1, replica_groups=mesh['groups'=2,'lon'=8,'lat'=2] {'lon','lat'}, dimensions={0} | all-to-all | bytes 393216 | tf_op jit(solution)/shard_map/all_to_all | solution.py:560
  55.3 4.2 %last.1 = (f32[512,128]{1,0:T(8,128)}, f32[512,128]{1,0:T(8,128)}, f32[512,128]{1,0:T(8,128)}, f32[8,72,128]{2,1,0:T(8,128)S(1)}, f32[1,128]{1,0:T(1,128)S(1)}) custom-call(f32[16,8,128]{2,1,0:T(8,128)S(1)} %all_to_all.15.first, f32[16,24,128]{2,1,0:T(8,128)S(1)} %all_to_all.16.second, f32[512,8192]{1,0:T(8,128)S(1)} %copy-done.1, s32[512,128]{1,0:T(8,128)S(1)} %copy-done.5, ...), custom_call_target="tpu_custom_call" | custom-call | tf_op jit(solution)/shard_map/last/pallas_call | solution.py:510
  59.5 1.3 %collective-permute-start.3 = (f32[1,128]{1,0:T(1,128)S(1)}, f32[1,128]{1,0:T(1,128)S(1)}, u32[]{:S(2)}, u32[]{:S(2)}) collective-permute-start(f32[1,128]{1,0:T(1,128)S(1)} %get-tuple-element.45), channel_id=1, source_target_pairs={{1,0},{3,2},{5,4},{7,6},{9,8},{11,10},{13,12},{15,14},{17,16},{19,... | collective-permute-start | bytes 1544 | tf_op jit(solution)/shard_map/ppermute | solution.py:568
  60.8 1.7 %collective-permute-done.3 = f32[1,128]{1,0:T(1,128)S(1)} collective-permute-done((f32[1,128]{1,0:T(1,128)S(1)}, f32[1,128]{1,0:T(1,128)S(1)}, u32[]{:S(2)}, u32[]{:S(2)}) %collective-permute-start.3) | collective-permute-done | bytes 544 | tf_op jit(solution)/shard_map/ppermute | solution.py:568
  62.5 13.4 %all_to_all.17.parts = f32[8,72,128]{2,1,0:T(8,128)S(1)} all-to-all(f32[8,72,128]{2,1,0:T(8,128)S(1)} %dynamic_update_slice.3), channel_id=1, replica_groups=mesh['groups'=2,'lon'=8,'lat'=2] {'lon'}, dimensions={0} | all-to-all | bytes 589824 | tf_op jit(solution)/shard_map/all_to_all | solution.py:570
  75.9 1.1 %bands.1 = f32[3,1,64,1024]{3,2,1,0:T(8,128)} custom-call(f32[8,72,128]{2,1,0:T(8,128)S(1)} %all_to_all.17.parts), custom_call_target="tpu_custom_call" | custom-call | tf_op jit(solution)/shard_map/bands/pallas_call | solution.py:510
  (16 shorter events, 0.1 us)
Async XLA Ops:
  0.6 1.0 %copy-start.2 = (s32[512,128]{1,0:T(8,128)S(1)}, s32[512,128]{1,0:T(8,128)}, u32[]{:S(2)}) copy-start(s32[512,128]{1,0:T(8,128)} %ocean.7) | copy-start | bytes 786436
  1.6 0.9 %copy-start.4 = (s32[512,128]{1,0:T(8,128)S(1)}, s32[512,128]{1,0:T(8,128)}, u32[]{:S(2)}) copy-start(s32[512,128]{1,0:T(8,128)} %coarse.7) | copy-start | bytes 786436
  2.5 0.9 %copy-start.6 = (f32[512,128]{1,0:T(8,128)S(1)}, f32[512,128]{1,0:T(8,128)}, u32[]{:S(2)}) copy-start(f32[512,128]{1,0:T(8,128)} %lam.3) | copy-start | bytes 786436
  3.5 0.9 %copy-start.7 = (f32[512,128]{1,0:T(8,128)S(1)}, f32[512,128]{1,0:T(8,128)}, u32[]{:S(2)}) copy-start(f32[512,128]{1,0:T(8,128)} %east.3) | copy-start | bytes 786436
  4.4 0.9 %copy-start.8 = (f32[512,128]{1,0:T(8,128)S(1)}, f32[512,128]{1,0:T(8,128)}, u32[]{:S(2)}) copy-start(f32[512,128]{1,0:T(8,128)} %north.3) | copy-start | bytes 786436
  5.4 0.9 %copy-start.9 = (f32[512,128]{1,0:T(8,128)S(1)}, f32[512,128]{1,0:T(8,128)}, u32[]{:S(2)}) copy-start(f32[512,128]{1,0:T(8,128)} %depth.3) | copy-start | bytes 786436
  6.3 0.9 %copy-start.10 = (f32[512,128]{1,0:T(8,128)S(1)}, f32[512,128]{1,0:T(8,128)}, u32[]{:S(2)}) copy-start(f32[512,128]{1,0:T(8,128)} %drag.3) | copy-start | bytes 786436
  8.6 9.1 %collective-permute-start = (f32[8,512]{1,0:T(8,128)S(1)}, f32[8,512]{1,0:T(8,128)S(1)}, u32[]{:S(2)}, u32[]{:S(2)}) collective-permute-start(f32[8,512]{1,0:T(8,128)S(1)} %get-tuple-element.25.own_east), channel_id=1, source_target_pairs={{0,2},{2,4},{4,6},{6,8},{8,10},{10,12},{12,14},{14,0},{1,3},{3,5},... | collective-permute-start | bytes 49160 | tf_op jit(solution)/shard_map/ppermute | solution.py:534
  11.6 6.1 %collective-permute-start.1 = (f32[8,512]{1,0:T(8,128)S(1)}, f32[8,512]{1,0:T(8,128)S(1)}, u32[]{:S(2)}, u32[]{:S(2)}) collective-permute-start(f32[8,512]{1,0:T(8,128)S(1)} %get-tuple-element.26.own_west), channel_id=1, source_target_pairs={{2,0},{4,2},{6,4},{8,6},{10,8},{12,10},{14,12},{0,14},{3,1},{5,3},... | collective-permute-start | bytes 49160 | tf_op jit(solution)/shard_map/ppermute | solution.py:535
  14.7 3.0 %collective-permute-start.2 = (f32[8,128]{1,0:T(8,128)S(1)}, f32[8,128]{1,0:T(8,128)S(1)}, u32[]{:S(2)}, u32[]{:S(2)}) collective-permute-start(f32[8,128]{1,0:T(8,128)S(1)} %get-tuple-element.27.own_lat), channel_id=1, source_target_pairs={{0,1},{1,0},{2,3},{3,2},{4,5},{5,4},{6,7},{7,6},{8,9},{9,8},{10,11... | collective-permute-start | bytes 12296 | tf_op jit(solution)/shard_map/ppermute | solution.py:536
  29.5 5.8 %copy-start = (f32[512,8192]{1,0:T(8,128)S(1)}, f32[512,8192]{1,0:T(8,128)}, u32[]{:S(2)}) copy-start(f32[512,8192]{1,0:T(8,128)} %green.3) | copy-start | bytes 50331652
  35.2 0.9 %copy-start.3 = (s32[512,128]{1,0:T(8,128)S(1)}, s32[512,128]{1,0:T(8,128)}, u32[]{:S(2)}) copy-start(s32[512,128]{1,0:T(8,128)} %ocean.7) | copy-start | bytes 786436
  36.2 0.9 %copy-start.5 = (s32[512,128]{1,0:T(8,128)S(1)}, s32[512,128]{1,0:T(8,128)}, u32[]{:S(2)}) copy-start(s32[512,128]{1,0:T(8,128)} %coarse.7) | copy-start | bytes 786436
  37.1 18.2 %copy-start.1 = (f32[512,8192]{1,0:T(8,128)S(1)}, f32[512,8192]{1,0:T(8,128)}, u32[]{:S(2)}) copy-start(f32[512,8192]{1,0:T(8,128)} %green.3) | copy-start | bytes 50331652
  59.5 3.0 %collective-permute-start.3 = (f32[1,128]{1,0:T(1,128)S(1)}, f32[1,128]{1,0:T(1,128)S(1)}, u32[]{:S(2)}, u32[]{:S(2)}) collective-permute-start(f32[1,128]{1,0:T(1,128)S(1)} %get-tuple-element.45), channel_id=1, source_target_pairs={{1,0},{3,2},{5,4},{7,6},{9,8},{11,10},{13,12},{15,14},{17,16},{19,... | collective-permute-start | bytes 1544 | tf_op jit(solution)/shard_map/ppermute | solution.py:568

commit v2 on v1

--- a/solution.py
+++ b/solution.py
@@ -143,24 +143,25 @@
     )
 
 
-def green_product(green_ref, load_row, acc_ref):
-    points, total = green_ref.shape
+def green_product(green_ref, load_row, acc_ref, first=0, points=None):
+    total = green_ref.shape[1]
+    points = green_ref.shape[0] - first if points is None else points
     tall = 32
 
     def step(index, carry):
-        at = pl.ds(pl.multiple_of(index * tall, tall), tall)
+        start = pl.multiple_of(index * tall, tall)
         acc = jnp.zeros((tall, LANES), f32)
         for k in range(total // LANES):
-            acc = acc + green_ref[at, k * LANES : (k + 1) * LANES] * jnp.broadcast_to(
-                load_row(k), (tall, LANES)
-            )
-        acc_ref[at, :] = acc
+            acc = acc + green_ref[
+                pl.ds(first + start, tall), k * LANES : (k + 1) * LANES
+            ] * jnp.broadcast_to(load_row(k), (tall, LANES))
+        acc_ref[pl.ds(start, tall), :] = acc
         return carry
 
     lax.fori_loop(0, points // tall, step, 0)
     return lax.dot_general(
-        jnp.ones((8, LANES), f32), acc_ref[...], (((1,), (1,)), ((), ())), precision=HIGHEST,
-        preferred_element_type=f32,
+        jnp.ones((8, LANES), f32), acc_ref[0:points, :], (((1,), (1,)), ((), ())),
+        precision=HIGHEST, preferred_element_type=f32,
     )
 
 
@@ -188,7 +189,14 @@
     return jnp.concatenate([first, block[:-1]], 0)
 
 
-def pack_kernel(lam, east, north, depth, drag, ocean, coarse, to_east, to_west, to_lat, *, points):
+def pack_kernel(*refs, points):
+    far, (to_east, to_west, to_lat), near, done = refs[:7], refs[7:10], refs[10:17], refs[17]
+    copies = [pltpu.make_async_copy(far[k], near[k], done.at[k]) for k in range(7)]
+    for copy in copies:
+        copy.start()
+    for copy in copies:
+        copy.wait()
+    lam, east, north, depth, drag, ocean, coarse = near
     rows = lam.shape[0]
     lat = lax.axis_index("lat")
     sides = take_sides(
@@ -427,11 +435,11 @@
     payload[other, begin + tall : begin + tall + 1, :] = edge
 
 
-def last_kernel(
-    first, second, green, coarse, ocean, held, adj_u_in, adj_v_in, lines, lat_lines,
-    lam_out, east_out, north_out, payload, edge, acc, loads, *, points, n_lon, n_lat,
+def edge_kernel(
+    first, second, green, ocean, held, lines, lat_lines,
+    edge, loads, start_pot, put, north_line, acc, *, points, n_lon, n_lat,
 ):
-    rows = coarse.shape[0]
+    rows = held.shape[0]
     blocks = points // LANES
     tall = rows // LANES
     lat = lax.axis_index("lat")
@@ -450,7 +458,8 @@
             loads[here * blocks : (here + 1) * blocks, :] = (
                 total * first[here, blocks : 2 * blocks, :]
             )
-    potential = green_product(green, lambda k: loads[k : k + 1, :], acc)
+    potential = green_product(green, lambda k: loads[k : k + 1, :], acc, 0, LANES)
+    start_pot[...] = potential
     west, east, other = neighbours(n_lon, n_lat)
     begin = 4 * blocks
     lam_w = unfold(second[west, begin : begin + tall, :])
@@ -458,30 +467,43 @@
     lam_l = second[other, begin + tall : begin + tall + 1, :]
     add_e = lines[C_E : C_E + 1, :] * lam_e
     add_w = lines[G_W : G_W + 1, :] - lines[C_W : C_W + 1, :] * lam_w
-    put = put_sides(
-        jnp.concatenate([add_w, add_e, jnp.zeros((6, rows), f32)], 0),
-        [((0, slope_ratio), (1, -slope_ratio)), (None, (1, 1.0))],
-    )
     c_l = lat_lines[C_L : C_L + 1, :]
     g_l = lat_lines[G_L : G_L + 1, :]
     from_north = jnp.where(lat == 0, c_l * lam_l, 0.0)
     from_south = jnp.where(lat == 1, g_l - c_l * lam_l, 0.0)
+    put[...] = put_sides(
+        jnp.concatenate([add_w, add_e, jnp.zeros((6, rows), f32)], 0),
+        [((0, slope_ratio), (1, -slope_ratio)), (None, (1, 1.0))],
+    )
+    put[0:1, :LANES] = put[0:1, :LANES] + slope_ratio * from_south
+    put[rows - 1 : rows, :LANES] = put[rows - 1 : rows, :LANES] - slope_ratio * from_north
+    north_line[...] = from_north
+    edge[...] = ocean[0:1, :].astype(f32) * (
+        held[0:1, :] + put[0:1, :LANES] - attract_coef * potential[0:1, :]
+    )
+
+
+def last_kernel(
+    loads, start_pot, put, north_line, green, coarse, ocean, held, adj_u_in, adj_v_in,
+    lam_out, east_out, north_out, payload, acc, *, points, n_lon,
+):
+    rows = coarse.shape[0]
+    potential = start_pot[...]
+    if points > LANES:
+        rest = green_product(green, lambda k: loads[k : k + 1, :], acc, LANES, points - LANES)
+        potential = jnp.concatenate([potential, rest], 1)
     row = iota((STEP_ROWS, LANES), 0)
     for start in range(0, rows, STEP_ROWS):
         at = slice(start, start + STEP_ROWS)
         pot = spread(potential, local_ids(coarse[at, :], points))
-        value = held[at, :] + put[at, :LANES] - attract_coef * pot
         north = adj_v_in[at, :]
-        if start == 0:
-            value = value + jnp.where(row == 0, slope_ratio * from_south, 0.0)
         if start == rows - STEP_ROWS:
-            last = row == STEP_ROWS - 1
-            value = value - jnp.where(last, slope_ratio * from_north, 0.0)
-            north = north + jnp.where(last, from_north, 0.0)
-        lam_out[at, :] = ocean[at, :].astype(f32) * value
+            north = north + jnp.where(row == STEP_ROWS - 1, north_line[...], 0.0)
+        lam_out[at, :] = ocean[at, :].astype(f32) * (
+            held[at, :] + put[at, :LANES] - attract_coef * pot
+        )
         east_out[at, :] = adj_u_in[at, :] + put[at, LANES:]
         north_out[at, :] = north
-    edge[...] = lam_out[0:1, :]
     span = rows // n_lon
     for target in range(n_lon):
         stop = (target + 1) * span
@@ -505,15 +527,17 @@
         bands[2, 0, :, at] = parts[k, 1 : span + 1, :] - here
 
 
-def call(kernel, shapes, scratch, args, name):
+def call(kernel, shapes, scratch, args, name, far=False):
     vmem = pl.BlockSpec(memory_space=pltpu.VMEM)
+    shapes = [(shape, f32) if isinstance(shape[0], int) else shape for shape in shapes]
     return pl.pallas_call(
         kernel,
-        out_shape=[jax.ShapeDtypeStruct(shape, f32) for shape in shapes],
-        in_specs=[vmem] * len(args),
+        out_shape=[jax.ShapeDtypeStruct(shape, kind) for shape, kind in shapes],
+        in_specs=[pl.BlockSpec(memory_space=pltpu.HBM) if far else vmem] * len(args),
         out_specs=[vmem] * len(shapes),
         scratch_shapes=scratch,
-        compiler_params=pltpu.CompilerParams(vmem_limit_bytes=16 << 20),
+        compiler_params=pltpu.CompilerParams(vmem_limit_bytes=(52 << 20) if far else 16 << 20),
+        cost_estimate=pl.CostEstimate(flops=4 << 30, bytes_accessed=16 << 20, transcendentals=0),
         name=name,
     )(*args)
 
@@ -525,10 +549,12 @@
     owners = n_lon * n_lat
     grid = (rows, cols)
     fields = (lam_in, flux_east, flux_north, depth, drag, ocean, coarse_of)
-    to_east, to_west, to_lat = call(
+    to_east, to_west, to_lat, *fields = call(
         functools.partial(pack_kernel, points=points),
-        [(8, rows), (8, rows), (8, cols)], [], fields, "pack",
-    )
+        [(8, rows), (8, rows), (8, cols)] + [(grid, field.dtype) for field in fields],
+        [pltpu.SemaphoreType.DMA((7,))], fields, "pack", far=True,
+    )
+    ocean, coarse_of = fields[5:]
     forward = [(k, (k + 1) % n_lon) for k in range(n_lon)]
     backward = [(target, source) for source, target in forward]
     from_west = lax.ppermute(to_east, "lon", forward)
@@ -559,11 +585,17 @@
     )
     second = lax.all_to_all(payload, ("lon", "lat"), 0, 0, tiled=True)
     span = rows // n_lon
-    lam, east, north, payload, edge = call(
-        functools.partial(last_kernel, points=points, n_lon=n_lon, n_lat=n_lat),
-        [grid, grid, grid, (n_lon, span + 8, cols), (1, cols)],
-        [pltpu.VMEM((points, LANES), f32), pltpu.VMEM((owners * blocks, LANES), f32)],
-        (first, second, green, coarse_of, ocean, held, adj_u, adj_v, lines, lat_lines), "last",
+    edge, loads, start_pot, put, north_line = call(
+        functools.partial(edge_kernel, points=points, n_lon=n_lon, n_lat=n_lat),
+        [(1, cols), (owners * blocks, LANES), (8, LANES), (rows, 2 * cols), (1, cols)],
+        [pltpu.VMEM((LANES, LANES), f32)],
+        (first, second, green, ocean, held, lines, lat_lines), "edge",
+    )
+    lam, east, north, payload = call(
+        functools.partial(last_kernel, points=points, n_lon=n_lon),
+        [grid, grid, grid, (n_lon, span + 8, cols)],
+        [pltpu.VMEM((points, LANES), f32)],
+        (loads, start_pot, put, north_line, green, coarse_of, ocean, held, adj_u, adj_v), "last",
     )
     edge = lax.ppermute(edge, "lat", [(1, 0)])
     payload = lax.dynamic_update_slice(payload, edge[None], (n_lon - 1, span, 0))

time: 77.5 us -> 64.2 us (0.83)
  local copies, waits for them, and re-layouts: 14.3 us -> 0.05 us
  Pallas kernels: 16.5 us -> 18.6 us
  waiting for transfers between devices: 1.72 us -> 0.01 us
    unnamed x22 -> x8, local copies, waits for them, and re-layouts: 14.3 us -> 0.02 us
    pallas_call x6 -> x7, Pallas kernels: 16.5 us -> 18.6 us  [call(): pl.pallas_call(kernel, out_shape=[jax.ShapeDtypeStruct(shape, kind) for s...]
    ppermute x1, waiting for transfers between devices: 1.72 us -> 0.01 us  [body(): edge = lax.ppermute(edge, 'lat', [(1, 0)])]
  transfers between devices with their start and end apart: 4 -> 4, of which waited for: 1 -> 0; matrix products, arithmetic and copies ran while one was open for 0% -> 0% of each run, Pallas kernels for 4% -> 10%
where the time goes in v2:
time: 64.2 us; the launch traced here: 63.9 us
  blocking collectives  37.1 us (58%)
  Pallas kernels  18.6 us (29%)
  starting transfers between devices  7.42 us (12%)
  between operations  0.74 us (1%)
    pallas_call x7, Pallas kernels, call(): pl.pallas_call(kernel, out_shape=[jax.ShapeDtypeStruct(shape, kind) for s...  18.6 us
    all_to_all x1, blocking collectives, body(): parts = lax.all_to_all(payload, 'lon', 0, 0, tiled=True)  13.8 us
    all_to_all x1, blocking collectives, body(): first = lax.all_to_all(payload, ('lon', 'lat'), 0, 0, tiled=True)  11.7 us
    all_to_all x1, blocking collectives, body(): second = lax.all_to_all(payload, ('lon', 'lat'), 0, 0, tiled=True)  11.6 us
    ppermute x1, starting transfers between devices, body(): from_east = lax.ppermute(to_west, 'lon', backward)  3.1 us
    ppermute x1, starting transfers between devices, body(): from_west = lax.ppermute(to_east, 'lon', forward)  3.02 us
    ppermute x1, starting transfers between devices, body(): edge = lax.ppermute(edge, 'lat', [(1, 0)])  1.29 us
  transfers between devices with their start and end apart: 4, of which 0 were waited for; matrix products, arithmetic and copies ran while one was open for 0% of the time, Pallas kernels for 10%

profile of v2, /device:TPU:0, one launch (start us, length us, event | category | flops | bytes accessed | tf_op | source)
XLA Modules:
  0.0 63.9 jit_solution(9848280750789668762)
XLA Ops:
  0.6 2.9 %pack.1 = (f32[8,512]{1,0:T(8,128)S(1)}, f32[8,512]{1,0:T(8,128)S(1)}, f32[8,128]{1,0:T(8,128)S(1)}, f32[512,128]{1,0:T(8,128)S(1)}, f32[512,128]{1,0:T(8,128)S(...) custom-call(f32[512,128]{1,0:T(8,128)} %refs_0_.1, ...), custom_call_target="tpu_custom_call" | custom-call | flops 4294967296 | bytes 16777216 | tf_op jit(solution)/shard_map/pack/pallas_call | solution.py:533
  3.5 0.0 slice-start
  3.5 3.0 %collective-permute-start = (f32[8,512]{1,0:T(8,128)S(1)}, f32[8,512]{1,0:T(8,128)S(1)}, u32[]{:S(2)}, u32[]{:S(2)}) collective-permute-start(f32[8,512]{1,0:T(8,128)S(1)} %get-tuple-element.36.own_east), channel_id=1, source_target_pairs={{0,2},{2,4},{4,6},{6,8},{8,10},{10,12},{12,14},{14,0},{1,3},{3,5},... | collective-permute-start | bytes 49160 | tf_op jit(solution)/shard_map/ppermute | solution.py:560
  6.5 3.1 %collective-permute-start.1 = (f32[8,512]{1,0:T(8,128)S(1)}, f32[8,512]{1,0:T(8,128)S(1)}, u32[]{:S(2)}, u32[]{:S(2)}) collective-permute-start(f32[8,512]{1,0:T(8,128)S(1)} %get-tuple-element.37.own_west), channel_id=1, source_target_pairs={{2,0},{4,2},{6,4},{8,6},{10,8},{12,10},{14,12},{0,14},{3,1},{5,3},... | collective-permute-start | bytes 49160 | tf_op jit(solution)/shard_map/ppermute | solution.py:561
  9.6 0.0 collective-permute-start.2
  9.6 3.0 %inner.1 = (f32[512,128]{1,0:T(8,128)S(1)}, f32[512,128]{1,0:T(8,128)S(1)}, f32[512,128]{1,0:T(8,128)S(1)}, f32[512,128]{1,0:T(8,128)S(1)}, f32[512,128]{1,0:T(8,128)S(1)}, /*index=5*/f32[48,32]{1,0:T(8,128)S(1)}) custom-call(f32[512,128]{1,0:T(8,128)S(1)} %get-tuple-element.39.lam, f32[512,128]{1,0:T(8,128)S(1)} %get-tuple-element.40.east, ...), custom_call_target="tpu_custom_call" | custom-call | flops 4294967296 | bytes 16777216 | tf_op jit(solution)/shard_map/inner/pallas_call | solution.py:533
  12.7 0.0 collective-permute-done.2.from_lat
  12.7 0.0 collective-permute-done.from_west
  12.7 0.0 collective-permute-done.1.from_east
  12.7 0.0 slice-start.2
  12.7 0.0 slice-start.3
  12.7 0.3 rim.1
  13.0 11.7 %all_to_all.15.first = f32[16,8,128]{2,1,0:T(8,128)S(1)} all-to-all(f32[16,8,128]{2,1,0:T(8,128)S(1)} %get-tuple-element.47), channel_id=1, replica_groups=mesh['groups'=2,'lon'=8,'lat'=2] {'lon','lat'}, dimensions={0} | all-to-all | bytes 131072 | tf_op jit(solution)/shard_map/all_to_all | solution.py:573
  24.7 0.0 slice-done
  24.7 0.0 slice-done.1
  24.7 0.0 slice-done.2
  24.7 6.6 %second.1 = (f32[16,24,128]{2,1,0:T(8,128)S(1)}, f32[512,128]{1,0:T(8,128)S(1)}, f32[512,128]{1,0:T(8,128)S(1)}, f32[512,128]{1,0:T(8,128)S(1)}) custom-call(f32[16,8,128]{2,1,0:T(8,128)S(1)} %all_to_all.15.first, f32[512,8192]{1,0:T(8,128)S(1)} %bitcast.2, s32[512,128]{1,0:T(8,128)S(1)} %get-tuple-element.45.coarse, ...), custom_call_target="tpu_custom_call" | custom-call | flops 4294967296 | bytes 16777216 | tf_op jit(solution)/shard_map/second/pallas_call | solution.py:533
  31.3 11.6 %all_to_all.16.second = f32[16,24,128]{2,1,0:T(8,128)S(1)} all-to-all(f32[16,24,128]{2,1,0:T(8,128)S(1)} %get-tuple-element.55), channel_id=1, replica_groups=mesh['groups'=2,'lon'=8,'lat'=2] {'lon','lat'}, dimensions={0} | all-to-all | bytes 393216 | tf_op jit(solution)/shard_map/all_to_all | solution.py:586
  42.9 1.3 %edge.1 = (f32[1,128]{1,0:T(1,128)S(1)}, f32[64,128]{1,0:T(8,128)S(1)}, f32[8,128]{1,0:T(8,128)S(1)}, f32[512,256]{1,0:T(8,128)S(1)}, f32[1,128]{1,0:T(1,128)S(1)}) custom-call(f32[16,8,128]{2,1,0:T(8,128)S(1)} %all_to_all.15.first, f32[16,24,128]{2,1,0:T(8,128)S(1)} %all_to_all.16.second, f32[512,8192]{1,0:T(8,128)S(1)} %bitcast.2, ...), custom_call_target="tpu_custom_call" | custom-call | flops 4294967296 | bytes 16777216 | tf_op jit(solution)/shard_map/edge/pallas_call | solution.py:533
  44.2 1.3 %collective-permute-start.3 = (f32[1,128]{1,0:T(1,128)S(1)}, f32[1,128]{1,0:T(1,128)S(1)}, u32[]{:S(2)}, u32[]{:S(2)}) collective-permute-start(f32[1,128]{1,0:T(1,128)S(1)} %get-tuple-element.67), channel_id=1, source_target_pairs={{1,0},{3,2},{5,4},{7,6},{9,8},{11,10},{13,12},{15,14},{17,16},{19,... | collective-permute-start | bytes 1544 | tf_op jit(solution)/shard_map/ppermute | solution.py:600
  45.5 3.4 %last.1 = (f32[512,128]{1,0:T(8,128)}, f32[512,128]{1,0:T(8,128)}, f32[512,128]{1,0:T(8,128)}, f32[8,72,128]{2,1,0:T(8,128)S(1)}) custom-call(f32[64,128]{1,0:T(8,128)S(1)} %get-tuple-element.57.loads, f32[8,128]{1,0:T(8,128)S(1)} %get-tuple-element.58.start_pot, f32[512,256]{1,0:T(8,128)S(1)} %get-tuple-element.59.put, ...), custom_call_target="tpu_custom_call" | custom-call | flops 4294967296 | bytes 16777216 | tf_op jit(solution)/shard_map/last/pallas_call | solution.py:533
  48.9 0.0 collective-permute-done.3
  49.0 13.8 %all_to_all.17.parts = f32[8,72,128]{2,1,0:T(8,128)S(1)} all-to-all(f32[8,72,128]{2,1,0:T(8,128)S(1)} %dynamic_update_slice.3), channel_id=1, replica_groups=mesh['groups'=2,'lon'=8,'lat'=2] {'lon'}, dimensions={0} | all-to-all | bytes 589824 | tf_op jit(solution)/shard_map/all_to_all | solution.py:602
  62.8 1.1 %bands.1 = f32[3,1,64,1024]{3,2,1,0:T(8,128)} custom-call(f32[8,72,128]{2,1,0:T(8,128)S(1)} %all_to_all.17.parts), custom_call_target="tpu_custom_call" | custom-call | flops 4294967296 | bytes 16777216 | tf_op jit(solution)/shard_map/bands/pallas_call | solution.py:533
  (4 shorter events, 0.0 us)
Async XLA Ops:
  3.5 21.2 %slice-start = ((s8[16777216]{0:T(1024)(128)(4,1)}), s8[4194304]{0:T(1024)(128)(4,1)S(1)}, s32[]{:S(2)}) async-start(s8[16777216]{0:T(1024)(128)(4,1)} %bitcast.1), calls=%async_computation.3 | async-start | bytes 8388608
  3.5 9.2 %collective-permute-start = (f32[8,512]{1,0:T(8,128)S(1)}, f32[8,512]{1,0:T(8,128)S(1)}, u32[]{:S(2)}, u32[]{:S(2)}) collective-permute-start(f32[8,512]{1,0:T(8,128)S(1)} %get-tuple-element.36.own_east), channel_id=1, source_target_pairs={{0,2},{2,4},{4,6},{6,8},{8,10},{10,12},{12,14},{14,0},{1,3},{3,5},... | collective-permute-start | bytes 49160 | tf_op jit(solution)/shard_map/ppermute | solution.py:560
  6.5 6.2 %collective-permute-start.1 = (f32[8,512]{1,0:T(8,128)S(1)}, f32[8,512]{1,0:T(8,128)S(1)}, u32[]{:S(2)}, u32[]{:S(2)}) collective-permute-start(f32[8,512]{1,0:T(8,128)S(1)} %get-tuple-element.37.own_west), channel_id=1, source_target_pairs={{2,0},{4,2},{6,4},{8,6},{10,8},{12,10},{14,12},{0,14},{3,1},{5,3},... | collective-permute-start | bytes 49160 | tf_op jit(solution)/shard_map/ppermute | solution.py:561
  9.6 3.0 %collective-permute-start.2 = (f32[8,128]{1,0:T(8,128)S(1)}, f32[8,128]{1,0:T(8,128)S(1)}, u32[]{:S(2)}, u32[]{:S(2)}) collective-permute-start(f32[8,128]{1,0:T(8,128)S(1)} %get-tuple-element.38.own_lat), channel_id=1, source_target_pairs={{0,1},{1,0},{2,3},{3,2},{4,5},{5,4},{6,7},{7,6},{8,9},{9,8},{10,11... | collective-permute-start | bytes 12296 | tf_op jit(solution)/shard_map/ppermute | solution.py:562
  9.6 15.0 %slice-start.1 = ((s8[16777216]{0:T(1024)(128)(4,1)}), s8[4194304]{0:T(1024)(128)(4,1)S(1)}, s32[]{:S(2)}) async-start(s8[16777216]{0:T(1024)(128)(4,1)} %bitcast.1), calls=%async_computation.4 | async-start | bytes 8388608
  12.7 12.0 %slice-start.2 = ((s8[16777216]{0:T(1024)(128)(4,1)}), s8[4194304]{0:T(1024)(128)(4,1)S(1)}, s32[]{:S(2)}) async-start(s8[16777216]{0:T(1024)(128)(4,1)} %bitcast.1), calls=%async_computation.5 | async-start | bytes 8388608
  12.7 12.0 %slice-start.3 = ((s8[16777216]{0:T(1024)(128)(4,1)}), s8[4194304]{0:T(1024)(128)(4,1)S(1)}, s32[]{:S(2)}) async-start(s8[16777216]{0:T(1024)(128)(4,1)} %bitcast.1), calls=%async_computation.6 | async-start | bytes 8388608
  44.2 4.7 %collective-permute-start.3 = (f32[1,128]{1,0:T(1,128)S(1)}, f32[1,128]{1,0:T(1,128)S(1)}, u32[]{:S(2)}, u32[]{:S(2)}) collective-permute-start(f32[1,128]{1,0:T(1,128)S(1)} %get-tuple-element.67), channel_id=1, source_target_pairs={{1,0},{3,2},{5,4},{7,6},{9,8},{11,10},{13,12},{15,14},{17,16},{19,... | collective-permute-start | bytes 1544 | tf_op jit(solution)/shard_map/ppermute | solution.py:600

commit v3 on v2

v3 whole, which is shorter than its diff:
```python
import functools

import jax
import jax.numpy as jnp
from jax import lax
from jax.experimental import pallas as pl
from jax.experimental.pallas import tpu as pltpu
from jax.sharding import PartitionSpec as P

f32 = jnp.float32
bf16 = jnp.bfloat16
i32 = jnp.int32

LANES = 128
LOW = 32
HIGH = 16
PIECES = 2
SEG_ROWS = 128
STEP_ROWS = 64

flux_ratio = 0.25
slope_ratio = 0.25
drag_step = 1.0
attract_coef = 0.5

LAM, DEPTH, DRAG, OCEAN, POINT, FLUX = range(6)
ADJ, RATIO, GAIN, BASE, MASK, OWN_ID, FAR_ID = range(7)
ADJ_L, C_L, G_L, ID_L, OWN_L = range(5)


def iota(shape, dim):
    return lax.broadcasted_iota(i32, shape, dim)


def roll_east(x):
    return pltpu.roll(x, LANES - 1, 1)


def roll_west(x):
    return pltpu.roll(x, 1, 1)


def local_ids(ids, points):
    return lax.bitwise_and(ids, points - 1)


def bf16_pieces(values, count=PIECES):
    out = []
    for piece in range(count):
        top = values.astype(bf16).astype(f32)
        out.append(top)
        if piece < count - 1:
            values = values - top
    return out


def one_hots(ids, points):
    blocks = points // LANES
    high = lax.shift_right_logical(ids, 5)
    high = lax.bitwise_and(high, 3) * blocks + lax.shift_right_logical(high, 2)
    low = lax.bitwise_and(ids, LOW - 1)
    high_iota = iota((HIGH, LANES), 0)
    low_iota = iota((LOW, LANES), 0)
    left, right = [], []
    for row in range(ids.shape[0]):
        mask = jnp.broadcast_to(high[row : row + 1], (HIGH, LANES)) == high_iota
        left.append(jnp.where(mask, 1.0, 0.0).astype(bf16))
        mask = jnp.broadcast_to(low[row : row + 1], (LOW, LANES)) == low_iota
        right.append(jnp.where(mask, 1.0, 0.0).astype(bf16))
    return jnp.concatenate(left, 1), jnp.concatenate(right, 1)


def segment_part(values, left, right, with_counts=False):
    parts = []
    for piece in bf16_pieces(values):
        line = jnp.concatenate(
            [
                jnp.broadcast_to(piece[row : row + 1], (HIGH, LANES)).astype(bf16)
                for row in range(values.shape[0])
            ],
            1,
        )
        parts.append(left * line)
    if with_counts:
        parts.append(left)
    return lax.dot_general(
        jnp.concatenate(parts, 0), right, (((1,), (1,)), ((), ())), preferred_element_type=f32
    )


def segment_few(values, ids, points):
    return sum_pieces(segment_part(values, *one_hots(ids, points)))


def sum_pieces(parts):
    total = parts[:HIGH]
    for piece in range(1, PIECES):
        total = total + parts[piece * HIGH : (piece + 1) * HIGH]
    return total


def as_points(table, points):
    blocks = points // LANES
    return jnp.concatenate([table[q * blocks : (q + 1) * blocks] for q in range(4)], 1)


def fold(line):
    return jnp.concatenate(
        [line[:, k * LANES : (k + 1) * LANES] for k in range(line.shape[1] // LANES)], 0
    )


def unfold(block):
    return jnp.concatenate([block[k : k + 1] for k in range(block.shape[0])], 1)


def take_sides(block, count=3):
    sub, lane = iota((8, LANES), 0), iota((8, LANES), 1)
    pick = ((sub == 0) & (lane == 0)) | ((sub == 1) & (lane == LANES - 1))
    pick = pick.astype(f32).astype(bf16)
    out = None
    for piece in reversed(bf16_pieces(block, count)):
        part = lax.dot_general(
            pick, piece.astype(bf16), (((1,), (1,)), ((), ())), preferred_element_type=f32
        )
        out = part if out is None else out + part
    return out


def put_sides(pair, entries):
    half = pair.shape[0] // 2
    lines = jnp.concatenate([unfold(pair[:half]), unfold(pair[half:])], 0)
    rows = lines.shape[1]
    pieces = bf16_pieces(lines, 3)
    stack = jnp.concatenate(pieces + [jnp.zeros((2, rows), f32)], 0)
    sub, lane = iota((8, LANES), 0), iota((8, LANES), 1)
    west = (sub < 6) & (lax.bitwise_and(sub, 1) == 0) & (lane == 0)
    east = (sub < 6) & (lax.bitwise_and(sub, 1) == 1) & (lane == LANES - 1)
    picks = [jnp.where(west, first, jnp.where(east, last, 0.0)) for first, last in entries]
    return lax.dot_general(
        stack, jnp.concatenate(picks, 1), (((0,), (0,)), ((), ())), preferred_element_type=f32
    )


def green_product(green_ref, load_row, acc_ref, first=0, points=None):
    total = green_ref.shape[1]
    points = green_ref.shape[0] - first if points is None else points
    tall = LANES

    def step(index, carry):
        start = pl.multiple_of(index * tall, tall)
        acc = jnp.zeros((tall, LANES), f32)
        for k in range(total // LANES):
            acc = acc + green_ref[
                pl.ds(first + start, tall), k * LANES : (k + 1) * LANES
            ] * jnp.broadcast_to(load_row(k), (tall, LANES))
        acc_ref[pl.ds(start, tall), :] = acc
        return carry

    lax.fori_loop(0, points // tall, step, 0)
    out = None
    for piece in reversed(bf16_pieces(acc_ref[0:points, :], 3)):
        part = lax.dot_general(
            jnp.ones((8, LANES), bf16), piece.astype(bf16), (((1,), (1,)), ((), ())),
            preferred_element_type=f32,
        )
        out = part if out is None else out + part
    return out


def spread(potential, ids):
    points = potential.shape[1]
    rows = ids.shape[0]
    low = lax.bitwise_and(ids, LANES - 1)
    block = lax.shift_right_logical(ids, 7)
    out = None
    for k in range(points // LANES):
        table = potential[:, k * LANES : (k + 1) * LANES]
        table = jnp.broadcast_to(table[None], (rows // 8, 8, LANES)).reshape(rows, LANES)
        value = jnp.take_along_axis(table, low, axis=1, mode="promise_in_bounds")
        out = value if out is None else jnp.where(block == k, value, out)
    return out


def next_rows(ref, start, count):
    if start + count < ref.shape[0]:
        return ref[start + 1 : start + count + 1, :]
    return jnp.concatenate([ref[start + 1 :, :], jnp.zeros((1, LANES), ref.dtype)], 0)


def south_rows(first, block):
    return jnp.concatenate([first, block[:-1]], 0)


def pack_kernel(*refs, points):
    far, (to_east, to_west, to_lat), near, done = refs[:7], refs[7:10], refs[10:17], refs[17]
    copies = [pltpu.make_async_copy(far[k], near[k], done.at[k]) for k in range(7)]
    for copy in copies:
        copy.start()
    lam, east, north, depth, drag, ocean, coarse = near
    rows = lam.shape[0]
    tall = rows // LANES
    lat = lax.axis_index("lat")
    order = (
        (LAM, 0, lam, 3), (FLUX, 1, east, 3), (None, 2, north, 0), (DEPTH, 3, depth, 3),
        (DRAG, 4, drag, 3), (OCEAN, 5, ocean, 1), (POINT, 6, coarse, 2),
    )
    for field, index, ref, pieces in order:
        copies[index].wait()
        if field is None:
            continue
        block = ref[...]
        if field == POINT:
            block = local_ids(block, points)
        sides = take_sides(block.astype(f32), pieces)
        at = slice(field * tall, (field + 1) * tall)
        to_west[at, :] = fold(sides[0:1])
        to_east[at, :] = fold(sides[1:2])

    def border(row):
        return jnp.concatenate(
            [
                lam[row : row + 1, :],
                depth[row : row + 1, :],
                drag[row : row + 1, :],
                ocean[row : row + 1, :].astype(f32),
                local_ids(coarse[row : row + 1, :], points).astype(f32),
                north[row : row + 1, :],
                jnp.zeros((2, LANES), f32),
            ],
            0,
        )

    to_lat[...] = jnp.where(lat == 0, border(rows - 1), border(0))


def inner_kernel(
    lam, east, north, depth, drag, ocean, coarse,
    held, gu, cu, gv, cv, sums, left, right, held_sides, source, *, points,
):
    rows = lam.shape[0]
    inner = iota((STEP_ROWS, LANES), 1) < LANES - 1
    carry = jnp.zeros((1, LANES), f32)
    for start in range(0, rows, STEP_ROWS):
        at = slice(start, start + STEP_ROWS)
        lam_c, depth_c, drag_c = lam[at, :], depth[at, :], drag[at, :]
        ocean_c = ocean[at, :].astype(f32)
        damp = jnp.where(
            inner,
            ocean_c * roll_east(ocean_c) / (1.0 + drag_step * 0.5 * (drag_c + roll_east(drag_c))),
            0.0,
        )
        ratio = damp * (flux_ratio * 0.5) * (depth_c + roll_east(depth_c))
        adj_u = damp * east[at, :] + ratio * (roll_east(lam_c) - lam_c)
        cu[at, :] = ratio
        gu[at, :] = damp * adj_u
        ocean_n = next_rows(ocean, start, STEP_ROWS).astype(f32)
        damp = (
            ocean_c
            * ocean_n
            / (1.0 + drag_step * 0.5 * (drag_c + next_rows(drag, start, STEP_ROWS)))
        )
        ratio = damp * (flux_ratio * 0.5) * (depth_c + next_rows(depth, start, STEP_ROWS))
        adj_v = damp * north[at, :] + ratio * (next_rows(lam, start, STEP_ROWS) - lam_c)
        cv[at, :] = ratio
        gv[at, :] = damp * adj_v
        src = slope_ratio * (roll_west(adj_u) - adj_u + south_rows(carry, adj_v) - adj_v)
        carry = adj_v[STEP_ROWS - 1 :]
        source[at, :] = src
        held[at, :] = lam_c + src
    total = jnp.zeros(sums.shape, f32)
    for start in range(0, rows, SEG_ROWS):
        at = slice(start, start + SEG_ROWS)
        cells = slice(start * LANES, (start + SEG_ROWS) * LANES)
        high, low = one_hots(local_ids(coarse[at, :], points), points)
        left[:, cells] = high
        right[:, cells] = low
        total = total + segment_part(source[at, :], high, low, True)
    sums[...] = total
    sides = take_sides(held[...])
    held_sides[...] = jnp.concatenate([fold(sides[0:1]), fold(sides[1:2])], 0)


def face(low, high, flux):
    damp = low[OCEAN] * high[OCEAN] / (1.0 + drag_step * 0.5 * (low[DRAG] + high[DRAG]))
    ratio = damp * (flux_ratio * 0.5) * (low[DEPTH] + high[DEPTH])
    adj = damp * flux + ratio * (high[LAM] - low[LAM])
    return adj, ratio, damp * adj


def west_rows():
    return iota((8, LANES), 0) < 4


def rim_kernel(
    own_east, own_west, own_lat, from_west, from_east, from_lat, sums, held_sides,
    payload, faces, lat_lines, *, points,
):
    lat = lax.axis_index("lat")
    half = held_sides.shape[0] // 2

    def pair(west, east):
        return [
            jnp.concatenate(
                [west[k * half : (k + 1) * half, :], east[k * half : (k + 1) * half, :]], 0
            )
            for k in range(6)
        ]

    own, far = pair(own_west, own_east), pair(from_west, from_east)
    is_west = west_rows()
    low = [jnp.where(is_west, there, here) for here, there in zip(own, far)]
    high = [jnp.where(is_west, here, there) for here, there in zip(own, far)]
    adj, ratio, gain = face(low, high, low[FLUX])
    mine, other = own_lat[...], from_lat[...]
    lower = jnp.where(lat == 0, mine, other)
    upper = jnp.where(lat == 0, other, mine)
    lower = [lower[k : k + 1] for k in range(6)]
    upper = [upper[k : k + 1] for k in range(6)]
    adj_l, c_l, g_l = face(lower, upper, lower[FLUX])
    lat_lines[...] = jnp.concatenate(
        [
            adj_l, c_l, g_l, other[POINT : POINT + 1], mine[POINT : POINT + 1],
            jnp.zeros((3, LANES), f32),
        ],
        0,
    )
    sign = jnp.where(is_west, slope_ratio, -slope_ratio)
    sign_l = jnp.where(lat == 0, -slope_ratio, slope_ratio)
    flow = sign * adj
    sub, lane = lax.bitwise_and(iota((8, LANES), 0), half - 1), iota((8, LANES), 1)
    corner = ((lat == 0) & (sub == half - 1) & (lane == LANES - 1)) | (
        (lat == 1) & (sub == 0) & (lane == 0)
    )
    at_corner = jnp.where(
        is_west,
        jnp.broadcast_to(adj_l[:, 0:1], (8, LANES)),
        jnp.broadcast_to(adj_l[:, LANES - 1 :], (8, LANES)),
    )
    faces[ADJ] = adj
    faces[RATIO] = ratio
    faces[GAIN] = gain
    faces[BASE] = held_sides[...] + flow + jnp.where(corner, sign_l * at_corner, 0.0)
    faces[MASK] = own[OCEAN]
    faces[OWN_ID] = own[POINT]
    faces[FAR_ID] = far[POINT]
    pad = jnp.zeros((1, LANES), f32)
    values = jnp.concatenate([flow, sign_l * adj_l, pad], 0)
    ids = jnp.concatenate([own[POINT], mine[POINT : POINT + 1], pad], 0).astype(i32)
    total = sum_pieces(sums[...]) + segment_few(values, ids, points)
    counts = as_points(sums[PIECES * HIGH : (PIECES + 1) * HIGH, :], points)
    inverse = 1.0 / counts
    loads = as_points(total, points) * inverse
    part = jnp.concatenate([loads, inverse], 0)
    if part.shape[0] < 8:
        part = jnp.concatenate([part, jnp.zeros((8 - part.shape[0], LANES), f32)], 0)
    for target in range(payload.shape[0]):
        payload[target] = part


def neighbours(n_lon, n_lat):
    lon, lat = lax.axis_index("lon"), lax.axis_index("lat")
    west = lax.rem(lon + n_lon - 1, n_lon) * n_lat + lat
    east = lax.rem(lon + 1, n_lon) * n_lat + lat
    other = lon * n_lat + (1 - lat)
    return west, east, other


def second_kernel(
    first, green, coarse, ocean, held_in, gu, cu, gv, cv, left, right, faces, lat_lines,
    payload, held, adj_u_out, adj_v_out, lam_sides, lam_edge, acc, lam, source,
    *, points, n_lon, n_lat,
):
    rows = coarse.shape[0]
    blocks = points // LANES
    lat = lax.axis_index("lat")
    south_end = jnp.where(lat == 1, 1.0, 0.0)
    north_end = jnp.where(lat == 0, 1.0, 0.0)
    potential = green_product(
        green, lambda k: first[k // blocks, k % blocks : k % blocks + 1, :], acc
    )
    put = put_sides(faces[ADJ], [(slope_ratio, -slope_ratio)])
    adj_l = lat_lines[ADJ_L : ADJ_L + 1, :]
    c_l = lat_lines[C_L : C_L + 1, :]
    g_l = lat_lines[G_L : G_L + 1, :]
    row = iota((STEP_ROWS, LANES), 0)
    lam[rows : rows + 8, :] = jnp.zeros((8, LANES), f32)
    for start in range(0, rows, STEP_ROWS):
        at = slice(start, start + STEP_ROWS)
        pot = spread(potential, local_ids(coarse[at, :], points))
        value = held_in[at, :] + put[at, :] - attract_coef * pot
        if start == 0:
            value = value + jnp.where(row == 0, south_end * slope_ratio * adj_l, 0.0)
        if start == rows - STEP_ROWS:
            value = value - jnp.where(row == STEP_ROWS - 1, north_end * slope_ratio * adj_l, 0.0)
        lam[at, :] = ocean[at, :].astype(f32) * value
    carry = jnp.zeros((1, LANES), f32)
    for start in range(0, rows, STEP_ROWS):
        at = slice(start, start + STEP_ROWS)
        lam_c = lam[at, :]
        adj_u = gu[at, :] + cu[at, :] * (roll_east(lam_c) - lam_c)
        adj_v = gv[at, :] + cv[at, :] * (lam[start + 1 : start + STEP_ROWS + 1, :] - lam_c)
        src = slope_ratio * (roll_west(adj_u) - adj_u + south_rows(carry, adj_v) - adj_v)
        carry = adj_v[STEP_ROWS - 1 :]
        adj_u_out[at, :] = adj_u
        adj_v_out[at, :] = adj_v
        source[at, :] = src
        held[at, :] = lam_c + src
    is_west = west_rows()
    sides = faces[MASK] * (
        faces[BASE] - attract_coef * spread(potential, faces[OWN_ID].astype(i32))
    )
    lam_sides[...] = sides
    pull = faces[RATIO] * sides
    flow = slope_ratio * jnp.where(is_west, pull, pull - faces[GAIN])
    edge = jnp.where(lat == 0, lam[rows - 1 : rows, :], lam[0:1, :])
    lam_edge[...] = edge
    pull = c_l * edge
    flow_l = slope_ratio * jnp.where(lat == 0, pull - g_l, pull)
    pad = jnp.zeros((1, LANES), f32)
    total = segment_part(
        jnp.concatenate([flow, flow_l, pad], 0),
        *one_hots(
            jnp.concatenate([faces[OWN_ID], lat_lines[OWN_L : OWN_L + 1, :], pad], 0).astype(i32),
            points,
        ),
    )
    for start in range(0, rows, SEG_ROWS):
        cells = slice(start * LANES, (start + SEG_ROWS) * LANES)
        total = total + segment_part(
            source[start : start + SEG_ROWS, :], left[:, cells], right[:, cells]
        )
    own = as_points(sum_pieces(total), points)
    far_id = faces[FAR_ID].astype(i32)
    half = far_id.shape[0] // 2

    def away(values, ids):
        return as_points(segment_few(-values, ids, points), points)

    west_part = away(flow[:half], far_id[:half])
    east_part = away(flow[half:], far_id[half:])
    lat_part = away(
        jnp.concatenate([flow_l, pad], 0),
        jnp.concatenate([lat_lines[ID_L : ID_L + 1, :], pad], 0).astype(i32),
    )
    part = jnp.concatenate([own, east_part, west_part, lat_part], 0)
    spare = payload.shape[1] - part.shape[0]
    part = jnp.concatenate([part, jnp.zeros((spare, LANES), f32)], 0)
    for target in range(payload.shape[0]):
        payload[target] = part
    west, east, other = neighbours(n_lon, n_lat)
    begin = 4 * blocks
    payload[west, begin : begin + half, :] = sides[:half]
    payload[east, begin : begin + half, :] = sides[half:]
    payload[other, begin + half : begin + half + 1, :] = edge


def edge_kernel(
    first, second, green, ocean, held, faces, lat_lines, lam_sides, lam_edge,
    edge, loads, start_pot, put, north_line, acc, *, points, n_lon, n_lat,
):
    rows = held.shape[0]
    blocks = points // LANES
    half = rows // LANES
    lat = lax.axis_index("lat")
    for lon in range(n_lon):
        for band in range(n_lat):
            here = lon * n_lat + band
            west = (lon - 1) % n_lon * n_lat + band
            east = (lon + 1) % n_lon * n_lat + band
            other = lon * n_lat + 1 - band
            total = (
                second[here, :blocks, :]
                + second[west, blocks : 2 * blocks, :]
                + second[east, 2 * blocks : 3 * blocks, :]
                + second[other, 3 * blocks : 4 * blocks, :]
            )
            loads[here * blocks : (here + 1) * blocks, :] = (
                total * first[here, blocks : 2 * blocks, :]
            )
    potential = green_product(green, lambda k: loads[k : k + 1, :], acc, 0, LANES)
    start_pot[...] = potential
    west, east, other = neighbours(n_lon, n_lat)
    begin = 4 * blocks
    far = jnp.concatenate(
        [second[west, begin : begin + half, :], second[east, begin : begin + half, :]], 0
    )
    rise = jnp.where(west_rows(), lam_sides[...] - far, far - lam_sides[...])
    adj = faces[GAIN] + faces[RATIO] * rise
    put[...] = put_sides(adj, [(slope_ratio, -slope_ratio), (0.0, 1.0)])
    rise = second[other, begin + half : begin + half + 1, :] - lam_edge[...]
    adj_l = lat_lines[G_L : G_L + 1, :] + lat_lines[C_L : C_L + 1, :] * jnp.where(
        lat == 0, rise, -rise
    )
    from_north = jnp.where(lat == 0, adj_l, 0.0)
    from_south = jnp.where(lat == 1, adj_l, 0.0)
    put[0:1, :LANES] = put[0:1, :LANES] + slope_ratio * from_south
    put[rows - 1 : rows, :LANES] = put[rows - 1 : rows, :LANES] - slope_ratio * from_north
    north_line[...] = from_north
    edge[...] = ocean[0:1, :].astype(f32) * (
        held[0:1, :] + put[0:1, :LANES] - attract_coef * potential[0:1, :]
    )


def last_kernel(
    loads, start_pot, put, north_line, green, coarse, ocean, held, adj_u_in, adj_v_in,
    lam_out, east_out, north_out, payload, acc, *, points, n_lon,
):
    rows = coarse.shape[0]
    potential = start_pot[...]
    if points > LANES:
        rest = green_product(green, lambda k: loads[k : k + 1, :], acc, LANES, points - LANES)
        potential = jnp.concatenate([potential, rest], 1)
    row = iota((STEP_ROWS, LANES), 0)
    for start in range(0, rows, STEP_ROWS):
        at = slice(start, start + STEP_ROWS)
        pot = spread(potential, local_ids(coarse[at, :], points))
        north = adj_v_in[at, :]
        if start == rows - STEP_ROWS:
            north = north + jnp.where(row == STEP_ROWS - 1, north_line[...], 0.0)
        lam_out[at, :] = ocean[at, :].astype(f32) * (
            held[at, :] + put[at, :LANES] - attract_coef * pot
        )
        east_out[at, :] = adj_u_in[at, :] + put[at, LANES:]
        north_out[at, :] = north
    span = rows // n_lon
    for target in range(n_lon):
        stop = (target + 1) * span
        payload[target, :span, :] = lam_out[target * span : stop, :]
        if target < n_lon - 1:
            payload[target, span : span + 8, :] = lam_out[stop : stop + 8, :]
        else:
            payload[target, span : span + 8, :] = jnp.zeros((8, LANES), f32)


def bands_kernel(parts, bands):
    count, tall, _ = parts.shape
    span = tall - 8
    lane = iota((span, LANES), 1)
    for k in range(count):
        here = parts[k, :span, :]
        east = parts[(k + 1) % count, :span, :]
        at = slice(k * LANES, (k + 1) * LANES)
        bands[0, 0, :, at] = here
        bands[1, 0, :, at] = jnp.where(lane == LANES - 1, roll_east(east), roll_east(here)) - here
        bands[2, 0, :, at] = parts[k, 1 : span + 1, :] - here


def call(kernel, shapes, scratch, args, name, far=False):
    vmem = pl.BlockSpec(memory_space=pltpu.VMEM)
    shapes = [(shape, f32) if isinstance(shape[0], int) else shape for shape in shapes]
    return pl.pallas_call(
        kernel,
        out_shape=[jax.ShapeDtypeStruct(shape, kind) for shape, kind in shapes],
        in_specs=[pl.BlockSpec(memory_space=pltpu.HBM) if far else vmem] * len(args),
        out_specs=[vmem] * len(shapes),
        scratch_shapes=scratch,
        compiler_params=pltpu.CompilerParams(vmem_limit_bytes=(52 << 20) if far else 16 << 20),
        cost_estimate=pl.CostEstimate(flops=4 << 30, bytes_accessed=16 << 20, transcendentals=0),
        name=name,
    )(*args)


def body(n_lon, n_lat, lam_in, flux_east, flux_north, depth, drag, ocean, coarse_of, green):
    rows, cols = lam_in.shape
    points = green.shape[0]
    blocks = points // LANES
    owners = n_lon * n_lat
    grid = (rows, cols)
    fields = (lam_in, flux_east, flux_north, depth, drag, ocean, coarse_of)
    tall = rows // LANES
    to_east, to_west, to_lat, *fields = call(
        functools.partial(pack_kernel, points=points),
        [(6 * tall, cols), (6 * tall, cols), (8, cols)]
        + [(grid, field.dtype) for field in fields],
        [pltpu.SemaphoreType.DMA((7,))], fields, "pack", far=True,
    )
    ocean, coarse_of = fields[5:]
    forward = [(k, (k + 1) % n_lon) for k in range(n_lon)]
    backward = [(target, source) for source, target in forward]
    from_west = lax.ppermute(to_east, "lon", forward)
    from_east = lax.ppermute(to_west, "lon", backward)
    from_lat = lax.ppermute(to_lat, "lat", [(0, 1), (1, 0)])
    held, gu, cu, gv, cv, sums, left, right, held_sides = call(
        functools.partial(inner_kernel, points=points),
        [grid] * 5
        + [((PIECES + 1) * HIGH, LOW), ((HIGH, rows * cols), bf16), ((LOW, rows * cols), bf16)]
        + [(2 * tall, cols)],
        [pltpu.VMEM(grid, f32)], fields, "inner",
    )
    payload, faces, lat_lines = call(
        functools.partial(rim_kernel, points=points),
        [(owners, 8, LANES), (7, 2 * tall, cols), (8, cols)], [],
        (to_east, to_west, to_lat, from_west, from_east, from_lat, sums, held_sides), "rim",
    )
    first = lax.all_to_all(payload, ("lon", "lat"), 0, 0, tiled=True)
    deep = -(-(4 * blocks + tall + 1) // 8) * 8
    payload, held, adj_u, adj_v, lam_sides, lam_edge = call(
        functools.partial(second_kernel, points=points, n_lon=n_lon, n_lat=n_lat),
        [(owners, deep, LANES), grid, grid, grid, (2 * tall, cols), (1, cols)],
        [
            pltpu.VMEM((points, LANES), f32),
            pltpu.VMEM((rows + 8, cols), f32),
            pltpu.VMEM(grid, f32),
        ],
        (first, green, coarse_of, ocean, held, gu, cu, gv, cv, left, right, faces, lat_lines),
        "second",
    )
    second = lax.all_to_all(payload, ("lon", "lat"), 0, 0, tiled=True)
    span = rows // n_lon
    edge, loads, start_pot, put, north_line = call(
        functools.partial(edge_kernel, points=points, n_lon=n_lon, n_lat=n_lat),
        [(1, cols), (owners * blocks, LANES), (8, LANES), (rows, 2 * cols), (1, cols)],
        [pltpu.VMEM((LANES, LANES), f32)],
        (first, second, green, ocean, held, faces, lat_lines, lam_sides, lam_edge), "edge",
    )
    lam, east, north, payload = call(
        functools.partial(last_kernel, points=points, n_lon=n_lon),
        [grid, grid, grid, (n_lon, span + 8, cols)],
        [pltpu.VMEM((points, LANES), f32)],
        (loads, start_pot, put, north_line, green, coarse_of, ocean, held, adj_u, adj_v), "last",
    )
    edge = lax.ppermute(edge, "lat", [(1, 0)])
    payload = lax.dynamic_update_slice(payload, edge[None], (n_lon - 1, span, 0))
    parts = lax.all_to_all(payload, "lon", 0, 0, tiled=True)
    (bands,) = call(bands_kernel, [(3, 1, span, n_lon * cols)], [], (parts,), "bands")
    return lam, east, north, bands


def solution(mesh):
    cells = P(("groups", "lat"), "lon")
    n_lon, n_lat = mesh.shape["lon"], mesh.shape["lat"]
    return jax.shard_map(
        functools.partial(body, n_lon, n_lat),
        mesh=mesh,
        in_specs=(cells,) * 6 + (P("lat", "lon"), P(("lon", "lat"), None)),
        out_specs=(cells,) * 3 + (P(None, ("groups", "lat"), "lon", None),),
        check_vma=False,
    )
```

time: 64.2 us -> 61.5 us (0.958)
  Pallas kernels: 18.6 us -> 15.8 us
    pallas_call x7, Pallas kernels: 18.6 us -> 15.8 us  [call(): pl.pallas_call(kernel, out_shape=[jax.ShapeDtypeStruct(shape, kind) for s...]
where the time goes in v3:
time: 61.5 us; the launch traced here: 61.3 us
  blocking collectives  37.3 us (61%)
  Pallas kernels  15.8 us (26%)
  starting transfers between devices  7.42 us (12%)
  between operations  0.74 us (1%)
    pallas_call x7, Pallas kernels, call(): pl.pallas_call(kernel, out_shape=[jax.ShapeDtypeStruct(shape, kind) for s...  15.8 us
    all_to_all x1, blocking collectives, body(): parts = lax.all_to_all(payload, 'lon', 0, 0, tiled=True)  13.8 us
    all_to_all x1, blocking collectives, body(): first = lax.all_to_all(payload, ('lon', 'lat'), 0, 0, tiled=True)  11.9 us
    all_to_all x1, blocking collectives, body(): second = lax.all_to_all(payload, ('lon', 'lat'), 0, 0, tiled=True)  11.6 us
    ppermute x1, starting transfers between devices, body(): from_east = lax.ppermute(to_west, 'lon', backward)  3.1 us
    ppermute x1, starting transfers between devices, body(): from_west = lax.ppermute(to_east, 'lon', forward)  3.02 us
    ppermute x1, starting transfers between devices, body(): edge = lax.ppermute(edge, 'lat', [(1, 0)])  1.29 us
  transfers between devices with their start and end apart: 4, of which 0 were waited for; matrix products, arithmetic and copies ran while one was open for 0% of the time, Pallas kernels for 10%

profile of v3, /device:TPU:0, one launch (start us, length us, event | category | flops | bytes accessed | tf_op | source)
XLA Modules:
  0.0 61.3 jit_solution(7455519637634062114)
XLA Ops:
  0.6 2.3 %pack.1 = (f32[24,128]{1,0:T(8,128)S(1)}, f32[24,128]{1,0:T(8,128)S(1)}, f32[8,128]{1,0:T(8,128)S(1)}, f32[512,128]{1,0:T(8,128)S(1)}, f32[512,128]{1,0:T(8,128)...) custom-call(f32[512,128]{1,0:T(8,128)} %refs_0_.1, ...), custom_call_target="tpu_custom_call" | custom-call | flops 4294967296 | bytes 16777216 | tf_op jit(solution)/shard_map/pack/pallas_call | solution.py:552
  2.9 3.0 %collective-permute-start = (f32[24,128]{1,0:T(8,128)S(1)}, f32[24,128]{1,0:T(8,128)S(1)}, u32[]{:S(2)}, u32[]{:S(2)}) collective-permute-start(f32[24,128]{1,0:T(8,128)S(1)} %get-tuple-element.41.own_east), channel_id=1, source_target_pairs={{0,2},{2,4},{4,6},{6,8},{8,10},{10,12},{12,14},{14,0},{1,3},{3,5},... | collective-permute-start | bytes 36872 | tf_op jit(solution)/shard_map/ppermute | solution.py:581
  5.9 3.1 %collective-permute-start.1 = (f32[24,128]{1,0:T(8,128)S(1)}, f32[24,128]{1,0:T(8,128)S(1)}, u32[]{:S(2)}, u32[]{:S(2)}) collective-permute-start(f32[24,128]{1,0:T(8,128)S(1)} %get-tuple-element.42.own_west), channel_id=1, source_target_pairs={{2,0},{4,2},{6,4},{8,6},{10,8},{12,10},{14,12},{0,14},{3,1},{5,3},... | collective-permute-start | bytes 36872 | tf_op jit(solution)/shard_map/ppermute | solution.py:582
  9.0 0.0 collective-permute-start.2
  9.0 2.8 %inner.1 = (f32[512,128]{1,0:T(8,128)S(1)}, f32[512,128]{1,0:T(8,128)S(1)}, f32[512,128]{1,0:T(8,128)S(1)}, f32[512,128]{1,0:T(8,128)S(1)}, f32[512,128]{1,0:T(8...) custom-call(f32[512,128]{1,0:T(8,128)S(1)} %get-tuple-element.44.lam, ...), custom_call_target="tpu_custom_call" | custom-call | flops 4294967296 | bytes 16777216 | tf_op jit(solution)/shard_map/inner/pallas_call | solution.py:552
  11.8 0.0 collective-permute-done.2.from_lat
  11.8 0.0 collective-permute-done.from_west
  11.8 0.0 collective-permute-done.1.from_east
  11.8 0.0 slice-start.2
  11.9 0.0 slice-start.3
  11.9 0.3 rim.1
  12.1 11.9 %all_to_all.15.first = f32[16,8,128]{2,1,0:T(8,128)S(1)} all-to-all(f32[16,8,128]{2,1,0:T(8,128)S(1)} %get-tuple-element.53), channel_id=1, replica_groups=mesh['groups'=2,'lon'=8,'lat'=2] {'lon','lat'}, dimensions={0} | all-to-all | bytes 131072 | tf_op jit(solution)/shard_map/all_to_all | solution.py:596
  24.0 0.0 slice-done
  24.0 0.0 slice-done.1
  24.0 0.0 slice-done.2
  24.0 0.0 slice-done.3
  24.0 5.6 %second.1 = (f32[16,24,128]{2,1,0:T(8,128)S(1)}, f32[512,128]{1,0:T(8,128)S(1)}, f32[512,128]{1,0:T(8,128)S(1)}, f32[512,128]{1,0:T(8,128)S(1)}, f32[8,128]{1,0:T(8,128)S(1)}, /*index=5*/f32[1,128]{1,0:T(1,128)S(1)}) custom-call(f32[16,8,128]{2,1,0:T(8,128)S(1)} %all_to_all.15.first, f32[512,8192]{1,0:T(8,128)S(1)} %bitcast.2, ...), custom_call_target="tpu_custom_call" | custom-call | flops 4294967296 | bytes 16777216 | tf_op jit(solution)/shard_map/second/pallas_call | solution.py:552
  29.7 11.6 %all_to_all.16.second = f32[16,24,128]{2,1,0:T(8,128)S(1)} all-to-all(f32[16,24,128]{2,1,0:T(8,128)S(1)} %get-tuple-element.63), channel_id=1, replica_groups=mesh['groups'=2,'lon'=8,'lat'=2] {'lon','lat'}, dimensions={0} | all-to-all | bytes 393216 | tf_op jit(solution)/shard_map/all_to_all | solution.py:609
  41.3 0.6 %edge.1 = (f32[1,128]{1,0:T(1,128)S(1)}, f32[64,128]{1,0:T(8,128)S(1)}, f32[8,128]{1,0:T(8,128)S(1)}, f32[512,256]{1,0:T(8,128)S(1)}, f32[1,128]{1,0:T(1,128)S(1)}) custom-call(f32[16,8,128]{2,1,0:T(8,128)S(1)} %all_to_all.15.first, f32[16,24,128]{2,1,0:T(8,128)S(1)} %all_to_all.16.second, f32[512,8192]{1,0:T(8,128)S(1)} %bitcast.2, ...), custom_call_target="tpu_custom_call" | custom-call | flops 4294967296 | bytes 16777216 | tf_op jit(solution)/shard_map/edge/pallas_call | solution.py:552
  41.9 1.3 %collective-permute-start.3 = (f32[1,128]{1,0:T(1,128)S(1)}, f32[1,128]{1,0:T(1,128)S(1)}, u32[]{:S(2)}, u32[]{:S(2)}) collective-permute-start(f32[1,128]{1,0:T(1,128)S(1)} %get-tuple-element.77), channel_id=1, source_target_pairs={{1,0},{3,2},{5,4},{7,6},{9,8},{11,10},{13,12},{15,14},{17,16},{19,... | collective-permute-start | bytes 1544 | tf_op jit(solution)/shard_map/ppermute | solution.py:623
  43.2 3.1 %last.1 = (f32[512,128]{1,0:T(8,128)}, f32[512,128]{1,0:T(8,128)}, f32[512,128]{1,0:T(8,128)}, f32[8,72,128]{2,1,0:T(8,128)S(1)}) custom-call(f32[64,128]{1,0:T(8,128)S(1)} %get-tuple-element.67.loads, f32[8,128]{1,0:T(8,128)S(1)} %get-tuple-element.68.start_pot, f32[512,256]{1,0:T(8,128)S(1)} %get-tuple-element.69.put, ...), custom_call_target="tpu_custom_call" | custom-call | flops 4294967296 | bytes 16777216 | tf_op jit(solution)/shard_map/last/pallas_call | solution.py:552
  46.3 0.0 collective-permute-done.3
  46.4 13.8 %all_to_all.17.parts = f32[8,72,128]{2,1,0:T(8,128)S(1)} all-to-all(f32[8,72,128]{2,1,0:T(8,128)S(1)} %dynamic_update_slice.3), channel_id=1, replica_groups=mesh['groups'=2,'lon'=8,'lat'=2] {'lon'}, dimensions={0} | all-to-all | bytes 589824 | tf_op jit(solution)/shard_map/all_to_all | solution.py:625
  60.2 1.1 %bands.1 = f32[3,1,64,1024]{3,2,1,0:T(8,128)} custom-call(f32[8,72,128]{2,1,0:T(8,128)S(1)} %all_to_all.17.parts), custom_call_target="tpu_custom_call" | custom-call | flops 4294967296 | bytes 16777216 | tf_op jit(solution)/shard_map/bands/pallas_call | solution.py:552
  (4 shorter events, 0.0 us)
Async XLA Ops:
  2.9 8.9 %collective-permute-start = (f32[24,128]{1,0:T(8,128)S(1)}, f32[24,128]{1,0:T(8,128)S(1)}, u32[]{:S(2)}, u32[]{:S(2)}) collective-permute-start(f32[24,128]{1,0:T(8,128)S(1)} %get-tuple-element.41.own_east), channel_id=1, source_target_pairs={{0,2},{2,4},{4,6},{6,8},{8,10},{10,12},{12,14},{14,0},{1,3},{3,5},... | collective-permute-start | bytes 36872 | tf_op jit(solution)/shard_map/ppermute | solution.py:581
  5.9 5.9 %collective-permute-start.1 = (f32[24,128]{1,0:T(8,128)S(1)}, f32[24,128]{1,0:T(8,128)S(1)}, u32[]{:S(2)}, u32[]{:S(2)}) collective-permute-start(f32[24,128]{1,0:T(8,128)S(1)} %get-tuple-element.42.own_west), channel_id=1, source_target_pairs={{2,0},{4,2},{6,4},{8,6},{10,8},{12,10},{14,12},{0,14},{3,1},{5,3},... | collective-permute-start | bytes 36872 | tf_op jit(solution)/shard_map/ppermute | solution.py:582
  9.0 2.8 %collective-permute-start.2 = (f32[8,128]{1,0:T(8,128)S(1)}, f32[8,128]{1,0:T(8,128)S(1)}, u32[]{:S(2)}, u32[]{:S(2)}) collective-permute-start(f32[8,128]{1,0:T(8,128)S(1)} %get-tuple-element.43.own_lat), channel_id=1, source_target_pairs={{0,1},{1,0},{2,3},{3,2},{4,5},{5,4},{6,7},{7,6},{8,9},{9,8},{10,11... | collective-permute-start | bytes 12296 | tf_op jit(solution)/shard_map/ppermute | solution.py:583
  9.0 15.0 %slice-start = ((s8[16777216]{0:T(1024)(128)(4,1)}), s8[4194304]{0:T(1024)(128)(4,1)S(1)}, s32[]{:S(2)}) async-start(s8[16777216]{0:T(1024)(128)(4,1)} %bitcast.1), calls=%async_computation.3 | async-start | bytes 8388608
  9.0 15.0 %slice-start.1 = ((s8[16777216]{0:T(1024)(128)(4,1)}), s8[4194304]{0:T(1024)(128)(4,1)S(1)}, s32[]{:S(2)}) async-start(s8[16777216]{0:T(1024)(128)(4,1)} %bitcast.1), calls=%async_computation.4 | async-start | bytes 8388608
  11.8 12.2 %slice-start.2 = ((s8[16777216]{0:T(1024)(128)(4,1)}), s8[4194304]{0:T(1024)(128)(4,1)S(1)}, s32[]{:S(2)}) async-start(s8[16777216]{0:T(1024)(128)(4,1)} %bitcast.1), calls=%async_computation.5 | async-start | bytes 8388608
  11.9 12.2 %slice-start.3 = ((s8[16777216]{0:T(1024)(128)(4,1)}), s8[4194304]{0:T(1024)(128)(4,1)S(1)}, s32[]{:S(2)}) async-start(s8[16777216]{0:T(1024)(128)(4,1)} %bitcast.1), calls=%async_computation.6 | async-start | bytes 8388608
  41.9 4.4 %collective-permute-start.3 = (f32[1,128]{1,0:T(1,128)S(1)}, f32[1,128]{1,0:T(1,128)S(1)}, u32[]{:S(2)}, u32[]{:S(2)}) collective-permute-start(f32[1,128]{1,0:T(1,128)S(1)} %get-tuple-element.77), channel_id=1, source_target_pairs={{1,0},{3,2},{5,4},{7,6},{9,8},{11,10},{13,12},{15,14},{17,16},{19,... | collective-permute-start | bytes 1544 | tf_op jit(solution)/shard_map/ppermute | solution.py:623

commit v4 on v3

--- a/solution.py
+++ b/solution.py
@@ -15,8 +15,8 @@
 LOW = 32
 HIGH = 16
 PIECES = 2
-SEG_ROWS = 128
-STEP_ROWS = 64
+SEG_ROWS = 256
+STEP_ROWS = 128
 
 flux_ratio = 0.25
 slope_ratio = 0.25
@@ -425,11 +425,12 @@
             points,
         ),
     )
-    for start in range(0, rows, SEG_ROWS):
-        cells = slice(start * LANES, (start + SEG_ROWS) * LANES)
-        total = total + segment_part(
-            source[start : start + SEG_ROWS, :], left[:, cells], right[:, cells]
-        )
+    def add(index, total):
+        at = pl.ds(pl.multiple_of(index * SEG_ROWS, SEG_ROWS), SEG_ROWS)
+        cells = pl.ds(pl.multiple_of(index * SEG_ROWS * LANES, SEG_ROWS * LANES), SEG_ROWS * LANES)
+        return total + segment_part(source[at, :], left[:, cells], right[:, cells])
+
+    total = lax.fori_loop(0, rows // SEG_ROWS, add, total)
     own = as_points(sum_pieces(total), points)
     far_id = faces[FAR_ID].astype(i32)
     half = far_id.shape[0] // 2
@@ -443,16 +444,16 @@
         jnp.concatenate([flow_l, pad], 0),
         jnp.concatenate([lat_lines[ID_L : ID_L + 1, :], pad], 0).astype(i32),
     )
+    west, east, other = neighbours(n_lon, n_lat)
     part = jnp.concatenate([own, east_part, west_part, lat_part], 0)
-    spare = payload.shape[1] - part.shape[0]
-    part = jnp.concatenate([part, jnp.zeros((spare, LANES), f32)], 0)
-    for target in range(payload.shape[0]):
-        payload[target] = part
-    west, east, other = neighbours(n_lon, n_lat)
     begin = 4 * blocks
-    payload[west, begin : begin + half, :] = sides[:half]
-    payload[east, begin : begin + half, :] = sides[half:]
-    payload[other, begin + half : begin + half + 1, :] = edge
+    deep = begin + half
+    edge_rows = jnp.concatenate([edge, jnp.zeros((half - 1, LANES), f32)], 0)
+    for target in range(n_lon * n_lat):
+        shared = jnp.where(
+            target == west, sides[:half], jnp.where(target == east, sides[half:], edge_rows)
+        )
+        payload[target * deep : (target + 1) * deep, :] = jnp.concatenate([part, shared], 0)
 
 
 def edge_kernel(
@@ -462,33 +463,35 @@
     rows = held.shape[0]
     blocks = points // LANES
     half = rows // LANES
+    deep = 4 * blocks + half
     lat = lax.axis_index("lat")
+
+    def received(owner, kind):
+        start = owner * deep + kind * blocks
+        return second[start : start + blocks, :]
+
     for lon in range(n_lon):
         for band in range(n_lat):
             here = lon * n_lat + band
             west = (lon - 1) % n_lon * n_lat + band
             east = (lon + 1) % n_lon * n_lat + band
             other = lon * n_lat + 1 - band
-            total = (
-                second[here, :blocks, :]
-                + second[west, blocks : 2 * blocks, :]
-                + second[east, 2 * blocks : 3 * blocks, :]
-                + second[other, 3 * blocks : 4 * blocks, :]
-            )
+            total = received(here, 0) + received(west, 1) + received(east, 2) + received(other, 3)
             loads[here * blocks : (here + 1) * blocks, :] = (
                 total * first[here, blocks : 2 * blocks, :]
             )
     potential = green_product(green, lambda k: loads[k : k + 1, :], acc, 0, LANES)
     start_pot[...] = potential
     west, east, other = neighbours(n_lon, n_lat)
-    begin = 4 * blocks
-    far = jnp.concatenate(
-        [second[west, begin : begin + half, :], second[east, begin : begin + half, :]], 0
-    )
+
+    def shared(owner, count):
+        return second[pl.ds(owner * deep + 4 * blocks, count), :]
+
+    far = jnp.concatenate([shared(west, half), shared(east, half)], 0)
     rise = jnp.where(west_rows(), lam_sides[...] - far, far - lam_sides[...])
     adj = faces[GAIN] + faces[RATIO] * rise
     put[...] = put_sides(adj, [(slope_ratio, -slope_ratio), (0.0, 1.0)])
-    rise = second[other, begin + half : begin + half + 1, :] - lam_edge[...]
+    rise = shared(other, 1) - lam_edge[...]
     adj_l = lat_lines[G_L : G_L + 1, :] + lat_lines[C_L : C_L + 1, :] * jnp.where(
         lat == 0, rise, -rise
     )
@@ -503,57 +506,78 @@
 
 
 def last_kernel(
-    loads, start_pot, put, north_line, green, coarse, ocean, held, adj_u_in, adj_v_in,
-    lam_out, east_out, north_out, payload, acc, *, points, n_lon,
+    loads, start_pot, put, green, coarse, ocean, held, lam_out, payload, acc, *, points, n_lon,
 ):
     rows = coarse.shape[0]
     potential = start_pot[...]
     if points > LANES:
         rest = green_product(green, lambda k: loads[k : k + 1, :], acc, LANES, points - LANES)
         potential = jnp.concatenate([potential, rest], 1)
-    row = iota((STEP_ROWS, LANES), 0)
     for start in range(0, rows, STEP_ROWS):
         at = slice(start, start + STEP_ROWS)
         pot = spread(potential, local_ids(coarse[at, :], points))
-        north = adj_v_in[at, :]
-        if start == rows - STEP_ROWS:
-            north = north + jnp.where(row == STEP_ROWS - 1, north_line[...], 0.0)
         lam_out[at, :] = ocean[at, :].astype(f32) * (
             held[at, :] + put[at, :LANES] - attract_coef * pot
         )
-        east_out[at, :] = adj_u_in[at, :] + put[at, LANES:]
-        north_out[at, :] = north
     span = rows // n_lon
     for target in range(n_lon):
-        stop = (target + 1) * span
-        payload[target, :span, :] = lam_out[target * span : stop, :]
+        start = target * (span + 1)
+        payload[start : start + span, :] = lam_out[target * span : (target + 1) * span, :]
         if target < n_lon - 1:
-            payload[target, span : span + 8, :] = lam_out[stop : stop + 8, :]
+            stop = (target + 1) * span
+            payload[start + span : start + span + 1, :] = lam_out[stop : stop + 1, :]
         else:
-            payload[target, span : span + 8, :] = jnp.zeros((8, LANES), f32)
-
-
-def bands_kernel(parts, bands):
-    count, tall, _ = parts.shape
-    span = tall - 8
+            payload[start + span : start + span + 1, :] = jnp.zeros((1, LANES), f32)
+
+
+def bands_kernel(
+    parts, lam, adj_u, adj_v, put, north_line,
+    lam_out, east_out, north_out, bands, east, north, planes, done, *, count,
+):
+    span = parts.shape[0] // count - 1
+    rows = lam.shape[0]
+    copies = [
+        pltpu.make_async_copy(lam, lam_out, done.at[0]),
+        pltpu.make_async_copy(east, east_out, done.at[1]),
+        pltpu.make_async_copy(north, north_out, done.at[2]),
+    ] + [
+        pltpu.make_async_copy(planes.at[k], bands.at[k, 0], done.at[3 + k]) for k in range(3)
+    ]
+    copies[0].start()
     lane = iota((span, LANES), 1)
     for k in range(count):
-        here = parts[k, :span, :]
-        east = parts[(k + 1) % count, :span, :]
+        start = k * (span + 1)
+        planes[0, :, k * LANES : (k + 1) * LANES] = parts[start : start + span, :]
+    copies[3].start()
+    for k in range(count):
+        start = k * (span + 1)
+        here = parts[start : start + span, :]
+        planes[2, :, k * LANES : (k + 1) * LANES] = parts[start + 1 : start + 1 + span, :] - here
+    copies[5].start()
+    for k in range(count):
         at = slice(k * LANES, (k + 1) * LANES)
-        bands[0, 0, :, at] = here
-        bands[1, 0, :, at] = jnp.where(lane == LANES - 1, roll_east(east), roll_east(here)) - here
-        bands[2, 0, :, at] = parts[k, 1 : span + 1, :] - here
-
-
-def call(kernel, shapes, scratch, args, name, far=False):
+        here = planes[0, :, at]
+        after = (k + 1) % count
+        there = planes[0, :, after * LANES : (after + 1) * LANES]
+        planes[1, :, at] = jnp.where(lane == LANES - 1, roll_east(there), roll_east(here)) - here
+    copies[4].start()
+    east[...] = adj_u[...] + put[:, LANES:]
+    copies[1].start()
+    north[...] = adj_v[...]
+    north[rows - 1 : rows, :] = adj_v[rows - 1 : rows, :] + north_line[...]
+    copies[2].start()
+    for copy in copies:
+        copy.wait()
+
+
+def call(kernel, shapes, scratch, args, name, far=False, far_out=False):
     vmem = pl.BlockSpec(memory_space=pltpu.VMEM)
     shapes = [(shape, f32) if isinstance(shape[0], int) else shape for shape in shapes]
     return pl.pallas_call(
         kernel,
         out_shape=[jax.ShapeDtypeStruct(shape, kind) for shape, kind in shapes],
         in_specs=[pl.BlockSpec(memory_space=pltpu.HBM) if far else vmem] * len(args),
-        out_specs=[vmem] * len(shapes),
+        out_specs=[pl.BlockSpec(memory_space=pl.ANY) if far_out else vmem] * len(shapes),
         scratch_shapes=scratch,
         compiler_params=pltpu.CompilerParams(vmem_limit_bytes=(52 << 20) if far else 16 << 20),
         cost_estimate=pl.CostEstimate(flops=4 << 30, bytes_accessed=16 << 20, transcendentals=0),
@@ -594,10 +618,10 @@
         (to_east, to_west, to_lat, from_west, from_east, from_lat, sums, held_sides), "rim",
     )
     first = lax.all_to_all(payload, ("lon", "lat"), 0, 0, tiled=True)
-    deep = -(-(4 * blocks + tall + 1) // 8) * 8
+    deep = 4 * blocks + tall
     payload, held, adj_u, adj_v, lam_sides, lam_edge = call(
         functools.partial(second_kernel, points=points, n_lon=n_lon, n_lat=n_lat),
-        [(owners, deep, LANES), grid, grid, grid, (2 * tall, cols), (1, cols)],
+        [(owners * deep, LANES), grid, grid, grid, (2 * tall, cols), (1, cols)],
         [
             pltpu.VMEM((points, LANES), f32),
             pltpu.VMEM((rows + 8, cols), f32),
@@ -606,7 +630,9 @@
         (first, green, coarse_of, ocean, held, gu, cu, gv, cv, left, right, faces, lat_lines),
         "second",
     )
-    second = lax.all_to_all(payload, ("lon", "lat"), 0, 0, tiled=True)
+    second = lax.all_to_all(
+        payload.reshape(owners, deep, 1, LANES), ("lon", "lat"), 0, 0, tiled=True
+    ).reshape(payload.shape)
     span = rows // n_lon
     edge, loads, start_pot, put, north_line = call(
         functools.partial(edge_kernel, points=points, n_lon=n_lon, n_lat=n_lat),
@@ -614,17 +640,30 @@
         [pltpu.VMEM((LANES, LANES), f32)],
         (first, second, green, ocean, held, faces, lat_lines, lam_sides, lam_edge), "edge",
     )
-    lam, east, north, payload = call(
+    lam, payload = call(
         functools.partial(last_kernel, points=points, n_lon=n_lon),
-        [grid, grid, grid, (n_lon, span + 8, cols)],
+        [grid, (rows + n_lon, cols)],
         [pltpu.VMEM((points, LANES), f32)],
-        (loads, start_pot, put, north_line, green, coarse_of, ocean, held, adj_u, adj_v), "last",
+        (loads, start_pot, put, green, coarse_of, ocean, held), "last",
     )
     edge = lax.ppermute(edge, "lat", [(1, 0)])
-    payload = lax.dynamic_update_slice(payload, edge[None], (n_lon - 1, span, 0))
-    parts = lax.all_to_all(payload, "lon", 0, 0, tiled=True)
-    (bands,) = call(bands_kernel, [(3, 1, span, n_lon * cols)], [], (parts,), "bands")
-    return lam, east, north, bands
+    payload = lax.dynamic_update_slice(payload, edge, (rows + n_lon - 1, 0))
+    parts = lax.all_to_all(
+        payload.reshape(n_lon, span + 1, 1, LANES), "lon", 0, 0, tiled=True
+    ).reshape(payload.shape)
+    return tuple(
+        call(
+            functools.partial(bands_kernel, count=n_lon),
+            [grid, grid, grid, (3, 1, span, n_lon * cols)],
+            [
+                pltpu.VMEM(grid, f32),
+                pltpu.VMEM(grid, f32),
+                pltpu.VMEM((3, span, n_lon * cols), f32),
+                pltpu.SemaphoreType.DMA((6,)),
+            ],
+            (parts, lam, adj_u, adj_v, put, north_line), "bands", far_out=True,
+        )
+    )
 
 
 def solution(mesh):

time: 61.5 us -> 59.2 us (0.963)
  Pallas kernels: 15.8 us -> 14.3 us
  blocking collectives: 37.3 us -> 36.4 us
    pallas_call x7, Pallas kernels: 15.8 us -> 14.3 us  [call(): pl.pallas_call(kernel, out_shape=[jax.ShapeDtypeStruct(shape, kind) for s...]
    all_to_all x2, blocking collectives: 25.4 us -> 24.5 us  [the longest x1 13.5 us: body(): lax.all_to_all(payload.reshape(n_lon, span + 1, 1, LANES), 'lon', 0, 0, t...]
  transfers between devices with their start and end apart: 4 -> 4, of which waited for: 0 -> 0; matrix products, arithmetic and copies ran while one was open for 0% -> 0% of each run, Pallas kernels for 10% -> 9%
where the time goes in v4:
time: 59.2 us; the launch traced here: 58.9 us
  blocking collectives  36.4 us (61%)
  Pallas kernels  14.3 us (24%)
  starting transfers between devices  7.42 us (13%)
  between operations  0.75 us (1%)
    pallas_call x7, Pallas kernels, call(): pl.pallas_call(kernel, out_shape=[jax.ShapeDtypeStruct(shape, kind) for s...  14.3 us
    all_to_all x1, blocking collectives, body(): lax.all_to_all(payload.reshape(n_lon, span + 1, 1, LANES), 'lon', 0, 0, t...  13.5 us
    all_to_all x1, blocking collectives, body(): first = lax.all_to_all(payload, ('lon', 'lat'), 0, 0, tiled=True)  11.8 us
    all_to_all x1, blocking collectives, body(): lax.all_to_all(payload.reshape(owners, deep, 1, LANES), ('lon', 'lat'), 0...  11.1 us
    ppermute x1, starting transfers between devices, body(): from_east = lax.ppermute(to_west, 'lon', backward)  3.1 us
    ppermute x1, starting transfers between devices, body(): from_west = lax.ppermute(to_east, 'lon', forward)  3.02 us
    ppermute x1, starting transfers between devices, body(): edge = lax.ppermute(edge, 'lat', [(1, 0)])  1.29 us
  transfers between devices with their start and end apart: 4, of which 0 were waited for; matrix products, arithmetic and copies ran while one was open for 0% of the time, Pallas kernels for 9%

profile of v4, /device:TPU:0, one launch (start us, length us, event | category | flops | bytes accessed | tf_op | source)
XLA Modules:
  0.0 58.9 jit_solution(2167162521801218930)
XLA Ops:
  0.6 2.3 %pack.1 = (f32[24,128]{1,0:T(8,128)S(1)}, f32[24,128]{1,0:T(8,128)S(1)}, f32[8,128]{1,0:T(8,128)S(1)}, f32[512,128]{1,0:T(8,128)S(1)}, f32[512,128]{1,0:T(8,128)...) custom-call(f32[512,128]{1,0:T(8,128)} %refs_0_.1, ...), custom_call_target="tpu_custom_call" | custom-call | flops 4294967296 | bytes 16777216 | tf_op jit(solution)/shard_map/pack/pallas_call | solution.py:576
  2.9 3.0 %collective-permute-start = (f32[24,128]{1,0:T(8,128)S(1)}, f32[24,128]{1,0:T(8,128)S(1)}, u32[]{:S(2)}, u32[]{:S(2)}) collective-permute-start(f32[24,128]{1,0:T(8,128)S(1)} %get-tuple-element.39.own_east), channel_id=1, source_target_pairs={{0,2},{2,4},{4,6},{6,8},{8,10},{10,12},{12,14},{14,0},{1,3},{3,5},... | collective-permute-start | bytes 36872 | tf_op jit(solution)/shard_map/ppermute | solution.py:605
  5.9 3.1 %collective-permute-start.1 = (f32[24,128]{1,0:T(8,128)S(1)}, f32[24,128]{1,0:T(8,128)S(1)}, u32[]{:S(2)}, u32[]{:S(2)}) collective-permute-start(f32[24,128]{1,0:T(8,128)S(1)} %get-tuple-element.40.own_west), channel_id=1, source_target_pairs={{2,0},{4,2},{6,4},{8,6},{10,8},{12,10},{14,12},{0,14},{3,1},{5,3},... | collective-permute-start | bytes 36872 | tf_op jit(solution)/shard_map/ppermute | solution.py:606
  9.0 0.0 collective-permute-start.2
  9.0 2.8 %inner.1 = (f32[512,128]{1,0:T(8,128)S(1)}, f32[512,128]{1,0:T(8,128)S(1)}, f32[512,128]{1,0:T(8,128)S(1)}, f32[512,128]{1,0:T(8,128)S(1)}, f32[512,128]{1,0:T(8...) custom-call(f32[512,128]{1,0:T(8,128)S(1)} %get-tuple-element.42.lam, ...), custom_call_target="tpu_custom_call" | custom-call | flops 4294967296 | bytes 16777216 | tf_op jit(solution)/shard_map/inner/pallas_call | solution.py:576
  11.9 0.0 collective-permute-done.2.from_lat
  11.9 0.0 collective-permute-done.from_west
  11.9 0.0 collective-permute-done.1.from_east
  11.9 0.0 slice-start.2
  11.9 0.0 slice-start.3
  11.9 0.3 rim.1
  12.2 11.8 %all_to_all.15.first = f32[16,8,128]{2,1,0:T(8,128)S(1)} all-to-all(f32[16,8,128]{2,1,0:T(8,128)S(1)} %get-tuple-element.51), channel_id=1, replica_groups=mesh['groups'=2,'lon'=8,'lat'=2] {'lon','lat'}, dimensions={0} | all-to-all | bytes 131072 | tf_op jit(solution)/shard_map/all_to_all | solution.py:620
  24.0 0.0 slice-done
  24.0 0.0 slice-done.1
  24.0 0.0 slice-done.2
  24.0 0.0 slice-done.3
  24.0 4.9 %second.1 = (f32[320,128]{1,0:T(8,128)S(1)}, f32[512,128]{1,0:T(8,128)S(1)}, f32[512,128]{1,0:T(8,128)S(1)}, f32[512,128]{1,0:T(8,128)S(1)}, f32[8,128]{1,0:T(8,128)S(1)}, /*index=5*/f32[1,128]{1,0:T(1,128)S(1)}) custom-call(f32[16,8,128]{2,1,0:T(8,128)S(1)} %all_to_all.15.first, f32[512,8192]{1,0:T(8,128)S(1)} %bitcast.5, ...), custom_call_target="tpu_custom_call" | custom-call | flops 4294967296 | bytes 16777216 | tf_op jit(solution)/shard_map/second/pallas_call | solution.py:576
  29.0 11.1 %all_to_all.16 = f32[16,20,1,128]{3,2,1,0:T(1,128)S(1)} all-to-all(f32[16,20,1,128]{3,2,1,0:T(1,128)S(1)} %bitcast.9), channel_id=1, replica_groups=mesh['groups'=2,'lon'=8,'lat'=2] {'lon','lat'}, dimensions={0} | all-to-all | bytes 327680 | tf_op jit(solution)/shard_map/all_to_all | solution.py:633
  40.0 0.6 %edge.1 = (f32[1,128]{1,0:T(1,128)S(1)}, f32[64,128]{1,0:T(8,128)S(1)}, f32[8,128]{1,0:T(8,128)S(1)}, f32[512,256]{1,0:T(8,128)S(1)}, f32[1,128]{1,0:T(1,128)S(1)}) custom-call(f32[16,8,128]{2,1,0:T(8,128)S(1)} %all_to_all.15.first, f32[320,128]{1,0:T(8,128)S(1)} %bitcast.6, f32[512,8192]{1,0:T(8,128)S(1)} %bitcast.5, ...), custom_call_target="tpu_custom_call" | custom-call | flops 4294967296 | bytes 16777216 | tf_op jit(solution)/shard_map/edge/pallas_call | solution.py:576
  40.7 1.3 %collective-permute-start.3 = (f32[1,128]{1,0:T(1,128)S(1)}, f32[1,128]{1,0:T(1,128)S(1)}, u32[]{:S(2)}, u32[]{:S(2)}) collective-permute-start(f32[1,128]{1,0:T(1,128)S(1)} %get-tuple-element.69), channel_id=1, source_target_pairs={{1,0},{3,2},{5,4},{7,6},{9,8},{11,10},{13,12},{15,14},{17,16},{19,... | collective-permute-start | bytes 1544 | tf_op jit(solution)/shard_map/ppermute | solution.py:649
  42.0 2.2 %last.1 = (f32[512,128]{1,0:T(8,128)S(1)}, f32[520,128]{1,0:T(8,128)S(1)}) custom-call(f32[64,128]{1,0:T(8,128)S(1)} %get-tuple-element.65.loads, f32[8,128]{1,0:T(8,128)S(1)} %get-tuple-element.66.start_pot, f32[512,256]{1,0:T(8,128)S(1)} %get-tuple-element.67.put, f32[512,8192]{1,0:T(8,128)S(1)} %bitcast.5, s32[512,128]{1,0:T(8,128)S(1)} %get-tuple-element.48.coarse, ...), custom_call_target="tpu_custom_call" | custom-call | flops 4294967296 | bytes 16777216 | tf_op jit(solution)/shard_map/last/pallas_call | solution.py:576
  44.2 0.0 collective-permute-done.3
  44.3 13.5 %all_to_all.17 = f32[8,65,1,128]{3,2,1,0:T(1,128)S(1)} all-to-all(f32[8,65,1,128]{3,2,1,0:T(1,128)S(1)} %bitcast.7), channel_id=1, replica_groups=mesh['groups'=2,'lon'=8,'lat'=2] {'lon'}, dimensions={0} | all-to-all | bytes 532480 | tf_op jit(solution)/shard_map/all_to_all | solution.py:651
  57.7 1.2 %bands.1 = (f32[512,128]{1,0:T(8,128)}, f32[512,128]{1,0:T(8,128)}, f32[512,128]{1,0:T(8,128)}, f32[3,1,64,1024]{3,2,1,0:T(8,128)}) custom-call(f32[520,128]{1,0:T(8,128)S(1)} %bitcast.8, f32[512,128]{1,0:T(8,128)S(1)} %get-tuple-element.70.lam, f32[512,128]{1,0:T(8,128)S(1)} %get-tuple-element.71.adj_u, f32[512,128]{1,0:T(8,128)S(1)} %get-tuple-element.72.adj_v, ...), custom_call_target="tpu_custom_call" | custom-call | flops 4294967296 | bytes 16777216 | tf_op jit(solution)/shard_map/bands/pallas_call | solution.py:576
  (4 shorter events, 0.0 us)
Async XLA Ops:
  2.9 9.0 %collective-permute-start = (f32[24,128]{1,0:T(8,128)S(1)}, f32[24,128]{1,0:T(8,128)S(1)}, u32[]{:S(2)}, u32[]{:S(2)}) collective-permute-start(f32[24,128]{1,0:T(8,128)S(1)} %get-tuple-element.39.own_east), channel_id=1, source_target_pairs={{0,2},{2,4},{4,6},{6,8},{8,10},{10,12},{12,14},{14,0},{1,3},{3,5},... | collective-permute-start | bytes 36872 | tf_op jit(solution)/shard_map/ppermute | solution.py:605
  5.9 6.0 %collective-permute-start.1 = (f32[24,128]{1,0:T(8,128)S(1)}, f32[24,128]{1,0:T(8,128)S(1)}, u32[]{:S(2)}, u32[]{:S(2)}) collective-permute-start(f32[24,128]{1,0:T(8,128)S(1)} %get-tuple-element.40.own_west), channel_id=1, source_target_pairs={{2,0},{4,2},{6,4},{8,6},{10,8},{12,10},{14,12},{0,14},{3,1},{5,3},... | collective-permute-start | bytes 36872 | tf_op jit(solution)/shard_map/ppermute | solution.py:606
  9.0 2.8 %collective-permute-start.2 = (f32[8,128]{1,0:T(8,128)S(1)}, f32[8,128]{1,0:T(8,128)S(1)}, u32[]{:S(2)}, u32[]{:S(2)}) collective-permute-start(f32[8,128]{1,0:T(8,128)S(1)} %get-tuple-element.41.own_lat), channel_id=1, source_target_pairs={{0,1},{1,0},{2,3},{3,2},{4,5},{5,4},{6,7},{7,6},{8,9},{9,8},{10,11... | collective-permute-start | bytes 12296 | tf_op jit(solution)/shard_map/ppermute | solution.py:607
  9.0 15.0 %slice-start = ((s8[16777216]{0:T(1024)(128)(4,1)}), s8[4194304]{0:T(1024)(128)(4,1)S(1)}, s32[]{:S(2)}) async-start(s8[16777216]{0:T(1024)(128)(4,1)} %bitcast.4), calls=%async_computation.3 | async-start | bytes 8388608
  9.0 15.0 %slice-start.1 = ((s8[16777216]{0:T(1024)(128)(4,1)}), s8[4194304]{0:T(1024)(128)(4,1)S(1)}, s32[]{:S(2)}) async-start(s8[16777216]{0:T(1024)(128)(4,1)} %bitcast.4), calls=%async_computation.4 | async-start | bytes 8388608
  11.9 12.1 %slice-start.2 = ((s8[16777216]{0:T(1024)(128)(4,1)}), s8[4194304]{0:T(1024)(128)(4,1)S(1)}, s32[]{:S(2)}) async-start(s8[16777216]{0:T(1024)(128)(4,1)} %bitcast.4), calls=%async_computation.5 | async-start | bytes 8388608
  11.9 12.1 %slice-start.3 = ((s8[16777216]{0:T(1024)(128)(4,1)}), s8[4194304]{0:T(1024)(128)(4,1)S(1)}, s32[]{:S(2)}) async-start(s8[16777216]{0:T(1024)(128)(4,1)} %bitcast.4), calls=%async_computation.6 | async-start | bytes 8388608
  40.7 3.5 %collective-permute-start.3 = (f32[1,128]{1,0:T(1,128)S(1)}, f32[1,128]{1,0:T(1,128)S(1)}, u32[]{:S(2)}, u32[]{:S(2)}) collective-permute-start(f32[1,128]{1,0:T(1,128)S(1)} %get-tuple-element.69), channel_id=1, source_target_pairs={{1,0},{3,2},{5,4},{7,6},{9,8},{11,10},{13,12},{15,14},{17,16},{19,... | collective-permute-start | bytes 1544 | tf_op jit(solution)/shard_map/ppermute | solution.py:649

commit v5 on v4

--- a/solution.py
+++ b/solution.py
@@ -142,24 +142,9 @@
     )
 
 
-def green_product(green_ref, load_row, acc_ref, first=0, points=None):
-    total = green_ref.shape[1]
-    points = green_ref.shape[0] - first if points is None else points
-    tall = LANES
-
-    def step(index, carry):
-        start = pl.multiple_of(index * tall, tall)
-        acc = jnp.zeros((tall, LANES), f32)
-        for k in range(total // LANES):
-            acc = acc + green_ref[
-                pl.ds(first + start, tall), k * LANES : (k + 1) * LANES
-            ] * jnp.broadcast_to(load_row(k), (tall, LANES))
-        acc_ref[pl.ds(start, tall), :] = acc
-        return carry
-
-    lax.fori_loop(0, points // tall, step, 0)
+def sum_lanes(block):
     out = None
-    for piece in reversed(bf16_pieces(acc_ref[0:points, :], 3)):
+    for piece in reversed(bf16_pieces(block, 3)):
         part = lax.dot_general(
             jnp.ones((8, LANES), bf16), piece.astype(bf16), (((1,), (1,)), ((), ())),
             preferred_element_type=f32,
@@ -168,18 +153,55 @@
     return out
 
 
-def spread(potential, ids):
-    points = potential.shape[1]
+def green_rows(green_ref, start, load_row):
+    acc = jnp.zeros((LANES, LANES), f32)
+    for k in range(green_ref.shape[1] // LANES):
+        acc = acc + green_ref[
+            pl.ds(start, LANES), k * LANES : (k + 1) * LANES
+        ] * jnp.broadcast_to(load_row(k), (LANES, LANES))
+    return acc
+
+
+def look_up(table, ids):
     rows = ids.shape[0]
+    table = jnp.broadcast_to(table[None], (rows // 8, 8, LANES)).reshape(rows, LANES)
+    return jnp.take_along_axis(table, ids, axis=1, mode="promise_in_bounds")
+
+
+def spread(tables, ids):
     low = lax.bitwise_and(ids, LANES - 1)
     block = lax.shift_right_logical(ids, 7)
     out = None
-    for k in range(points // LANES):
-        table = potential[:, k * LANES : (k + 1) * LANES]
-        table = jnp.broadcast_to(table[None], (rows // 8, 8, LANES)).reshape(rows, LANES)
-        value = jnp.take_along_axis(table, low, axis=1, mode="promise_in_bounds")
+    for k, table in enumerate(tables):
+        value = look_up(table, low)
         out = value if out is None else jnp.where(block == k, value, out)
     return out
+
+
+def green_spread(green, coarse, load_row, acc, tables, pot, first):
+    points = green.shape[0]
+    rows = coarse.shape[0]
+
+    def settle(index):
+        table = sum_lanes(acc[...])
+        tables[index] = table
+        for start in range(0, rows, STEP_ROWS):
+            at = slice(start, start + STEP_ROWS)
+            ids = local_ids(coarse[at, :], points)
+            value = look_up(table, lax.bitwise_and(ids, LANES - 1))
+            pot[at, :] = jnp.where(lax.shift_right_logical(ids, 7) == index, value, pot[at, :])
+
+    def step(index, carry):
+        block = green_rows(green, index * LANES, load_row)
+        settle(index - 1)
+        acc[...] = block
+        return carry
+
+    if first == 0:
+        acc[...] = green_rows(green, 0, load_row)
+    for index in range(1, points // LANES):
+        step(index, 0)
+    settle(points // LANES - 1)
 
 
 def next_rows(ref, start, count):
@@ -368,7 +390,7 @@
 
 def second_kernel(
     first, green, coarse, ocean, held_in, gu, cu, gv, cv, left, right, faces, lat_lines,
-    payload, held, adj_u_out, adj_v_out, lam_sides, lam_edge, acc, lam, source,
+    payload, held, adj_u_out, adj_v_out, lam_sides, lam_edge, acc, tables, pot, lam, source,
     *, points, n_lon, n_lat,
 ):
     rows = coarse.shape[0]
@@ -376,8 +398,9 @@
     lat = lax.axis_index("lat")
     south_end = jnp.where(lat == 1, 1.0, 0.0)
     north_end = jnp.where(lat == 0, 1.0, 0.0)
-    potential = green_product(
-        green, lambda k: first[k // blocks, k % blocks : k % blocks + 1, :], acc
+    green_spread(
+        green, coarse, lambda k: first[k // blocks, k % blocks : k % blocks + 1, :],
+        acc, tables, pot, 0,
     )
     put = put_sides(faces[ADJ], [(slope_ratio, -slope_ratio)])
     adj_l = lat_lines[ADJ_L : ADJ_L + 1, :]
@@ -387,8 +410,7 @@
     lam[rows : rows + 8, :] = jnp.zeros((8, LANES), f32)
     for start in range(0, rows, STEP_ROWS):
         at = slice(start, start + STEP_ROWS)
-        pot = spread(potential, local_ids(coarse[at, :], points))
-        value = held_in[at, :] + put[at, :] - attract_coef * pot
+        value = held_in[at, :] + put[at, :] - attract_coef * pot[at, :]
         if start == 0:
             value = value + jnp.where(row == 0, south_end * slope_ratio * adj_l, 0.0)
         if start == rows - STEP_ROWS:
@@ -408,7 +430,8 @@
         held[at, :] = lam_c + src
     is_west = west_rows()
     sides = faces[MASK] * (
-        faces[BASE] - attract_coef * spread(potential, faces[OWN_ID].astype(i32))
+        faces[BASE]
+        - attract_coef * spread([tables[k] for k in range(blocks)], faces[OWN_ID].astype(i32))
     )
     lam_sides[...] = sides
     pull = faces[RATIO] * sides
@@ -458,7 +481,7 @@
 
 def edge_kernel(
     first, second, green, ocean, held, faces, lat_lines, lam_sides, lam_edge,
-    edge, loads, start_pot, put, north_line, acc, *, points, n_lon, n_lat,
+    edge, loads, acc, put, north_line, *, points, n_lon, n_lat,
 ):
     rows = held.shape[0]
     blocks = points // LANES
@@ -480,8 +503,8 @@
             loads[here * blocks : (here + 1) * blocks, :] = (
                 total * first[here, blocks : 2 * blocks, :]
             )
-    potential = green_product(green, lambda k: loads[k : k + 1, :], acc, 0, LANES)
-    start_pot[...] = potential
+    acc[...] = green_rows(green, 0, lambda k: loads[k : k + 1, :])
+    potential = sum_lanes(acc[...])
     west, east, other = neighbours(n_lon, n_lat)
 
     def shared(owner, count):
@@ -506,18 +529,16 @@
 
 
 def last_kernel(
-    loads, start_pot, put, green, coarse, ocean, held, lam_out, payload, acc, *, points, n_lon,
+    loads, start_acc, put, green, coarse, ocean, held, lam_out, payload, acc, tables, pot,
+    *, points, n_lon,
 ):
     rows = coarse.shape[0]
-    potential = start_pot[...]
-    if points > LANES:
-        rest = green_product(green, lambda k: loads[k : k + 1, :], acc, LANES, points - LANES)
-        potential = jnp.concatenate([potential, rest], 1)
+    acc[...] = start_acc[...]
+    green_spread(green, coarse, lambda k: loads[k : k + 1, :], acc, tables, pot, 1)
     for start in range(0, rows, STEP_ROWS):
         at = slice(start, start + STEP_ROWS)
-        pot = spread(potential, local_ids(coarse[at, :], points))
         lam_out[at, :] = ocean[at, :].astype(f32) * (
-            held[at, :] + put[at, :LANES] - attract_coef * pot
+            held[at, :] + put[at, :LANES] - attract_coef * pot[at, :]
         )
     span = rows // n_lon
     for target in range(n_lon):
@@ -619,14 +640,15 @@
     )
     first = lax.all_to_all(payload, ("lon", "lat"), 0, 0, tiled=True)
     deep = 4 * blocks + tall
+    green_scratch = [
+        pltpu.VMEM((LANES, LANES), f32),
+        pltpu.VMEM((blocks, 8, LANES), f32),
+        pltpu.VMEM(grid, f32),
+    ]
     payload, held, adj_u, adj_v, lam_sides, lam_edge = call(
         functools.partial(second_kernel, points=points, n_lon=n_lon, n_lat=n_lat),
         [(owners * deep, LANES), grid, grid, grid, (2 * tall, cols), (1, cols)],
-        [
-            pltpu.VMEM((points, LANES), f32),
-            pltpu.VMEM((rows + 8, cols), f32),
-            pltpu.VMEM(grid, f32),
-        ],
+        green_scratch + [pltpu.VMEM((rows + 8, cols), f32), pltpu.VMEM(grid, f32)],
         (first, green, coarse_of, ocean, held, gu, cu, gv, cv, left, right, faces, lat_lines),
         "second",
     )
@@ -634,17 +656,17 @@
         payload.reshape(owners, deep, 1, LANES), ("lon", "lat"), 0, 0, tiled=True
     ).reshape(payload.shape)
     span = rows // n_lon
-    edge, loads, start_pot, put, north_line = call(
+    edge, loads, start_acc, put, north_line = call(
         functools.partial(edge_kernel, points=points, n_lon=n_lon, n_lat=n_lat),
-        [(1, cols), (owners * blocks, LANES), (8, LANES), (rows, 2 * cols), (1, cols)],
-        [pltpu.VMEM((LANES, LANES), f32)],
+        [(1, cols), (owners * blocks, LANES), (LANES, LANES), (rows, 2 * cols), (1, cols)],
+        [],
         (first, second, green, ocean, held, faces, lat_lines, lam_sides, lam_edge), "edge",
     )
     lam, payload = call(
         functools.partial(last_kernel, points=points, n_lon=n_lon),
         [grid, (rows + n_lon, cols)],
-        [pltpu.VMEM((points, LANES), f32)],
-        (loads, start_pot, put, green, coarse_of, ocean, held), "last",
+        green_scratch,
+        (loads, start_acc, put, green, coarse_of, ocean, held), "last",
     )
     edge = lax.ppermute(edge, "lat", [(1, 0)])
     payload = lax.dynamic_update_slice(payload, edge, (rows + n_lon - 1, 0))

time: 59.2 us -> 58.2 us (0.983)
  Pallas kernels: 14.3 us -> 13.4 us
    pallas_call x7, Pallas kernels: 14.3 us -> 13.4 us  [call(): pl.pallas_call(kernel, out_shape=[jax.ShapeDtypeStruct(shape, kind) for s...]
  transfers between devices with their start and end apart: 4 -> 4, of which waited for: 0 -> 0; matrix products, arithmetic and copies ran while one was open for 0% -> 0% of each run, Pallas kernels for 9% -> 8%
where the time goes in v5:
time: 58.2 us; the launch traced here: 58 us
  blocking collectives  36.4 us (63%)
  Pallas kernels  13.4 us (23%)
  starting transfers between devices  7.42 us (13%)
  between operations  0.75 us (1%)
    all_to_all x1, blocking collectives, body(): lax.all_to_all(payload.reshape(n_lon, span + 1, 1, LANES), 'lon', 0, 0, t...  13.5 us
    pallas_call x7, Pallas kernels, call(): pl.pallas_call(kernel, out_shape=[jax.ShapeDtypeStruct(shape, kind) for s...  13.4 us
    all_to_all x1, blocking collectives, body(): first = lax.all_to_all(payload, ('lon', 'lat'), 0, 0, tiled=True)  11.8 us
    all_to_all x1, blocking collectives, body(): lax.all_to_all(payload.reshape(owners, deep, 1, LANES), ('lon', 'lat'), 0...  11.1 us
    ppermute x1, starting transfers between devices, body(): from_east = lax.ppermute(to_west, 'lon', backward)  3.1 us
    ppermute x1, starting transfers between devices, body(): from_west = lax.ppermute(to_east, 'lon', forward)  3.02 us
    ppermute x1, starting transfers between devices, body(): edge = lax.ppermute(edge, 'lat', [(1, 0)])  1.29 us
  transfers between devices with their start and end apart: 4, of which 0 were waited for; matrix products, arithmetic and copies ran while one was open for 0% of the time, Pallas kernels for 8%

profile of v5, /device:TPU:0, one launch (start us, length us, event | category | flops | bytes accessed | tf_op | source)
XLA Modules:
  0.0 58.0 jit_solution(237076891071723389)
XLA Ops:
  0.6 2.3 %pack.1 = (f32[24,128]{1,0:T(8,128)S(1)}, f32[24,128]{1,0:T(8,128)S(1)}, f32[8,128]{1,0:T(8,128)S(1)}, f32[512,128]{1,0:T(8,128)S(1)}, f32[512,128]{1,0:T(8,128)...) custom-call(f32[512,128]{1,0:T(8,128)} %refs_0_.1, ...), custom_call_target="tpu_custom_call" | custom-call | flops 4294967296 | bytes 16777216 | tf_op jit(solution)/shard_map/pack/pallas_call | solution.py:597
  2.9 3.0 %collective-permute-start = (f32[24,128]{1,0:T(8,128)S(1)}, f32[24,128]{1,0:T(8,128)S(1)}, u32[]{:S(2)}, u32[]{:S(2)}) collective-permute-start(f32[24,128]{1,0:T(8,128)S(1)} %get-tuple-element.39.own_east), channel_id=1, source_target_pairs={{0,2},{2,4},{4,6},{6,8},{8,10},{10,12},{12,14},{14,0},{1,3},{3,5},... | collective-permute-start | bytes 36872 | tf_op jit(solution)/shard_map/ppermute | solution.py:626
  5.9 3.1 %collective-permute-start.1 = (f32[24,128]{1,0:T(8,128)S(1)}, f32[24,128]{1,0:T(8,128)S(1)}, u32[]{:S(2)}, u32[]{:S(2)}) collective-permute-start(f32[24,128]{1,0:T(8,128)S(1)} %get-tuple-element.40.own_west), channel_id=1, source_target_pairs={{2,0},{4,2},{6,4},{8,6},{10,8},{12,10},{14,12},{0,14},{3,1},{5,3},... | collective-permute-start | bytes 36872 | tf_op jit(solution)/shard_map/ppermute | solution.py:627
  9.0 0.0 collective-permute-start.2
  9.0 2.8 %inner.1 = (f32[512,128]{1,0:T(8,128)S(1)}, f32[512,128]{1,0:T(8,128)S(1)}, f32[512,128]{1,0:T(8,128)S(1)}, f32[512,128]{1,0:T(8,128)S(1)}, f32[512,128]{1,0:T(8...) custom-call(f32[512,128]{1,0:T(8,128)S(1)} %get-tuple-element.42.lam, ...), custom_call_target="tpu_custom_call" | custom-call | flops 4294967296 | bytes 16777216 | tf_op jit(solution)/shard_map/inner/pallas_call | solution.py:597
  11.9 0.0 collective-permute-done.2.from_lat
  11.9 0.0 collective-permute-done.from_west
  11.9 0.0 collective-permute-done.1.from_east
  11.9 0.0 slice-start.2
  11.9 0.0 slice-start.3
  11.9 0.3 rim.1
  12.2 11.8 %all_to_all.15.first = f32[16,8,128]{2,1,0:T(8,128)S(1)} all-to-all(f32[16,8,128]{2,1,0:T(8,128)S(1)} %get-tuple-element.51), channel_id=1, replica_groups=mesh['groups'=2,'lon'=8,'lat'=2] {'lon','lat'}, dimensions={0} | all-to-all | bytes 131072 | tf_op jit(solution)/shard_map/all_to_all | solution.py:641
  24.0 0.0 slice-done
  24.0 0.0 slice-done.1
  24.0 0.0 slice-done.2
  24.0 0.0 slice-done.3
  24.0 4.4 %second.1 = (f32[320,128]{1,0:T(8,128)S(1)}, f32[512,128]{1,0:T(8,128)S(1)}, f32[512,128]{1,0:T(8,128)S(1)}, f32[512,128]{1,0:T(8,128)S(1)}, f32[8,128]{1,0:T(8,128)S(1)}, /*index=5*/f32[1,128]{1,0:T(1,128)S(1)}) custom-call(f32[16,8,128]{2,1,0:T(8,128)S(1)} %all_to_all.15.first, f32[512,8192]{1,0:T(8,128)S(1)} %bitcast.5, ...), custom_call_target="tpu_custom_call" | custom-call | flops 4294967296 | bytes 16777216 | tf_op jit(solution)/shard_map/second/pallas_call | solution.py:597
  28.5 11.1 %all_to_all.16 = f32[16,20,1,128]{3,2,1,0:T(1,128)S(1)} all-to-all(f32[16,20,1,128]{3,2,1,0:T(1,128)S(1)} %bitcast.9), channel_id=1, replica_groups=mesh['groups'=2,'lon'=8,'lat'=2] {'lon','lat'}, dimensions={0} | all-to-all | bytes 327680 | tf_op jit(solution)/shard_map/all_to_all | solution.py:655
  39.5 0.6 %edge.1 = (f32[1,128]{1,0:T(1,128)S(1)}, f32[64,128]{1,0:T(8,128)S(1)}, f32[128,128]{1,0:T(8,128)S(1)}, f32[512,256]{1,0:T(8,128)S(1)}, f32[1,128]{1,0:T(1,128)S(1)}) custom-call(f32[16,8,128]{2,1,0:T(8,128)S(1)} %all_to_all.15.first, f32[320,128]{1,0:T(8,128)S(1)} %bitcast.6, f32[512,8192]{1,0:T(8,128)S(1)} %bitcast.5, ...), custom_call_target="tpu_custom_call" | custom-call | flops 4294967296 | bytes 16777216 | tf_op jit(solution)/shard_map/edge/pallas_call | solution.py:597
  40.2 1.3 %collective-permute-start.3 = (f32[1,128]{1,0:T(1,128)S(1)}, f32[1,128]{1,0:T(1,128)S(1)}, u32[]{:S(2)}, u32[]{:S(2)}) collective-permute-start(f32[1,128]{1,0:T(1,128)S(1)} %get-tuple-element.69), channel_id=1, source_target_pairs={{1,0},{3,2},{5,4},{7,6},{9,8},{11,10},{13,12},{15,14},{17,16},{19,... | collective-permute-start | bytes 1544 | tf_op jit(solution)/shard_map/ppermute | solution.py:671
  41.5 1.8 %last.1 = (f32[512,128]{1,0:T(8,128)S(1)}, f32[520,128]{1,0:T(8,128)S(1)}) custom-call(f32[64,128]{1,0:T(8,128)S(1)} %get-tuple-element.65.loads, f32[128,128]{1,0:T(8,128)S(1)} %get-tuple-element.66.start_acc, f32[512,256]{1,0:T(8,128)S(1)} %get-tuple-element.67.put, f32[512,8192]{1,0:T(8,128)S(1)} %bitcast.5, s32[512,128]{1,0:T(8,128)S(1)} %get-tuple-element.48.coarse, ...), custom_call_target="tpu_custom_call" | custom-call | flops 4294967296 | bytes 16777216 | tf_op jit(solution)/shard_map/last/pallas_call | solution.py:597
  43.3 0.0 collective-permute-done.3
  43.3 13.5 %all_to_all.17 = f32[8,65,1,128]{3,2,1,0:T(1,128)S(1)} all-to-all(f32[8,65,1,128]{3,2,1,0:T(1,128)S(1)} %bitcast.7), channel_id=1, replica_groups=mesh['groups'=2,'lon'=8,'lat'=2] {'lon'}, dimensions={0} | all-to-all | bytes 532480 | tf_op jit(solution)/shard_map/all_to_all | solution.py:673
  56.8 1.2 %bands.1 = (f32[512,128]{1,0:T(8,128)}, f32[512,128]{1,0:T(8,128)}, f32[512,128]{1,0:T(8,128)}, f32[3,1,64,1024]{3,2,1,0:T(8,128)}) custom-call(f32[520,128]{1,0:T(8,128)S(1)} %bitcast.8, f32[512,128]{1,0:T(8,128)S(1)} %get-tuple-element.70.lam, f32[512,128]{1,0:T(8,128)S(1)} %get-tuple-element.71.adj_u, f32[512,128]{1,0:T(8,128)S(1)} %get-tuple-element.72.adj_v, ...), custom_call_target="tpu_custom_call" | custom-call | flops 4294967296 | bytes 16777216 | tf_op jit(solution)/shard_map/bands/pallas_call | solution.py:597
  (4 shorter events, 0.0 us)
Async XLA Ops:
  2.9 9.0 %collective-permute-start = (f32[24,128]{1,0:T(8,128)S(1)}, f32[24,128]{1,0:T(8,128)S(1)}, u32[]{:S(2)}, u32[]{:S(2)}) collective-permute-start(f32[24,128]{1,0:T(8,128)S(1)} %get-tuple-element.39.own_east), channel_id=1, source_target_pairs={{0,2},{2,4},{4,6},{6,8},{8,10},{10,12},{12,14},{14,0},{1,3},{3,5},... | collective-permute-start | bytes 36872 | tf_op jit(solution)/shard_map/ppermute | solution.py:626
  5.9 6.0 %collective-permute-start.1 = (f32[24,128]{1,0:T(8,128)S(1)}, f32[24,128]{1,0:T(8,128)S(1)}, u32[]{:S(2)}, u32[]{:S(2)}) collective-permute-start(f32[24,128]{1,0:T(8,128)S(1)} %get-tuple-element.40.own_west), channel_id=1, source_target_pairs={{2,0},{4,2},{6,4},{8,6},{10,8},{12,10},{14,12},{0,14},{3,1},{5,3},... | collective-permute-start | bytes 36872 | tf_op jit(solution)/shard_map/ppermute | solution.py:627
  9.0 2.8 %collective-permute-start.2 = (f32[8,128]{1,0:T(8,128)S(1)}, f32[8,128]{1,0:T(8,128)S(1)}, u32[]{:S(2)}, u32[]{:S(2)}) collective-permute-start(f32[8,128]{1,0:T(8,128)S(1)} %get-tuple-element.41.own_lat), channel_id=1, source_target_pairs={{0,1},{1,0},{2,3},{3,2},{4,5},{5,4},{6,7},{7,6},{8,9},{9,8},{10,11... | collective-permute-start | bytes 12296 | tf_op jit(solution)/shard_map/ppermute | solution.py:628
  9.0 15.0 %slice-start = ((s8[16777216]{0:T(1024)(128)(4,1)}), s8[4194304]{0:T(1024)(128)(4,1)S(1)}, s32[]{:S(2)}) async-start(s8[16777216]{0:T(1024)(128)(4,1)} %bitcast.4), calls=%async_computation.3 | async-start | bytes 8388608
  9.0 15.0 %slice-start.1 = ((s8[16777216]{0:T(1024)(128)(4,1)}), s8[4194304]{0:T(1024)(128)(4,1)S(1)}, s32[]{:S(2)}) async-start(s8[16777216]{0:T(1024)(128)(4,1)} %bitcast.4), calls=%async_computation.4 | async-start | bytes 8388608
  11.9 12.1 %slice-start.2 = ((s8[16777216]{0:T(1024)(128)(4,1)}), s8[4194304]{0:T(1024)(128)(4,1)S(1)}, s32[]{:S(2)}) async-start(s8[16777216]{0:T(1024)(128)(4,1)} %bitcast.4), calls=%async_computation.5 | async-start | bytes 8388608
  11.9 12.1 %slice-start.3 = ((s8[16777216]{0:T(1024)(128)(4,1)}), s8[4194304]{0:T(1024)(128)(4,1)S(1)}, s32[]{:S(2)}) async-start(s8[16777216]{0:T(1024)(128)(4,1)} %bitcast.4), calls=%async_computation.6 | async-start | bytes 8388608
  40.2 3.1 %collective-permute-start.3 = (f32[1,128]{1,0:T(1,128)S(1)}, f32[1,128]{1,0:T(1,128)S(1)}, u32[]{:S(2)}, u32[]{:S(2)}) collective-permute-start(f32[1,128]{1,0:T(1,128)S(1)} %get-tuple-element.69), channel_id=1, source_target_pairs={{1,0},{3,2},{5,4},{7,6},{9,8},{11,10},{13,12},{15,14},{17,16},{19,... | collective-permute-start | bytes 1544 | tf_op jit(solution)/shard_map/ppermute | solution.py:671

commit v6 on v5

--- a/solution.py
+++ b/solution.py
@@ -334,7 +334,7 @@
     low = [jnp.where(is_west, there, here) for here, there in zip(own, far)]
     high = [jnp.where(is_west, here, there) for here, there in zip(own, far)]
     adj, ratio, gain = face(low, high, low[FLUX])
-    mine, other = own_lat[...], from_lat[...]
+    mine, other = own_lat[...], from_lat[1 - lat]
     lower = jnp.where(lat == 0, mine, other)
     upper = jnp.where(lat == 0, other, mine)
     lower = [lower[k : k + 1] for k in range(6)]
@@ -566,6 +566,8 @@
     ]
     copies[0].start()
     lane = iota((span, LANES), 1)
+    top = (lax.axis_index("lat") == 1) & (lax.axis_index("lon") == count - 1)
+    last = (iota((span, LANES), 0) == span - 1) & top
     for k in range(count):
         start = k * (span + 1)
         planes[0, :, k * LANES : (k + 1) * LANES] = parts[start : start + span, :]
@@ -573,7 +575,8 @@
     for k in range(count):
         start = k * (span + 1)
         here = parts[start : start + span, :]
-        planes[2, :, k * LANES : (k + 1) * LANES] = parts[start + 1 : start + 1 + span, :] - here
+        north_of = jnp.where(last, 0.0, parts[start + 1 : start + 1 + span, :])
+        planes[2, :, k * LANES : (k + 1) * LANES] = north_of - here
     copies[5].start()
     for k in range(count):
         at = slice(k * LANES, (k + 1) * LANES)
@@ -625,7 +628,7 @@
     backward = [(target, source) for source, target in forward]
     from_west = lax.ppermute(to_east, "lon", forward)
     from_east = lax.ppermute(to_west, "lon", backward)
-    from_lat = lax.ppermute(to_lat, "lat", [(0, 1), (1, 0)])
+    from_lat = lax.all_gather(to_lat, "lat", axis=0)
     held, gu, cu, gv, cv, sums, left, right, held_sides = call(
         functools.partial(inner_kernel, points=points),
         [grid] * 5
@@ -668,7 +671,7 @@
         green_scratch,
         (loads, start_acc, put, green, coarse_of, ocean, held), "last",
     )
-    edge = lax.ppermute(edge, "lat", [(1, 0)])
+    edge = lax.all_gather(edge, "lat", axis=0)[1]
     payload = lax.dynamic_update_slice(payload, edge, (rows + n_lon - 1, 0))
     parts = lax.all_to_all(
         payload.reshape(n_lon, span + 1, 1, LANES), "lon", 0, 0, tiled=True

time: 58.2 us -> 58.3 us (level)
  blocking collectives: 36.4 us -> 37.8 us
  starting transfers between devices: 7.42 us -> 6.12 us
    all_gather x0 -> x2, blocking collectives: none -> 3.56 us  [the longest x1 1.8 us: body(): from_lat = lax.all_gather(to_lat, 'lat', axis=0)]
    all_to_all x1, blocking collectives: 11.8 us -> 10.3 us  [body(): first = lax.all_to_all(payload, ('lon', 'lat'), 0, 0, tiled=True)]
    ppermute x2 -> x0, starting transfers between devices: 1.29 us -> none  [the longest x1 1.29 us: body(): edge = lax.ppermute(edge, 'lat', [(1, 0)])]
    all_to_all x1, blocking collectives: 13.5 us -> 12.9 us  [body(): lax.all_to_all(payload.reshape(n_lon, span + 1, 1, LANES), 'lon', 0, 0, t...]
  transfers between devices with their start and end apart: 4 -> 2, of which waited for: 0 -> 0; matrix products, arithmetic and copies ran while one was open for 0% -> 0% of each run, Pallas kernels for 8% -> 5%
where the time goes in v6:
time: 58.3 us; the launch traced here: 58.1 us
  blocking collectives  37.8 us (65%)
  Pallas kernels  13.4 us (23%)
  starting transfers between devices  6.12 us (10%)
  between operations  0.71 us (1%)
    pallas_call x7, Pallas kernels, call(): pl.pallas_call(kernel, out_shape=[jax.ShapeDtypeStruct(shape, kind) for s...  13.4 us
    all_to_all x1, blocking collectives, body(): lax.all_to_all(payload.reshape(n_lon, span + 1, 1, LANES), 'lon', 0, 0, t...  12.9 us
    all_to_all x1, blocking collectives, body(): lax.all_to_all(payload.reshape(owners, deep, 1, LANES), ('lon', 'lat'), 0...  11.1 us
    all_to_all x1, blocking collectives, body(): first = lax.all_to_all(payload, ('lon', 'lat'), 0, 0, tiled=True)  10.3 us
    ppermute x1, starting transfers between devices, body(): from_east = lax.ppermute(to_west, 'lon', backward)  3.1 us
    ppermute x1, starting transfers between devices, body(): from_west = lax.ppermute(to_east, 'lon', forward)  3.02 us
    all_gather x1, blocking collectives, body(): from_lat = lax.all_gather(to_lat, 'lat', axis=0)  1.8 us
    all_gather x1, blocking collectives, body(): edge = lax.all_gather(edge, 'lat', axis=0)[1]  1.77 us
  transfers between devices with their start and end apart: 2, of which 0 were waited for; matrix products, arithmetic and copies ran while one was open for 0% of the time, Pallas kernels for 5%

profile of v6, /device:TPU:0, one launch (start us, length us, event | category | flops | bytes accessed | tf_op | source)
XLA Modules:
  0.0 58.1 jit_solution(2324056511748103704)
XLA Ops:
  0.6 2.3 %pack.1 = (f32[24,128]{1,0:T(8,128)S(1)}, f32[24,128]{1,0:T(8,128)S(1)}, f32[8,128]{1,0:T(8,128)S(1)}, f32[512,128]{1,0:T(8,128)S(1)}, f32[512,128]{1,0:T(8,128)...) custom-call(f32[512,128]{1,0:T(8,128)} %refs_0_.1, ...), custom_call_target="tpu_custom_call" | custom-call | flops 4294967296 | bytes 16777216 | tf_op jit(solution)/shard_map/pack/pallas_call | solution.py:600
  2.9 3.0 %collective-permute-start = (f32[24,128]{1,0:T(8,128)S(1)}, f32[24,128]{1,0:T(8,128)S(1)}, u32[]{:S(2)}, u32[]{:S(2)}) collective-permute-start(f32[24,128]{1,0:T(8,128)S(1)} %get-tuple-element.39.own_east), channel_id=1, source_target_pairs={{0,2},{2,4},{4,6},{6,8},{8,10},{10,12},{12,14},{14,0},{1,3},{3,5},... | collective-permute-start | bytes 36872 | tf_op jit(solution)/shard_map/ppermute | solution.py:629
  5.9 3.1 %collective-permute-start.1 = (f32[24,128]{1,0:T(8,128)S(1)}, f32[24,128]{1,0:T(8,128)S(1)}, u32[]{:S(2)}, u32[]{:S(2)}) collective-permute-start(f32[24,128]{1,0:T(8,128)S(1)} %get-tuple-element.40.own_west), channel_id=1, source_target_pairs={{2,0},{4,2},{6,4},{8,6},{10,8},{12,10},{14,12},{0,14},{3,1},{5,3},... | collective-permute-start | bytes 36872 | tf_op jit(solution)/shard_map/ppermute | solution.py:630
  9.0 0.0 slice-start
  9.0 0.0 slice-start.1
  9.0 2.8 %inner.1 = (f32[512,128]{1,0:T(8,128)S(1)}, f32[512,128]{1,0:T(8,128)S(1)}, f32[512,128]{1,0:T(8,128)S(1)}, f32[512,128]{1,0:T(8,128)S(1)}, f32[512,128]{1,0:T(8...) custom-call(f32[512,128]{1,0:T(8,128)S(1)} %get-tuple-element.42.lam, ...), custom_call_target="tpu_custom_call" | custom-call | flops 4294967296 | bytes 16777216 | tf_op jit(solution)/shard_map/inner/pallas_call | solution.py:600
  11.9 1.8 %all-gather = f32[16,128]{1,0:T(8,128)S(1)} all-gather(f32[8,128]{1,0:T(8,128)S(1)} %get-tuple-element.41.own_lat), channel_id=2, replica_groups=mesh['groups'=2,'lon'=8,'lat'=2] {'lat'}, dimensions={0}, use_global_device_ids=true | all-gather | bytes 12288 | tf_op jit(solution)/shard_map/all_gather | solution.py:631
  13.7 0.0 collective-permute-done.from_west
  13.7 0.0 collective-permute-done.1.from_east
  13.7 0.0 slice-start.2
  13.7 0.0 slice-start.3
  13.7 0.3 rim.1
  13.9 10.3 %all_to_all.15.first = f32[16,8,128]{2,1,0:T(8,128)S(1)} all-to-all(f32[16,8,128]{2,1,0:T(8,128)S(1)} %get-tuple-element.51), channel_id=1, replica_groups=mesh['groups'=2,'lon'=8,'lat'=2] {'lon','lat'}, dimensions={0} | all-to-all | bytes 131072 | tf_op jit(solution)/shard_map/all_to_all | solution.py:644
  24.2 0.0 slice-done
  24.2 0.0 slice-done.1
  24.2 0.0 slice-done.2
  24.2 0.0 slice-done.3
  24.3 4.4 %second.1 = (f32[320,128]{1,0:T(8,128)S(1)}, f32[512,128]{1,0:T(8,128)S(1)}, f32[512,128]{1,0:T(8,128)S(1)}, f32[512,128]{1,0:T(8,128)S(1)}, f32[8,128]{1,0:T(8,128)S(1)}, /*index=5*/f32[1,128]{1,0:T(1,128)S(1)}) custom-call(f32[16,8,128]{2,1,0:T(8,128)S(1)} %all_to_all.15.first, f32[512,8192]{1,0:T(8,128)S(1)} %bitcast.9, ...), custom_call_target="tpu_custom_call" | custom-call | flops 4294967296 | bytes 16777216 | tf_op jit(solution)/shard_map/second/pallas_call | solution.py:600
  28.7 11.1 %all_to_all.16 = f32[16,20,1,128]{3,2,1,0:T(1,128)S(1)} all-to-all(f32[16,20,1,128]{3,2,1,0:T(1,128)S(1)} %bitcast.13), channel_id=1, replica_groups=mesh['groups'=2,'lon'=8,'lat'=2] {'lon','lat'}, dimensions={0} | all-to-all | bytes 327680 | tf_op jit(solution)/shard_map/all_to_all | solution.py:658
  39.7 0.6 %edge.1 = (f32[1,128]{1,0:T(1,128)S(1)}, f32[64,128]{1,0:T(8,128)S(1)}, f32[128,128]{1,0:T(8,128)S(1)}, f32[512,256]{1,0:T(8,128)S(1)}, f32[1,128]{1,0:T(1,128)S(1)}) custom-call(f32[16,8,128]{2,1,0:T(8,128)S(1)} %all_to_all.15.first, f32[320,128]{1,0:T(8,128)S(1)} %bitcast.10, f32[512,8192]{1,0:T(8,128)S(1)} %bitcast.9, ...), custom_call_target="tpu_custom_call" | custom-call | flops 4294967296 | bytes 16777216 | tf_op jit(solution)/shard_map/edge/pallas_call | solution.py:600
  40.4 1.8 %all-gather.2 = f32[2,1,128]{2,1,0:T(1,128)S(1)} all-gather(f32[1,1,128]{2,1,0:T(1,128)S(1)} %bitcast.15), channel_id=3, replica_groups=mesh['groups'=2,'lon'=8,'lat'=2] {'lat'}, dimensions={0}, use_global_device_ids=true | all-gather | bytes 1536 | tf_op jit(solution)/shard_map/all_gather | solution.py:674
  42.1 1.8 %last.1 = (f32[512,128]{1,0:T(8,128)S(1)}, f32[520,128]{1,0:T(8,128)S(1)}) custom-call(f32[64,128]{1,0:T(8,128)S(1)} %get-tuple-element.65.loads, f32[128,128]{1,0:T(8,128)S(1)} %get-tuple-element.66.start_acc, f32[512,256]{1,0:T(8,128)S(1)} %get-tuple-element.67.put, f32[512,8192]{1,0:T(8,128)S(1)} %bitcast.9, s32[512,128]{1,0:T(8,128)S(1)} %get-tuple-element.48.coarse, ...), custom_call_target="tpu_custom_call" | custom-call | flops 4294967296 | bytes 16777216 | tf_op jit(solution)/shard_map/last/pallas_call | solution.py:600
  44.0 12.9 %all_to_all.17 = f32[8,65,1,128]{3,2,1,0:T(1,128)S(1)} all-to-all(f32[8,65,1,128]{3,2,1,0:T(1,128)S(1)} %bitcast.12), channel_id=1, replica_groups=mesh['groups'=2,'lon'=8,'lat'=2] {'lon'}, dimensions={0} | all-to-all | bytes 532480 | tf_op jit(solution)/shard_map/all_to_all | solution.py:676
  56.9 1.2 %bands.1 = (f32[512,128]{1,0:T(8,128)}, f32[512,128]{1,0:T(8,128)}, f32[512,128]{1,0:T(8,128)}, f32[3,1,64,1024]{3,2,1,0:T(8,128)}) custom-call(f32[520,128]{1,0:T(8,128)S(1)} %bitcast.11, f32[512,128]{1,0:T(8,128)S(1)} %get-tuple-element.70.lam, f32[512,128]{1,0:T(8,128)S(1)} %get-tuple-element.71.adj_u, f32[512,128]{1,0:T(8,128)S(1)} %get-tuple-element.72.adj_v, ...), custom_call_target="tpu_custom_call" | custom-call | flops 4294967296 | bytes 16777216 | tf_op jit(solution)/shard_map/bands/pallas_call | solution.py:600
  (3 shorter events, 0.0 us)
Async XLA Ops:
  2.9 10.8 %collective-permute-start = (f32[24,128]{1,0:T(8,128)S(1)}, f32[24,128]{1,0:T(8,128)S(1)}, u32[]{:S(2)}, u32[]{:S(2)}) collective-permute-start(f32[24,128]{1,0:T(8,128)S(1)} %get-tuple-element.39.own_east), channel_id=1, source_target_pairs={{0,2},{2,4},{4,6},{6,8},{8,10},{10,12},{12,14},{14,0},{1,3},{3,5},... | collective-permute-start | bytes 36872 | tf_op jit(solution)/shard_map/ppermute | solution.py:629
  5.9 7.7 %collective-permute-start.1 = (f32[24,128]{1,0:T(8,128)S(1)}, f32[24,128]{1,0:T(8,128)S(1)}, u32[]{:S(2)}, u32[]{:S(2)}) collective-permute-start(f32[24,128]{1,0:T(8,128)S(1)} %get-tuple-element.40.own_west), channel_id=1, source_target_pairs={{2,0},{4,2},{6,4},{8,6},{10,8},{12,10},{14,12},{0,14},{3,1},{5,3},... | collective-permute-start | bytes 36872 | tf_op jit(solution)/shard_map/ppermute | solution.py:630
  9.0 15.2 %slice-start = ((s8[16777216]{0:T(1024)(128)(4,1)}), s8[4194304]{0:T(1024)(128)(4,1)S(1)}, s32[]{:S(2)}) async-start(s8[16777216]{0:T(1024)(128)(4,1)} %bitcast.8), calls=%async_computation.3 | async-start | bytes 8388608
  9.0 15.2 %slice-start.1 = ((s8[16777216]{0:T(1024)(128)(4,1)}), s8[4194304]{0:T(1024)(128)(4,1)S(1)}, s32[]{:S(2)}) async-start(s8[16777216]{0:T(1024)(128)(4,1)} %bitcast.8), calls=%async_computation.4 | async-start | bytes 8388608
  13.7 10.6 %slice-start.2 = ((s8[16777216]{0:T(1024)(128)(4,1)}), s8[4194304]{0:T(1024)(128)(4,1)S(1)}, s32[]{:S(2)}) async-start(s8[16777216]{0:T(1024)(128)(4,1)} %bitcast.8), calls=%async_computation.5 | async-start | bytes 8388608
  13.7 10.6 %slice-start.3 = ((s8[16777216]{0:T(1024)(128)(4,1)}), s8[4194304]{0:T(1024)(128)(4,1)S(1)}, s32[]{:S(2)}) async-start(s8[16777216]{0:T(1024)(128)(4,1)} %bitcast.8), calls=%async_computation.6 | async-start | bytes 8388608

commit v7 on v6

--- a/solution.py
+++ b/solution.py
@@ -334,7 +334,7 @@
     low = [jnp.where(is_west, there, here) for here, there in zip(own, far)]
     high = [jnp.where(is_west, here, there) for here, there in zip(own, far)]
     adj, ratio, gain = face(low, high, low[FLUX])
-    mine, other = own_lat[...], from_lat[1 - lat]
+    mine, other = own_lat[...], from_lat[...]
     lower = jnp.where(lat == 0, mine, other)
     upper = jnp.where(lat == 0, other, mine)
     lower = [lower[k : k + 1] for k in range(6)]
@@ -628,7 +628,7 @@
     backward = [(target, source) for source, target in forward]
     from_west = lax.ppermute(to_east, "lon", forward)
     from_east = lax.ppermute(to_west, "lon", backward)
-    from_lat = lax.all_gather(to_lat, "lat", axis=0)
+    from_lat = lax.ppermute(to_lat, "lat", [(0, 1), (1, 0)])
     held, gu, cu, gv, cv, sums, left, right, held_sides = call(
         functools.partial(inner_kernel, points=points),
         [grid] * 5

time: 58.3 us -> 58.1 us (level)
    all_gather x1 -> x0, blocking collectives: 1.8 us -> none  [body(): from_lat = lax.all_gather(to_lat, 'lat', axis=0)]
    all_to_all x1, blocking collectives: 10.3 us -> 11.8 us  [body(): first = lax.all_to_all(payload, ('lon', 'lat'), 0, 0, tiled=True)]
  transfers between devices with their start and end apart: 2 -> 3, of which waited for: 0 -> 0; matrix products, arithmetic and copies ran while one was open for 0% -> 0% of each run, Pallas kernels for 5% -> 5%
where the time goes in v7:
time: 58.1 us; the launch traced here: 57.9 us
  blocking collectives  37.5 us (65%)
  Pallas kernels  13.4 us (23%)
  starting transfers between devices  6.13 us (11%)
  between operations  0.73 us (1%)
    pallas_call x7, Pallas kernels, call(): pl.pallas_call(kernel, out_shape=[jax.ShapeDtypeStruct(shape, kind) for s...  13.4 us
    all_to_all x1, blocking collectives, body(): lax.all_to_all(payload.reshape(n_lon, span + 1, 1, LANES), 'lon', 0, 0, t...  12.9 us
    all_to_all x1, blocking collectives, body(): first = lax.all_to_all(payload, ('lon', 'lat'), 0, 0, tiled=True)  11.8 us
    all_to_all x1, blocking collectives, body(): lax.all_to_all(payload.reshape(owners, deep, 1, LANES), ('lon', 'lat'), 0...  11.1 us
    ppermute x1, starting transfers between devices, body(): from_east = lax.ppermute(to_west, 'lon', backward)  3.1 us
    ppermute x1, starting transfers between devices, body(): from_west = lax.ppermute(to_east, 'lon', forward)  3.02 us
    all_gather x1, blocking collectives, body(): edge = lax.all_gather(edge, 'lat', axis=0)[1]  1.77 us
  transfers between devices with their start and end apart: 3, of which 0 were waited for; matrix products, arithmetic and copies ran while one was open for 0% of the time, Pallas kernels for 5%

profile of v7, /device:TPU:0, one launch (start us, length us, event | category | flops | bytes accessed | tf_op | source)
XLA Modules:
  0.0 57.9 jit_solution(11092801190689807229)
XLA Ops:
  0.6 2.3 %pack.1 = (f32[24,128]{1,0:T(8,128)S(1)}, f32[24,128]{1,0:T(8,128)S(1)}, f32[8,128]{1,0:T(8,128)S(1)}, f32[512,128]{1,0:T(8,128)S(1)}, f32[512,128]{1,0:T(8,128)...) custom-call(f32[512,128]{1,0:T(8,128)} %refs_0_.1, ...), custom_call_target="tpu_custom_call" | custom-call | flops 4294967296 | bytes 16777216 | tf_op jit(solution)/shard_map/pack/pallas_call | solution.py:600
  2.9 3.0 %collective-permute-start = (f32[24,128]{1,0:T(8,128)S(1)}, f32[24,128]{1,0:T(8,128)S(1)}, u32[]{:S(2)}, u32[]{:S(2)}) collective-permute-start(f32[24,128]{1,0:T(8,128)S(1)} %get-tuple-element.39.own_east), channel_id=1, source_target_pairs={{0,2},{2,4},{4,6},{6,8},{8,10},{10,12},{12,14},{14,0},{1,3},{3,5},... | collective-permute-start | bytes 36872 | tf_op jit(solution)/shard_map/ppermute | solution.py:629
  5.9 3.1 %collective-permute-start.1 = (f32[24,128]{1,0:T(8,128)S(1)}, f32[24,128]{1,0:T(8,128)S(1)}, u32[]{:S(2)}, u32[]{:S(2)}) collective-permute-start(f32[24,128]{1,0:T(8,128)S(1)} %get-tuple-element.40.own_west), channel_id=1, source_target_pairs={{2,0},{4,2},{6,4},{8,6},{10,8},{12,10},{14,12},{0,14},{3,1},{5,3},... | collective-permute-start | bytes 36872 | tf_op jit(solution)/shard_map/ppermute | solution.py:630
  9.0 0.0 collective-permute-start.2
  9.0 0.0 slice-start
  9.0 2.8 %inner.1 = (f32[512,128]{1,0:T(8,128)S(1)}, f32[512,128]{1,0:T(8,128)S(1)}, f32[512,128]{1,0:T(8,128)S(1)}, f32[512,128]{1,0:T(8,128)S(1)}, f32[512,128]{1,0:T(8...) custom-call(f32[512,128]{1,0:T(8,128)S(1)} %get-tuple-element.42.lam, ...), custom_call_target="tpu_custom_call" | custom-call | flops 4294967296 | bytes 16777216 | tf_op jit(solution)/shard_map/inner/pallas_call | solution.py:600
  11.9 0.0 collective-permute-done.2.from_lat
  11.9 0.0 collective-permute-done.from_west
  11.9 0.0 collective-permute-done.1.from_east
  11.9 0.0 slice-start.2
  11.9 0.0 slice-start.3
  11.9 0.3 rim.1
  12.2 11.8 %all_to_all.15.first = f32[16,8,128]{2,1,0:T(8,128)S(1)} all-to-all(f32[16,8,128]{2,1,0:T(8,128)S(1)} %get-tuple-element.51), channel_id=1, replica_groups=mesh['groups'=2,'lon'=8,'lat'=2] {'lon','lat'}, dimensions={0} | all-to-all | bytes 131072 | tf_op jit(solution)/shard_map/all_to_all | solution.py:644
  24.0 0.0 slice-done
  24.0 0.0 slice-done.1
  24.0 0.0 slice-done.2
  24.0 0.0 slice-done.3
  24.0 4.4 %second.1 = (f32[320,128]{1,0:T(8,128)S(1)}, f32[512,128]{1,0:T(8,128)S(1)}, f32[512,128]{1,0:T(8,128)S(1)}, f32[512,128]{1,0:T(8,128)S(1)}, f32[8,128]{1,0:T(8,128)S(1)}, /*index=5*/f32[1,128]{1,0:T(1,128)S(1)}) custom-call(f32[16,8,128]{2,1,0:T(8,128)S(1)} %all_to_all.15.first, f32[512,8192]{1,0:T(8,128)S(1)} %bitcast.8, ...), custom_call_target="tpu_custom_call" | custom-call | flops 4294967296 | bytes 16777216 | tf_op jit(solution)/shard_map/second/pallas_call | solution.py:600
  28.5 11.1 %all_to_all.16 = f32[16,20,1,128]{3,2,1,0:T(1,128)S(1)} all-to-all(f32[16,20,1,128]{3,2,1,0:T(1,128)S(1)} %bitcast.12), channel_id=1, replica_groups=mesh['groups'=2,'lon'=8,'lat'=2] {'lon','lat'}, dimensions={0} | all-to-all | bytes 327680 | tf_op jit(solution)/shard_map/all_to_all | solution.py:658
  39.5 0.6 %edge.1 = (f32[1,128]{1,0:T(1,128)S(1)}, f32[64,128]{1,0:T(8,128)S(1)}, f32[128,128]{1,0:T(8,128)S(1)}, f32[512,256]{1,0:T(8,128)S(1)}, f32[1,128]{1,0:T(1,128)S(1)}) custom-call(f32[16,8,128]{2,1,0:T(8,128)S(1)} %all_to_all.15.first, f32[320,128]{1,0:T(8,128)S(1)} %bitcast.9, f32[512,8192]{1,0:T(8,128)S(1)} %bitcast.8, ...), custom_call_target="tpu_custom_call" | custom-call | flops 4294967296 | bytes 16777216 | tf_op jit(solution)/shard_map/edge/pallas_call | solution.py:600
  40.2 1.8 %all-gather.1 = f32[2,1,128]{2,1,0:T(1,128)S(1)} all-gather(f32[1,1,128]{2,1,0:T(1,128)S(1)} %bitcast.13), channel_id=2, replica_groups=mesh['groups'=2,'lon'=8,'lat'=2] {'lat'}, dimensions={0}, use_global_device_ids=true | all-gather | bytes 1536 | tf_op jit(solution)/shard_map/all_gather | solution.py:674
  41.9 1.8 %last.1 = (f32[512,128]{1,0:T(8,128)S(1)}, f32[520,128]{1,0:T(8,128)S(1)}) custom-call(f32[64,128]{1,0:T(8,128)S(1)} %get-tuple-element.65.loads, f32[128,128]{1,0:T(8,128)S(1)} %get-tuple-element.66.start_acc, f32[512,256]{1,0:T(8,128)S(1)} %get-tuple-element.67.put, f32[512,8192]{1,0:T(8,128)S(1)} %bitcast.8, s32[512,128]{1,0:T(8,128)S(1)} %get-tuple-element.48.coarse, ...), custom_call_target="tpu_custom_call" | custom-call | flops 4294967296 | bytes 16777216 | tf_op jit(solution)/shard_map/last/pallas_call | solution.py:600
  43.8 12.9 %all_to_all.17 = f32[8,65,1,128]{3,2,1,0:T(1,128)S(1)} all-to-all(f32[8,65,1,128]{3,2,1,0:T(1,128)S(1)} %bitcast.11), channel_id=1, replica_groups=mesh['groups'=2,'lon'=8,'lat'=2] {'lon'}, dimensions={0} | all-to-all | bytes 532480 | tf_op jit(solution)/shard_map/all_to_all | solution.py:676
  56.7 1.2 %bands.1 = (f32[512,128]{1,0:T(8,128)}, f32[512,128]{1,0:T(8,128)}, f32[512,128]{1,0:T(8,128)}, f32[3,1,64,1024]{3,2,1,0:T(8,128)}) custom-call(f32[520,128]{1,0:T(8,128)S(1)} %bitcast.10, f32[512,128]{1,0:T(8,128)S(1)} %get-tuple-element.70.lam, f32[512,128]{1,0:T(8,128)S(1)} %get-tuple-element.71.adj_u, f32[512,128]{1,0:T(8,128)S(1)} %get-tuple-element.72.adj_v, ...), custom_call_target="tpu_custom_call" | custom-call | flops 4294967296 | bytes 16777216 | tf_op jit(solution)/shard_map/bands/pallas_call | solution.py:600
  (4 shorter events, 0.0 us)
Async XLA Ops:
  2.9 9.0 %collective-permute-start = (f32[24,128]{1,0:T(8,128)S(1)}, f32[24,128]{1,0:T(8,128)S(1)}, u32[]{:S(2)}, u32[]{:S(2)}) collective-permute-start(f32[24,128]{1,0:T(8,128)S(1)} %get-tuple-element.39.own_east), channel_id=1, source_target_pairs={{0,2},{2,4},{4,6},{6,8},{8,10},{10,12},{12,14},{14,0},{1,3},{3,5},... | collective-permute-start | bytes 36872 | tf_op jit(solution)/shard_map/ppermute | solution.py:629
  5.9 6.0 %collective-permute-start.1 = (f32[24,128]{1,0:T(8,128)S(1)}, f32[24,128]{1,0:T(8,128)S(1)}, u32[]{:S(2)}, u32[]{:S(2)}) collective-permute-start(f32[24,128]{1,0:T(8,128)S(1)} %get-tuple-element.40.own_west), channel_id=1, source_target_pairs={{2,0},{4,2},{6,4},{8,6},{10,8},{12,10},{14,12},{0,14},{3,1},{5,3},... | collective-permute-start | bytes 36872 | tf_op jit(solution)/shard_map/ppermute | solution.py:630
  9.0 2.8 %collective-permute-start.2 = (f32[8,128]{1,0:T(8,128)S(1)}, f32[8,128]{1,0:T(8,128)S(1)}, u32[]{:S(2)}, u32[]{:S(2)}) collective-permute-start(f32[8,128]{1,0:T(8,128)S(1)} %get-tuple-element.41.own_lat), channel_id=1, source_target_pairs={{0,1},{1,0},{2,3},{3,2},{4,5},{5,4},{6,7},{7,6},{8,9},{9,8},{10,11... | collective-permute-start | bytes 12296 | tf_op jit(solution)/shard_map/ppermute | solution.py:631
  9.0 15.0 %slice-start = ((s8[16777216]{0:T(1024)(128)(4,1)}), s8[4194304]{0:T(1024)(128)(4,1)S(1)}, s32[]{:S(2)}) async-start(s8[16777216]{0:T(1024)(128)(4,1)} %bitcast.7), calls=%async_computation.3 | async-start | bytes 8388608
  9.0 15.0 %slice-start.1 = ((s8[16777216]{0:T(1024)(128)(4,1)}), s8[4194304]{0:T(1024)(128)(4,1)S(1)}, s32[]{:S(2)}) async-start(s8[16777216]{0:T(1024)(128)(4,1)} %bitcast.7), calls=%async_computation.4 | async-start | bytes 8388608
  11.9 12.1 %slice-start.2 = ((s8[16777216]{0:T(1024)(128)(4,1)}), s8[4194304]{0:T(1024)(128)(4,1)S(1)}, s32[]{:S(2)}) async-start(s8[16777216]{0:T(1024)(128)(4,1)} %bitcast.7), calls=%async_computation.5 | async-start | bytes 8388608
  11.9 12.1 %slice-start.3 = ((s8[16777216]{0:T(1024)(128)(4,1)}), s8[4194304]{0:T(1024)(128)(4,1)S(1)}, s32[]{:S(2)}) async-start(s8[16777216]{0:T(1024)(128)(4,1)} %bitcast.7), calls=%async_computation.6 | async-start | bytes 8388608

commit v8 on v7

--- a/solution.py
+++ b/solution.py
@@ -15,6 +15,7 @@
 LOW = 32
 HIGH = 16
 PIECES = 2
+INNER_LIMIT = 36
 SEG_ROWS = 256
 STEP_ROWS = 128
 
@@ -25,7 +26,7 @@
 
 LAM, DEPTH, DRAG, OCEAN, POINT, FLUX = range(6)
 ADJ, RATIO, GAIN, BASE, MASK, OWN_ID, FAR_ID = range(7)
-ADJ_L, C_L, G_L, ID_L, OWN_L = range(5)
+ADJ_L, C_L, G_L, ID_L, OWN_L, MASK_L = range(6)
 
 
 def iota(shape, dim):
@@ -178,7 +179,7 @@
     return out
 
 
-def green_spread(green, coarse, load_row, acc, tables, pot, first):
+def green_spread(green, coarse, load_row, acc, tables, pot):
     points = green.shape[0]
     rows = coarse.shape[0]
 
@@ -197,8 +198,7 @@
         acc[...] = block
         return carry
 
-    if first == 0:
-        acc[...] = green_rows(green, 0, load_row)
+    acc[...] = green_rows(green, 0, load_row)
     for index in range(1, points // LANES):
         step(index, 0)
     settle(points // LANES - 1)
@@ -257,9 +257,11 @@
 
 
 def inner_kernel(
-    lam, east, north, depth, drag, ocean, coarse,
-    held, gu, cu, gv, cv, sums, left, right, held_sides, source, *, points,
+    lam, east, north, depth, drag, ocean, coarse, green,
+    held, gu, cu, gv, cv, sums, left, right, held_sides, green_top, source, done, *, points,
 ):
+    copy = pltpu.make_async_copy(green.at[pl.ds(0, LANES)], green_top, done)
+    copy.start()
     rows = lam.shape[0]
     inner = iota((STEP_ROWS, LANES), 1) < LANES - 1
     carry = jnp.zeros((1, LANES), f32)
@@ -301,6 +303,7 @@
     sums[...] = total
     sides = take_sides(held[...])
     held_sides[...] = jnp.concatenate([fold(sides[0:1]), fold(sides[1:2])], 0)
+    copy.wait()
 
 
 def face(low, high, flux):
@@ -343,7 +346,7 @@
     lat_lines[...] = jnp.concatenate(
         [
             adj_l, c_l, g_l, other[POINT : POINT + 1], mine[POINT : POINT + 1],
-            jnp.zeros((3, LANES), f32),
+            other[OCEAN : OCEAN + 1], jnp.zeros((2, LANES), f32),
         ],
         0,
     )
@@ -400,7 +403,7 @@
     north_end = jnp.where(lat == 0, 1.0, 0.0)
     green_spread(
         green, coarse, lambda k: first[k // blocks, k % blocks : k % blocks + 1, :],
-        acc, tables, pot, 0,
+        acc, tables, pot,
     )
     put = put_sides(faces[ADJ], [(slope_ratio, -slope_ratio)])
     adj_l = lat_lines[ADJ_L : ADJ_L + 1, :]
@@ -471,7 +474,20 @@
     part = jnp.concatenate([own, east_part, west_part, lat_part], 0)
     begin = 4 * blocks
     deep = begin + half
-    edge_rows = jnp.concatenate([edge, jnp.zeros((half - 1, LANES), f32)], 0)
+    first_lane = iota((1, LANES), 1) == 0
+
+    def corners(block):
+        return jnp.where(
+            first_lane,
+            block[0:1],
+            jnp.broadcast_to(block[half : half + 1, 0:1], (1, LANES)),
+        )
+
+    edge_rows = jnp.concatenate(
+        [edge, held[0:1, :], corners(faces[GAIN]), corners(faces[RATIO])]
+        + [jnp.zeros((1, LANES), f32)] * (half - 4),
+        0,
+    )
     for target in range(n_lon * n_lat):
         shared = jnp.where(
             target == west, sides[:half], jnp.where(target == east, sides[half:], edge_rows)
@@ -479,10 +495,13 @@
         payload[target * deep : (target + 1) * deep, :] = jnp.concatenate([part, shared], 0)
 
 
-def edge_kernel(
-    first, second, green, ocean, held, faces, lat_lines, lam_sides, lam_edge,
-    edge, loads, acc, put, north_line, *, points, n_lon, n_lat,
+def last_kernel(
+    first, second, green, green_north, coarse, ocean, held, faces, lat_lines, lam_sides, lam_edge,
+    lam_out, payload, put, north_line, loads, top, done, acc, tables, pot,
+    *, points, n_lon, n_lat,
 ):
+    copy = pltpu.make_async_copy(green_north, top, done)
+    copy.start()
     rows = held.shape[0]
     blocks = points // LANES
     half = rows // LANES
@@ -503,18 +522,16 @@
             loads[here * blocks : (here + 1) * blocks, :] = (
                 total * first[here, blocks : 2 * blocks, :]
             )
-    acc[...] = green_rows(green, 0, lambda k: loads[k : k + 1, :])
-    potential = sum_lanes(acc[...])
     west, east, other = neighbours(n_lon, n_lat)
 
-    def shared(owner, count):
-        return second[pl.ds(owner * deep + 4 * blocks, count), :]
-
-    far = jnp.concatenate([shared(west, half), shared(east, half)], 0)
+    def shared(owner, row, count):
+        return second[pl.ds(owner * deep + 4 * blocks + row, count), :]
+
+    far = jnp.concatenate([shared(west, 0, half), shared(east, 0, half)], 0)
     rise = jnp.where(west_rows(), lam_sides[...] - far, far - lam_sides[...])
     adj = faces[GAIN] + faces[RATIO] * rise
     put[...] = put_sides(adj, [(slope_ratio, -slope_ratio), (0.0, 1.0)])
-    rise = shared(other, 1) - lam_edge[...]
+    rise = shared(other, 0, 1) - lam_edge[...]
     adj_l = lat_lines[G_L : G_L + 1, :] + lat_lines[C_L : C_L + 1, :] * jnp.where(
         lat == 0, rise, -rise
     )
@@ -523,23 +540,25 @@
     put[0:1, :LANES] = put[0:1, :LANES] + slope_ratio * from_south
     put[rows - 1 : rows, :LANES] = put[rows - 1 : rows, :LANES] - slope_ratio * from_north
     north_line[...] = from_north
-    edge[...] = ocean[0:1, :].astype(f32) * (
-        held[0:1, :] + put[0:1, :LANES] - attract_coef * potential[0:1, :]
-    )
-
-
-def last_kernel(
-    loads, start_acc, put, green, coarse, ocean, held, lam_out, payload, acc, tables, pot,
-    *, points, n_lon,
-):
-    rows = coarse.shape[0]
-    acc[...] = start_acc[...]
-    green_spread(green, coarse, lambda k: loads[k : k + 1, :], acc, tables, pot, 1)
+    green_spread(green, coarse, lambda k: loads[k : k + 1, :], acc, tables, pot)
     for start in range(0, rows, STEP_ROWS):
         at = slice(start, start + STEP_ROWS)
         lam_out[at, :] = ocean[at, :].astype(f32) * (
             held[at, :] + put[at, :LANES] - attract_coef * pot[at, :]
         )
+    copy.wait()
+    potential = sum_lanes(green_rows(top, 0, lambda k: loads[k : k + 1, :]))[0:1]
+    diagonal = lambda owner: shared(owner + 1 - 2 * lat, 0, 1)
+    lam_n = shared(other, 0, 1)
+    lane = iota((1, LANES), 1)
+    rise = jnp.where(
+        lane == 0, lam_n - roll_west(diagonal(west)), roll_east(diagonal(east)) - lam_n
+    )
+    adj = shared(other, 2, 1) + shared(other, 3, 1) * rise
+    flow = jnp.where(lane == 0, adj, jnp.where(lane == LANES - 1, -adj, 0.0)) + adj_l
+    lam_north = lat_lines[MASK_L : MASK_L + 1, :] * (
+        shared(other, 1, 1) + slope_ratio * flow - attract_coef * potential
+    )
     span = rows // n_lon
     for target in range(n_lon):
         start = target * (span + 1)
@@ -548,7 +567,7 @@
             stop = (target + 1) * span
             payload[start + span : start + span + 1, :] = lam_out[stop : stop + 1, :]
         else:
-            payload[start + span : start + span + 1, :] = jnp.zeros((1, LANES), f32)
+            payload[start + span : start + span + 1, :] = lam_north
 
 
 def bands_kernel(
@@ -594,17 +613,18 @@
         copy.wait()
 
 
-def call(kernel, shapes, scratch, args, name, far=False, far_out=False):
+def call(kernel, shapes, scratch, args, name, far=(), far_out=(), limit=16, weight=4):
     vmem = pl.BlockSpec(memory_space=pltpu.VMEM)
+    away = pl.BlockSpec(memory_space=pl.ANY)
     shapes = [(shape, f32) if isinstance(shape[0], int) else shape for shape in shapes]
     return pl.pallas_call(
         kernel,
         out_shape=[jax.ShapeDtypeStruct(shape, kind) for shape, kind in shapes],
-        in_specs=[pl.BlockSpec(memory_space=pltpu.HBM) if far else vmem] * len(args),
-        out_specs=[pl.BlockSpec(memory_space=pl.ANY) if far_out else vmem] * len(shapes),
+        in_specs=[away if k in far else vmem for k in range(len(args))],
+        out_specs=[away if k in far_out else vmem for k in range(len(shapes))],
         scratch_shapes=scratch,
-        compiler_params=pltpu.CompilerParams(vmem_limit_bytes=(52 << 20) if far else 16 << 20),
-        cost_estimate=pl.CostEstimate(flops=4 << 30, bytes_accessed=16 << 20, transcendentals=0),
+        compiler_params=pltpu.CompilerParams(vmem_limit_bytes=limit << 20),
+        cost_estimate=pl.CostEstimate(flops=weight << 30, bytes_accessed=16 << 20, transcendentals=0),
         name=name,
     )(*args)
 
@@ -621,7 +641,7 @@
         functools.partial(pack_kernel, points=points),
         [(6 * tall, cols), (6 * tall, cols), (8, cols)]
         + [(grid, field.dtype) for field in fields],
-        [pltpu.SemaphoreType.DMA((7,))], fields, "pack", far=True,
+        [pltpu.SemaphoreType.DMA((7,))], fields, "pack", far=range(7), limit=52,
     )
     ocean, coarse_of = fields[5:]
     forward = [(k, (k + 1) % n_lon) for k in range(n_lon)]
@@ -629,17 +649,23 @@
     from_west = lax.ppermute(to_east, "lon", forward)
     from_east = lax.ppermute(to_west, "lon", backward)
     from_lat = lax.ppermute(to_lat, "lat", [(0, 1), (1, 0)])
-    held, gu, cu, gv, cv, sums, left, right, held_sides = call(
+    held, gu, cu, gv, cv, sums, left, right, held_sides, green_top = call(
         functools.partial(inner_kernel, points=points),
         [grid] * 5
         + [((PIECES + 1) * HIGH, LOW), ((HIGH, rows * cols), bf16), ((LOW, rows * cols), bf16)]
-        + [(2 * tall, cols)],
-        [pltpu.VMEM(grid, f32)], fields, "inner",
-    )
+        + [(2 * tall, cols), (LANES, green.shape[1])],
+        [pltpu.VMEM(grid, f32), pltpu.SemaphoreType.DMA(())], (*fields, green), "inner",
+        far=(7,), far_out=(9,), limit=INNER_LIMIT,
+    )
+    green_top, from_west, from_east, from_lat = lax.optimization_barrier(
+        (green_top, from_west, from_east, from_lat)
+    )
+    green_north = lax.ppermute(green_top, "lat", [(0, 1), (1, 0)])
     payload, faces, lat_lines = call(
         functools.partial(rim_kernel, points=points),
         [(owners, 8, LANES), (7, 2 * tall, cols), (8, cols)], [],
         (to_east, to_west, to_lat, from_west, from_east, from_lat, sums, held_sides), "rim",
+        weight=16,
     )
     first = lax.all_to_all(payload, ("lon", "lat"), 0, 0, tiled=True)
     deep = 4 * blocks + tall
@@ -659,20 +685,21 @@
         payload.reshape(owners, deep, 1, LANES), ("lon", "lat"), 0, 0, tiled=True
     ).reshape(payload.shape)
     span = rows // n_lon
-    edge, loads, start_acc, put, north_line = call(
-        functools.partial(edge_kernel, points=points, n_lon=n_lon, n_lat=n_lat),
-        [(1, cols), (owners * blocks, LANES), (LANES, LANES), (rows, 2 * cols), (1, cols)],
-        [],
-        (first, second, green, ocean, held, faces, lat_lines, lam_sides, lam_edge), "edge",
-    )
-    lam, payload = call(
-        functools.partial(last_kernel, points=points, n_lon=n_lon),
-        [grid, (rows + n_lon, cols)],
-        green_scratch,
-        (loads, start_acc, put, green, coarse_of, ocean, held), "last",
-    )
-    edge = lax.all_gather(edge, "lat", axis=0)[1]
-    payload = lax.dynamic_update_slice(payload, edge, (rows + n_lon - 1, 0))
+    lam, payload, put, north_line = call(
+        functools.partial(last_kernel, points=points, n_lon=n_lon, n_lat=n_lat),
+        [grid, (rows + n_lon, cols), (rows, 2 * cols), (1, cols)],
+        [
+            pltpu.VMEM((owners * blocks, LANES), f32),
+            pltpu.VMEM(green_top.shape, f32),
+            pltpu.SemaphoreType.DMA(()),
+        ]
+        + green_scratch,
+        (
+            first, second, green, green_north, coarse_of, ocean, held, faces, lat_lines,
+            lam_sides, lam_edge,
+        ),
+        "last", far=(3,),
+    )
     parts = lax.all_to_all(
         payload.reshape(n_lon, span + 1, 1, LANES), "lon", 0, 0, tiled=True
     ).reshape(payload.shape)
@@ -686,7 +713,7 @@
                 pltpu.VMEM((3, span, n_lon * cols), f32),
                 pltpu.SemaphoreType.DMA((6,)),
             ],
-            (parts, lam, adj_u, adj_v, put, north_line), "bands", far_out=True,
+            (parts, lam, adj_u, adj_v, put, north_line), "bands", far_out=range(4),
         )
     )
 

time: 58.1 us -> 181 us (3.12)
  Pallas kernels: 13.4 us -> 139 us
  blocking collectives: 37.5 us -> 33.7 us
    pallas_call x7 -> x6, Pallas kernels: 13.4 us -> 139 us  [call(): pl.pallas_call(kernel, out_shape=[jax.ShapeDtypeStruct(shape, kind) for s...]
  transfers between devices with their start and end apart: 3 -> 4, of which waited for: 0 -> 0; matrix products, arithmetic and copies ran while one was open for 0% -> 0% of each run, Pallas kernels for 5% -> 74%
where the time goes in v8:
time: 181 us
  Pallas kernels  139 us (77%)
  blocking collectives  33.7 us (19%)
  starting transfers between devices  6.7 us (4%)
    pallas_call x6, Pallas kernels, call(): pl.pallas_call(kernel, out_shape=[jax.ShapeDtypeStruct(shape, kind) for s...  139 us
    all_to_all x1, blocking collectives, body(): lax.all_to_all(payload.reshape(n_lon, span + 1, 1, LANES), 'lon', 0, 0, t...  12.3 us
    all_to_all x1, blocking collectives, body(): lax.all_to_all(payload.reshape(owners, deep, 1, LANES), ('lon', 'lat'), 0...  11.1 us
    all_to_all x1, blocking collectives, body(): first = lax.all_to_all(payload, ('lon', 'lat'), 0, 0, tiled=True)  10.3 us
  transfers between devices with their start and end apart: 4, of which 0 were waited for; matrix products, arithmetic and copies ran while one was open for 0% of the time, Pallas kernels for 74%

profile of v8, /device:TPU:0, one launch (start us, length us, event | category | flops | bytes accessed | tf_op | source)
XLA Modules:
  0.0 180.6 jit_solution(9101049661046039826)
XLA Ops:
  0.6 2.3 %pack.1 = (f32[24,128]{1,0:T(8,128)S(1)}, f32[24,128]{1,0:T(8,128)S(1)}, f32[8,128]{1,0:T(8,128)S(1)}, f32[512,128]{1,0:T(8,128)S(1)}, f32[512,128]{1,0:T(8,128)...) custom-call(f32[512,128]{1,0:T(8,128)} %refs_0_.1, ...), custom_call_target="tpu_custom_call" | custom-call | flops 4294967296 | bytes 16777216 | tf_op jit(solution)/shard_map/pack/pallas_call | solution.py:620
  2.9 3.0 %collective-permute-start = (f32[24,128]{1,0:T(8,128)S(1)}, f32[24,128]{1,0:T(8,128)S(1)}, u32[]{:S(2)}, u32[]{:S(2)}) collective-permute-start(f32[24,128]{1,0:T(8,128)S(1)} %get-tuple-element.41.own_east), channel_id=1, source_target_pairs={{0,2},{2,4},{4,6},{6,8},{8,10},{10,12},{12,14},{14,0},{1,3},{3,5},... | collective-permute-start | bytes 36872 | tf_op jit(solution)/shard_map/ppermute | solution.py:649
  5.9 3.1 %collective-permute-start.1 = (f32[24,128]{1,0:T(8,128)S(1)}, f32[24,128]{1,0:T(8,128)S(1)}, u32[]{:S(2)}, u32[]{:S(2)}) collective-permute-start(f32[24,128]{1,0:T(8,128)S(1)} %get-tuple-element.42.own_west), channel_id=1, source_target_pairs={{2,0},{4,2},{6,4},{8,6},{10,8},{12,10},{14,12},{0,14},{3,1},{5,3},... | collective-permute-start | bytes 36872 | tf_op jit(solution)/shard_map/ppermute | solution.py:650
  9.0 0.0 collective-permute-start.2
  9.0 128.2 %inner.1 = (f32[512,128]{1,0:T(8,128)S(1)}, f32[512,128]{1,0:T(8,128)S(1)}, f32[512,128]{1,0:T(8,128)S(1)}, f32[512,128]{1,0:T(8,128)S(1)}, f32[512,128]{1,0:T(8...) custom-call(f32[512,128]{1,0:T(8,128)S(1)} %get-tuple-element.44.lam, ...), custom_call_target="tpu_custom_call" | custom-call | flops 4294967296 | bytes 16777216 | tf_op jit(solution)/shard_map/inner/pallas_call | solution.py:620
  137.2 0.0 collective-permute-done.2.from_lat
  137.2 0.0 collective-permute-done.from_west
  137.2 0.0 collective-permute-done.1.from_east
  137.2 0.6 collective-permute-start.3
  137.8 0.0 slice-start
  137.8 0.0 slice-start.1
  137.8 0.0 slice-start.2
  137.8 0.3 rim.1
  138.1 10.3 %all_to_all.15.first = f32[16,8,128]{2,1,0:T(8,128)S(1)} all-to-all(f32[16,8,128]{2,1,0:T(8,128)S(1)} %get-tuple-element.57), channel_id=1, replica_groups=mesh['groups'=2,'lon'=8,'lat'=2] {'lon','lat'}, dimensions={0} | all-to-all | bytes 131072 | tf_op jit(solution)/shard_map/all_to_all | solution.py:670
  148.4 0.0 slice-done
  148.4 0.0 slice-done.1
  148.4 0.0 slice-done.2
  148.4 0.0 slice-done.3
  148.4 4.4 %second.1 = (f32[320,128]{1,0:T(8,128)S(1)}, f32[512,128]{1,0:T(8,128)S(1)}, f32[512,128]{1,0:T(8,128)S(1)}, f32[512,128]{1,0:T(8,128)S(1)}, f32[8,128]{1,0:T(8,128)S(1)}, /*index=5*/f32[1,128]{1,0:T(1,128)S(1)}) custom-call(f32[16,8,128]{2,1,0:T(8,128)S(1)} %all_to_all.15.first, f32[512,8192]{1,0:T(8,128)S(1)} %bitcast.5, ...), custom_call_target="tpu_custom_call" | custom-call | flops 4294967296 | bytes 16777216 | tf_op jit(solution)/shard_map/second/pallas_call | solution.py:620
  152.8 11.1 %all_to_all.16 = f32[16,20,1,128]{3,2,1,0:T(1,128)S(1)} all-to-all(f32[16,20,1,128]{3,2,1,0:T(1,128)S(1)} %bitcast.9), channel_id=1, replica_groups=mesh['groups'=2,'lon'=8,'lat'=2] {'lon','lat'}, dimensions={0} | all-to-all | bytes 327680 | tf_op jit(solution)/shard_map/all_to_all | solution.py:684
  163.9 0.0 collective-permute-done.3.green_north
  163.9 3.2 %last.1 = (f32[512,128]{1,0:T(8,128)S(1)}, f32[520,128]{1,0:T(8,128)S(1)}, f32[512,256]{1,0:T(8,128)S(1)}, f32[1,128]{1,0:T(1,128)S(1)}) custom-call(f32[16,8,128]{2,1,0:T(8,128)S(1)} %all_to_all.15.first, f32[320,128]{1,0:T(8,128)S(1)} %bitcast.6, f32[512,8192]{1,0:T(8,128)S(1)} %bitcast.5, f32[128,8192]{1,0:T(8,128)S(1)} %collective-permute-done.3.green_north, ...), custom_call_target="tpu_custom_call" | custom-call | flops 4294967296 | bytes 16777216 | tf_op jit(solution)/shard_map/last/pallas_call | solution.py:620
  167.1 12.3 %all_to_all.17 = f32[8,65,1,128]{3,2,1,0:T(1,128)S(1)} all-to-all(f32[8,65,1,128]{3,2,1,0:T(1,128)S(1)} %bitcast.7), channel_id=1, replica_groups=mesh['groups'=2,'lon'=8,'lat'=2] {'lon'}, dimensions={0} | all-to-all | bytes 532480 | tf_op jit(solution)/shard_map/all_to_all | solution.py:703
  179.4 1.2 bands.1
  (2 shorter events, 0.0 us)
Async XLA Ops:
  2.9 134.3 %collective-permute-start = (f32[24,128]{1,0:T(8,128)S(1)}, f32[24,128]{1,0:T(8,128)S(1)}, u32[]{:S(2)}, u32[]{:S(2)}) collective-permute-start(f32[24,128]{1,0:T(8,128)S(1)} %get-tuple-element.41.own_east), channel_id=1, source_target_pairs={{0,2},{2,4},{4,6},{6,8},{8,10},{10,12},{12,14},{14,0},{1,3},{3,5},... | collective-permute-start | bytes 36872 | tf_op jit(solution)/shard_map/ppermute | solution.py:649
  5.9 131.3 %collective-permute-start.1 = (f32[24,128]{1,0:T(8,128)S(1)}, f32[24,128]{1,0:T(8,128)S(1)}, u32[]{:S(2)}, u32[]{:S(2)}) collective-permute-start(f32[24,128]{1,0:T(8,128)S(1)} %get-tuple-element.42.own_west), channel_id=1, source_target_pairs={{2,0},{4,2},{6,4},{8,6},{10,8},{12,10},{14,12},{0,14},{3,1},{5,3},... | collective-permute-start | bytes 36872 | tf_op jit(solution)/shard_map/ppermute | solution.py:650
  9.0 128.2 %collective-permute-start.2 = (f32[8,128]{1,0:T(8,128)S(1)}, f32[8,128]{1,0:T(8,128)S(1)}, u32[]{:S(2)}, u32[]{:S(2)}) collective-permute-start(f32[8,128]{1,0:T(8,128)S(1)} %get-tuple-element.43.own_lat), channel_id=1, source_target_pairs={{0,1},{1,0},{2,3},{3,2},{4,5},{5,4},{6,7},{7,6},{8,9},{9,8},{10,11... | collective-permute-start | bytes 12296 | tf_op jit(solution)/shard_map/ppermute | solution.py:651
  137.2 26.6 %collective-permute-start.3 = (f32[128,8192]{1,0:T(8,128)}, f32[128,8192]{1,0:T(8,128)S(1)}, u32[]{:S(2)}, u32[]{:S(2)}) collective-permute-start(f32[128,8192]{1,0:T(8,128)} %get-tuple-element.68), channel_id=1, source_target_pairs={{0,1},{1,0},{2,3},{3,2},{4,5},{5,4},{6,7},{7,6},{8,9},{9,8},{10,11... | collective-permute-start | bytes 12582920 | tf_op jit(solution)/shard_map/ppermute | solution.py:663
  137.8 10.6 %slice-start = ((s8[16777216]{0:T(1024)(128)(4,1)}), s8[4194304]{0:T(1024)(128)(4,1)S(1)}, s32[]{:S(2)}) async-start(s8[16777216]{0:T(1024)(128)(4,1)} %bitcast.4), calls=%async_computation.3 | async-start | bytes 8388608
  137.8 10.6 %slice-start.1 = ((s8[16777216]{0:T(1024)(128)(4,1)}), s8[4194304]{0:T(1024)(128)(4,1)S(1)}, s32[]{:S(2)}) async-start(s8[16777216]{0:T(1024)(128)(4,1)} %bitcast.4), calls=%async_computation.4 | async-start | bytes 8388608
  137.8 10.6 %slice-start.2 = ((s8[16777216]{0:T(1024)(128)(4,1)}), s8[4194304]{0:T(1024)(128)(4,1)S(1)}, s32[]{:S(2)}) async-start(s8[16777216]{0:T(1024)(128)(4,1)} %bitcast.4), calls=%async_computation.5 | async-start | bytes 8388608
  137.8 10.6 %slice-start.3 = ((s8[16777216]{0:T(1024)(128)(4,1)}), s8[4194304]{0:T(1024)(128)(4,1)S(1)}, s32[]{:S(2)}) async-start(s8[16777216]{0:T(1024)(128)(4,1)} %bitcast.4), calls=%async_computation.6 | async-start | bytes 8388608

commit v9 on v8

--- a/solution.py
+++ b/solution.py
@@ -655,7 +655,7 @@
         + [((PIECES + 1) * HIGH, LOW), ((HIGH, rows * cols), bf16), ((LOW, rows * cols), bf16)]
         + [(2 * tall, cols), (LANES, green.shape[1])],
         [pltpu.VMEM(grid, f32), pltpu.SemaphoreType.DMA(())], (*fields, green), "inner",
-        far=(7,), far_out=(9,), limit=INNER_LIMIT,
+        far=(7,), limit=INNER_LIMIT,
     )
     green_top, from_west, from_east, from_lat = lax.optimization_barrier(
         (green_top, from_west, from_east, from_lat)

time: 181 us -> 59.4 us (0.33)
  Pallas kernels: 139 us -> 18.1 us
    pallas_call x6, Pallas kernels: 139 us -> 18.1 us  [call(): pl.pallas_call(kernel, out_shape=[jax.ShapeDtypeStruct(shape, kind) for s...]
  transfers between devices with their start and end apart: 4 -> 4, of which waited for: 0 -> 0; matrix products, arithmetic and copies ran while one was open for 0% -> 0% of each run, Pallas kernels for 74% -> 19%
where the time goes in v9:
time: 59.4 us; the launch traced here: 59.2 us
  blocking collectives  33.7 us (57%)
  Pallas kernels  18.1 us (30%)
  starting transfers between devices  6.7 us (11%)
  between operations  0.72 us (1%)
    pallas_call x6, Pallas kernels, call(): pl.pallas_call(kernel, out_shape=[jax.ShapeDtypeStruct(shape, kind) for s...  18.1 us
    all_to_all x1, blocking collectives, body(): lax.all_to_all(payload.reshape(n_lon, span + 1, 1, LANES), 'lon', 0, 0, t...  12.3 us
    all_to_all x1, blocking collectives, body(): lax.all_to_all(payload.reshape(owners, deep, 1, LANES), ('lon', 'lat'), 0...  11.1 us
    all_to_all x1, blocking collectives, body(): first = lax.all_to_all(payload, ('lon', 'lat'), 0, 0, tiled=True)  10.3 us
    ppermute x1, starting transfers between devices, body(): from_east = lax.ppermute(to_west, 'lon', backward)  3.1 us
    ppermute x1, starting transfers between devices, body(): from_west = lax.ppermute(to_east, 'lon', forward)  3.02 us
  transfers between devices with their start and end apart: 4, of which 0 were waited for; matrix products, arithmetic and copies ran while one was open for 0% of the time, Pallas kernels for 19%

profile of v9, /device:TPU:0, one launch (start us, length us, event | category | flops | bytes accessed | tf_op | source)
XLA Modules:
  0.0 59.2 jit_solution(8419541458028576009)
XLA Ops:
  0.6 2.3 %pack.1 = (f32[24,128]{1,0:T(8,128)S(1)}, f32[24,128]{1,0:T(8,128)S(1)}, f32[8,128]{1,0:T(8,128)S(1)}, f32[512,128]{1,0:T(8,128)S(1)}, f32[512,128]{1,0:T(8,128)...) custom-call(f32[512,128]{1,0:T(8,128)} %refs_0_.1, ...), custom_call_target="tpu_custom_call" | custom-call | flops 4294967296 | bytes 16777216 | tf_op jit(solution)/shard_map/pack/pallas_call | solution.py:620
  2.9 3.0 %collective-permute-start = (f32[24,128]{1,0:T(8,128)S(1)}, f32[24,128]{1,0:T(8,128)S(1)}, u32[]{:S(2)}, u32[]{:S(2)}) collective-permute-start(f32[24,128]{1,0:T(8,128)S(1)} %get-tuple-element.41.own_east), channel_id=1, source_target_pairs={{0,2},{2,4},{4,6},{6,8},{8,10},{10,12},{12,14},{14,0},{1,3},{3,5},... | collective-permute-start | bytes 36872 | tf_op jit(solution)/shard_map/ppermute | solution.py:649
  5.9 3.1 %collective-permute-start.1 = (f32[24,128]{1,0:T(8,128)S(1)}, f32[24,128]{1,0:T(8,128)S(1)}, u32[]{:S(2)}, u32[]{:S(2)}) collective-permute-start(f32[24,128]{1,0:T(8,128)S(1)} %get-tuple-element.42.own_west), channel_id=1, source_target_pairs={{2,0},{4,2},{6,4},{8,6},{10,8},{12,10},{14,12},{0,14},{3,1},{5,3},... | collective-permute-start | bytes 36872 | tf_op jit(solution)/shard_map/ppermute | solution.py:650
  9.0 0.0 collective-permute-start.2
  9.0 6.8 %inner.1 = (f32[512,128]{1,0:T(8,128)S(1)}, f32[512,128]{1,0:T(8,128)S(1)}, f32[512,128]{1,0:T(8,128)S(1)}, f32[512,128]{1,0:T(8,128)S(1)}, f32[512,128]{1,0:T(8...) custom-call(f32[512,128]{1,0:T(8,128)S(1)} %get-tuple-element.44.lam, ...), custom_call_target="tpu_custom_call" | custom-call | flops 4294967296 | bytes 16777216 | tf_op jit(solution)/shard_map/inner/pallas_call | solution.py:620
  15.8 0.0 collective-permute-done.2.from_lat
  15.8 0.0 collective-permute-done.from_west
  15.9 0.0 collective-permute-done.1.from_east
  15.9 0.6 collective-permute-start.3
  16.4 0.0 slice-start
  16.4 0.0 slice-start.1
  16.4 0.0 slice-start.2
  16.4 0.3 rim.1
  16.7 10.3 %all_to_all.15.first = f32[16,8,128]{2,1,0:T(8,128)S(1)} all-to-all(f32[16,8,128]{2,1,0:T(8,128)S(1)} %get-tuple-element.57), channel_id=1, replica_groups=mesh['groups'=2,'lon'=8,'lat'=2] {'lon','lat'}, dimensions={0} | all-to-all | bytes 131072 | tf_op jit(solution)/shard_map/all_to_all | solution.py:670
  27.0 0.0 slice-done
  27.0 0.0 slice-done.1
  27.0 0.0 slice-done.2
  27.0 0.0 slice-done.3
  27.0 4.4 %second.1 = (f32[320,128]{1,0:T(8,128)S(1)}, f32[512,128]{1,0:T(8,128)S(1)}, f32[512,128]{1,0:T(8,128)S(1)}, f32[512,128]{1,0:T(8,128)S(1)}, f32[8,128]{1,0:T(8,128)S(1)}, /*index=5*/f32[1,128]{1,0:T(1,128)S(1)}) custom-call(f32[16,8,128]{2,1,0:T(8,128)S(1)} %all_to_all.15.first, f32[512,8192]{1,0:T(8,128)S(1)} %bitcast.5, ...), custom_call_target="tpu_custom_call" | custom-call | flops 4294967296 | bytes 16777216 | tf_op jit(solution)/shard_map/second/pallas_call | solution.py:620
  31.4 11.1 %all_to_all.16 = f32[16,20,1,128]{3,2,1,0:T(1,128)S(1)} all-to-all(f32[16,20,1,128]{3,2,1,0:T(1,128)S(1)} %bitcast.9), channel_id=1, replica_groups=mesh['groups'=2,'lon'=8,'lat'=2] {'lon','lat'}, dimensions={0} | all-to-all | bytes 327680 | tf_op jit(solution)/shard_map/all_to_all | solution.py:684
  42.5 0.0 collective-permute-done.3.green_north
  42.5 3.2 %last.1 = (f32[512,128]{1,0:T(8,128)S(1)}, f32[520,128]{1,0:T(8,128)S(1)}, f32[512,256]{1,0:T(8,128)S(1)}, f32[1,128]{1,0:T(1,128)S(1)}) custom-call(f32[16,8,128]{2,1,0:T(8,128)S(1)} %all_to_all.15.first, f32[320,128]{1,0:T(8,128)S(1)} %bitcast.6, f32[512,8192]{1,0:T(8,128)S(1)} %bitcast.5, f32[128,8192]{1,0:T(8,128)S(1)} %collective-permute-done.3.green_north, ...), custom_call_target="tpu_custom_call" | custom-call | flops 4294967296 | bytes 16777216 | tf_op jit(solution)/shard_map/last/pallas_call | solution.py:620
  45.7 12.3 %all_to_all.17 = f32[8,65,1,128]{3,2,1,0:T(1,128)S(1)} all-to-all(f32[8,65,1,128]{3,2,1,0:T(1,128)S(1)} %bitcast.7), channel_id=1, replica_groups=mesh['groups'=2,'lon'=8,'lat'=2] {'lon'}, dimensions={0} | all-to-all | bytes 532480 | tf_op jit(solution)/shard_map/all_to_all | solution.py:703
  58.0 1.2 %bands.1 = (f32[512,128]{1,0:T(8,128)}, f32[512,128]{1,0:T(8,128)}, f32[512,128]{1,0:T(8,128)}, f32[3,1,64,1024]{3,2,1,0:T(8,128)}) custom-call(f32[520,128]{1,0:T(8,128)S(1)} %bitcast.8, f32[512,128]{1,0:T(8,128)S(1)} %get-tuple-element.73.lam, f32[512,128]{1,0:T(8,128)S(1)} %get-tuple-element.74.adj_u, f32[512,128]{1,0:T(8,128)S(1)} %get-tuple-element.75.adj_v, ...), custom_call_target="tpu_custom_call" | custom-call | flops 4294967296 | bytes 16777216 | tf_op jit(solution)/shard_map/bands/pallas_call | solution.py:620
  (2 shorter events, 0.0 us)
Async XLA Ops:
  2.9 12.9 %collective-permute-start = (f32[24,128]{1,0:T(8,128)S(1)}, f32[24,128]{1,0:T(8,128)S(1)}, u32[]{:S(2)}, u32[]{:S(2)}) collective-permute-start(f32[24,128]{1,0:T(8,128)S(1)} %get-tuple-element.41.own_east), channel_id=1, source_target_pairs={{0,2},{2,4},{4,6},{6,8},{8,10},{10,12},{12,14},{14,0},{1,3},{3,5},... | collective-permute-start | bytes 36872 | tf_op jit(solution)/shard_map/ppermute | solution.py:649
  5.9 9.9 %collective-permute-start.1 = (f32[24,128]{1,0:T(8,128)S(1)}, f32[24,128]{1,0:T(8,128)S(1)}, u32[]{:S(2)}, u32[]{:S(2)}) collective-permute-start(f32[24,128]{1,0:T(8,128)S(1)} %get-tuple-element.42.own_west), channel_id=1, source_target_pairs={{2,0},{4,2},{6,4},{8,6},{10,8},{12,10},{14,12},{0,14},{3,1},{5,3},... | collective-permute-start | bytes 36872 | tf_op jit(solution)/shard_map/ppermute | solution.py:650
  9.0 6.8 %collective-permute-start.2 = (f32[8,128]{1,0:T(8,128)S(1)}, f32[8,128]{1,0:T(8,128)S(1)}, u32[]{:S(2)}, u32[]{:S(2)}) collective-permute-start(f32[8,128]{1,0:T(8,128)S(1)} %get-tuple-element.43.own_lat), channel_id=1, source_target_pairs={{0,1},{1,0},{2,3},{3,2},{4,5},{5,4},{6,7},{7,6},{8,9},{9,8},{10,11... | collective-permute-start | bytes 12296 | tf_op jit(solution)/shard_map/ppermute | solution.py:651
  15.9 26.6 %collective-permute-start.3 = (f32[128,8192]{1,0:T(8,128)}, f32[128,8192]{1,0:T(8,128)S(1)}, u32[]{:S(2)}, u32[]{:S(2)}) collective-permute-start(f32[128,8192]{1,0:T(8,128)} %get-tuple-element.68), channel_id=1, source_target_pairs={{0,1},{1,0},{2,3},{3,2},{4,5},{5,4},{6,7},{7,6},{8,9},{9,8},{10,11... | collective-permute-start | bytes 12582920 | tf_op jit(solution)/shard_map/ppermute | solution.py:663
  16.4 10.6 %slice-start = ((s8[16777216]{0:T(1024)(128)(4,1)}), s8[4194304]{0:T(1024)(128)(4,1)S(1)}, s32[]{:S(2)}) async-start(s8[16777216]{0:T(1024)(128)(4,1)} %bitcast.4), calls=%async_computation.3 | async-start | bytes 8388608
  16.4 10.6 %slice-start.1 = ((s8[16777216]{0:T(1024)(128)(4,1)}), s8[4194304]{0:T(1024)(128)(4,1)S(1)}, s32[]{:S(2)}) async-start(s8[16777216]{0:T(1024)(128)(4,1)} %bitcast.4), calls=%async_computation.4 | async-start | bytes 8388608
  16.4 10.6 %slice-start.2 = ((s8[16777216]{0:T(1024)(128)(4,1)}), s8[4194304]{0:T(1024)(128)(4,1)S(1)}, s32[]{:S(2)}) async-start(s8[16777216]{0:T(1024)(128)(4,1)} %bitcast.4), calls=%async_computation.5 | async-start | bytes 8388608
  16.4 10.6 %slice-start.3 = ((s8[16777216]{0:T(1024)(128)(4,1)}), s8[4194304]{0:T(1024)(128)(4,1)S(1)}, s32[]{:S(2)}) async-start(s8[16777216]{0:T(1024)(128)(4,1)} %bitcast.4), calls=%async_computation.6 | async-start | bytes 8388608

commit v10 on v9

--- a/solution.py
+++ b/solution.py
@@ -258,10 +258,26 @@
 
 def inner_kernel(
     lam, east, north, depth, drag, ocean, coarse, green,
-    held, gu, cu, gv, cv, sums, left, right, held_sides, green_top, source, done, *, points,
+    held, gu, cu, gv, cv, sums, left, right, held_sides, green_top, source, top, done, *, points,
 ):
-    copy = pltpu.make_async_copy(green.at[pl.ds(0, LANES)], green_top, done)
-    copy.start()
+    tall = LANES // 4
+    parts = [pl.ds(k * tall, tall) for k in range(4)]
+    inward = [
+        pltpu.make_async_copy(green.at[part], top.at[part], done.at[k])
+        for k, part in enumerate(parts)
+    ]
+    outward = [
+        pltpu.make_async_copy(top.at[part], green_top.at[part], done.at[4 + k])
+        for k, part in enumerate(parts)
+    ]
+    for copy in inward:
+        copy.start()
+
+    def pass_on(which):
+        for k in which:
+            inward[k].wait()
+            outward[k].start()
+
     rows = lam.shape[0]
     inner = iota((STEP_ROWS, LANES), 1) < LANES - 1
     carry = jnp.zeros((1, LANES), f32)
@@ -292,8 +308,11 @@
         carry = adj_v[STEP_ROWS - 1 :]
         source[at, :] = src
         held[at, :] = lam_c + src
+    pass_on((0, 1))
     total = jnp.zeros(sums.shape, f32)
     for start in range(0, rows, SEG_ROWS):
+        if start == SEG_ROWS:
+            pass_on((2, 3))
         at = slice(start, start + SEG_ROWS)
         cells = slice(start * LANES, (start + SEG_ROWS) * LANES)
         high, low = one_hots(local_ids(coarse[at, :], points), points)
@@ -303,7 +322,8 @@
     sums[...] = total
     sides = take_sides(held[...])
     held_sides[...] = jnp.concatenate([fold(sides[0:1]), fold(sides[1:2])], 0)
-    copy.wait()
+    for copy in outward:
+        copy.wait()
 
 
 def face(low, high, flux):
@@ -654,8 +674,12 @@
         [grid] * 5
         + [((PIECES + 1) * HIGH, LOW), ((HIGH, rows * cols), bf16), ((LOW, rows * cols), bf16)]
         + [(2 * tall, cols), (LANES, green.shape[1])],
-        [pltpu.VMEM(grid, f32), pltpu.SemaphoreType.DMA(())], (*fields, green), "inner",
-        far=(7,), limit=INNER_LIMIT,
+        [
+            pltpu.VMEM(grid, f32),
+            pltpu.VMEM((LANES, green.shape[1]), f32),
+            pltpu.SemaphoreType.DMA((8,)),
+        ],
+        (*fields, green), "inner", far=(7,), far_out=(9,), limit=INNER_LIMIT,
     )
     green_top, from_west, from_east, from_lat = lax.optimization_barrier(
         (green_top, from_west, from_east, from_lat)

time: 59.4 us -> 58.1 us (0.978)
  Pallas kernels: 18.1 us -> 16.8 us
    pallas_call x6, Pallas kernels: 18.1 us -> 16.8 us  [call(): pl.pallas_call(kernel, out_shape=[jax.ShapeDtypeStruct(shape, kind) for s...]
  transfers between devices with their start and end apart: 4 -> 4, of which waited for: 0 -> 0; matrix products, arithmetic and copies ran while one was open for 0% -> 0% of each run, Pallas kernels for 19% -> 17%
where the time goes in v10:
time: 58.1 us; the launch traced here: 57.9 us
  blocking collectives  33.7 us (58%)
  Pallas kernels  16.8 us (29%)
  starting transfers between devices  6.7 us (12%)
  between operations  0.72 us (1%)
    pallas_call x6, Pallas kernels, call(): pl.pallas_call(kernel, out_shape=[jax.ShapeDtypeStruct(shape, kind) for s...  16.8 us
    all_to_all x1, blocking collectives, body(): lax.all_to_all(payload.reshape(n_lon, span + 1, 1, LANES), 'lon', 0, 0, t...  12.3 us
    all_to_all x1, blocking collectives, body(): lax.all_to_all(payload.reshape(owners, deep, 1, LANES), ('lon', 'lat'), 0...  11.1 us
    all_to_all x1, blocking collectives, body(): first = lax.all_to_all(payload, ('lon', 'lat'), 0, 0, tiled=True)  10.3 us
    ppermute x1, starting transfers between devices, body(): from_east = lax.ppermute(to_west, 'lon', backward)  3.1 us
    ppermute x1, starting transfers between devices, body(): from_west = lax.ppermute(to_east, 'lon', forward)  3.02 us
  transfers between devices with their start and end apart: 4, of which 0 were waited for; matrix products, arithmetic and copies ran while one was open for 0% of the time, Pallas kernels for 17%

profile of v10, /device:TPU:0, one launch (start us, length us, event | category | flops | bytes accessed | tf_op | source)
XLA Modules:
  0.0 57.9 jit_solution(4546050832398083374)
XLA Ops:
  0.6 2.3 %pack.1 = (f32[24,128]{1,0:T(8,128)S(1)}, f32[24,128]{1,0:T(8,128)S(1)}, f32[8,128]{1,0:T(8,128)S(1)}, f32[512,128]{1,0:T(8,128)S(1)}, f32[512,128]{1,0:T(8,128)...) custom-call(f32[512,128]{1,0:T(8,128)} %refs_0_.1, ...), custom_call_target="tpu_custom_call" | custom-call | flops 4294967296 | bytes 16777216 | tf_op jit(solution)/shard_map/pack/pallas_call | solution.py:640
  2.9 3.0 %collective-permute-start = (f32[24,128]{1,0:T(8,128)S(1)}, f32[24,128]{1,0:T(8,128)S(1)}, u32[]{:S(2)}, u32[]{:S(2)}) collective-permute-start(f32[24,128]{1,0:T(8,128)S(1)} %get-tuple-element.41.own_east), channel_id=1, source_target_pairs={{0,2},{2,4},{4,6},{6,8},{8,10},{10,12},{12,14},{14,0},{1,3},{3,5},... | collective-permute-start | bytes 36872 | tf_op jit(solution)/shard_map/ppermute | solution.py:669
  5.9 3.1 %collective-permute-start.1 = (f32[24,128]{1,0:T(8,128)S(1)}, f32[24,128]{1,0:T(8,128)S(1)}, u32[]{:S(2)}, u32[]{:S(2)}) collective-permute-start(f32[24,128]{1,0:T(8,128)S(1)} %get-tuple-element.42.own_west), channel_id=1, source_target_pairs={{2,0},{4,2},{6,4},{8,6},{10,8},{12,10},{14,12},{0,14},{3,1},{5,3},... | collective-permute-start | bytes 36872 | tf_op jit(solution)/shard_map/ppermute | solution.py:670
  9.0 0.0 collective-permute-start.2
  9.0 5.4 %inner.1 = (f32[512,128]{1,0:T(8,128)S(1)}, f32[512,128]{1,0:T(8,128)S(1)}, f32[512,128]{1,0:T(8,128)S(1)}, f32[512,128]{1,0:T(8,128)S(1)}, f32[512,128]{1,0:T(8...) custom-call(f32[512,128]{1,0:T(8,128)S(1)} %get-tuple-element.44.lam, ...), custom_call_target="tpu_custom_call" | custom-call | flops 4294967296 | bytes 16777216 | tf_op jit(solution)/shard_map/inner/pallas_call | solution.py:640
  14.5 0.0 collective-permute-done.2.from_lat
  14.5 0.0 collective-permute-done.from_west
  14.5 0.0 collective-permute-done.1.from_east
  14.5 0.6 collective-permute-start.3
  15.1 0.0 slice-start
  15.1 0.0 slice-start.1
  15.1 0.0 slice-start.2
  15.1 0.3 rim.1
  15.4 10.3 %all_to_all.15.first = f32[16,8,128]{2,1,0:T(8,128)S(1)} all-to-all(f32[16,8,128]{2,1,0:T(8,128)S(1)} %get-tuple-element.57), channel_id=1, replica_groups=mesh['groups'=2,'lon'=8,'lat'=2] {'lon','lat'}, dimensions={0} | all-to-all | bytes 131072 | tf_op jit(solution)/shard_map/all_to_all | solution.py:694
  25.7 0.0 slice-done
  25.7 0.0 slice-done.1
  25.7 0.0 slice-done.2
  25.7 0.0 slice-done.3
  25.7 4.4 %second.1 = (f32[320,128]{1,0:T(8,128)S(1)}, f32[512,128]{1,0:T(8,128)S(1)}, f32[512,128]{1,0:T(8,128)S(1)}, f32[512,128]{1,0:T(8,128)S(1)}, f32[8,128]{1,0:T(8,128)S(1)}, /*index=5*/f32[1,128]{1,0:T(1,128)S(1)}) custom-call(f32[16,8,128]{2,1,0:T(8,128)S(1)} %all_to_all.15.first, f32[512,8192]{1,0:T(8,128)S(1)} %bitcast.5, ...), custom_call_target="tpu_custom_call" | custom-call | flops 4294967296 | bytes 16777216 | tf_op jit(solution)/shard_map/second/pallas_call | solution.py:640
  30.1 11.1 %all_to_all.16 = f32[16,20,1,128]{3,2,1,0:T(1,128)S(1)} all-to-all(f32[16,20,1,128]{3,2,1,0:T(1,128)S(1)} %bitcast.9), channel_id=1, replica_groups=mesh['groups'=2,'lon'=8,'lat'=2] {'lon','lat'}, dimensions={0} | all-to-all | bytes 327680 | tf_op jit(solution)/shard_map/all_to_all | solution.py:708
  41.1 0.0 collective-permute-done.3.green_north
  41.1 3.2 %last.1 = (f32[512,128]{1,0:T(8,128)S(1)}, f32[520,128]{1,0:T(8,128)S(1)}, f32[512,256]{1,0:T(8,128)S(1)}, f32[1,128]{1,0:T(1,128)S(1)}) custom-call(f32[16,8,128]{2,1,0:T(8,128)S(1)} %all_to_all.15.first, f32[320,128]{1,0:T(8,128)S(1)} %bitcast.6, f32[512,8192]{1,0:T(8,128)S(1)} %bitcast.5, f32[128,8192]{1,0:T(8,128)S(1)} %collective-permute-done.3.green_north, ...), custom_call_target="tpu_custom_call" | custom-call | flops 4294967296 | bytes 16777216 | tf_op jit(solution)/shard_map/last/pallas_call | solution.py:640
  44.3 12.3 %all_to_all.17 = f32[8,65,1,128]{3,2,1,0:T(1,128)S(1)} all-to-all(f32[8,65,1,128]{3,2,1,0:T(1,128)S(1)} %bitcast.7), channel_id=1, replica_groups=mesh['groups'=2,'lon'=8,'lat'=2] {'lon'}, dimensions={0} | all-to-all | bytes 532480 | tf_op jit(solution)/shard_map/all_to_all | solution.py:727
  56.7 1.2 %bands.1 = (f32[512,128]{1,0:T(8,128)}, f32[512,128]{1,0:T(8,128)}, f32[512,128]{1,0:T(8,128)}, f32[3,1,64,1024]{3,2,1,0:T(8,128)}) custom-call(f32[520,128]{1,0:T(8,128)S(1)} %bitcast.8, f32[512,128]{1,0:T(8,128)S(1)} %get-tuple-element.73.lam, f32[512,128]{1,0:T(8,128)S(1)} %get-tuple-element.74.adj_u, f32[512,128]{1,0:T(8,128)S(1)} %get-tuple-element.75.adj_v, ...), custom_call_target="tpu_custom_call" | custom-call | flops 4294967296 | bytes 16777216 | tf_op jit(solution)/shard_map/bands/pallas_call | solution.py:640
  (2 shorter events, 0.0 us)
Async XLA Ops:
  2.9 11.6 %collective-permute-start = (f32[24,128]{1,0:T(8,128)S(1)}, f32[24,128]{1,0:T(8,128)S(1)}, u32[]{:S(2)}, u32[]{:S(2)}) collective-permute-start(f32[24,128]{1,0:T(8,128)S(1)} %get-tuple-element.41.own_east), channel_id=1, source_target_pairs={{0,2},{2,4},{4,6},{6,8},{8,10},{10,12},{12,14},{14,0},{1,3},{3,5},... | collective-permute-start | bytes 36872 | tf_op jit(solution)/shard_map/ppermute | solution.py:669
  5.9 8.6 %collective-permute-start.1 = (f32[24,128]{1,0:T(8,128)S(1)}, f32[24,128]{1,0:T(8,128)S(1)}, u32[]{:S(2)}, u32[]{:S(2)}) collective-permute-start(f32[24,128]{1,0:T(8,128)S(1)} %get-tuple-element.42.own_west), channel_id=1, source_target_pairs={{2,0},{4,2},{6,4},{8,6},{10,8},{12,10},{14,12},{0,14},{3,1},{5,3},... | collective-permute-start | bytes 36872 | tf_op jit(solution)/shard_map/ppermute | solution.py:670
  9.0 5.5 %collective-permute-start.2 = (f32[8,128]{1,0:T(8,128)S(1)}, f32[8,128]{1,0:T(8,128)S(1)}, u32[]{:S(2)}, u32[]{:S(2)}) collective-permute-start(f32[8,128]{1,0:T(8,128)S(1)} %get-tuple-element.43.own_lat), channel_id=1, source_target_pairs={{0,1},{1,0},{2,3},{3,2},{4,5},{5,4},{6,7},{7,6},{8,9},{9,8},{10,11... | collective-permute-start | bytes 12296 | tf_op jit(solution)/shard_map/ppermute | solution.py:671
  14.5 26.6 %collective-permute-start.3 = (f32[128,8192]{1,0:T(8,128)}, f32[128,8192]{1,0:T(8,128)S(1)}, u32[]{:S(2)}, u32[]{:S(2)}) collective-permute-start(f32[128,8192]{1,0:T(8,128)} %get-tuple-element.68), channel_id=1, source_target_pairs={{0,1},{1,0},{2,3},{3,2},{4,5},{5,4},{6,7},{7,6},{8,9},{9,8},{10,11... | collective-permute-start | bytes 12582920 | tf_op jit(solution)/shard_map/ppermute | solution.py:687
  15.1 10.6 %slice-start = ((s8[16777216]{0:T(1024)(128)(4,1)}), s8[4194304]{0:T(1024)(128)(4,1)S(1)}, s32[]{:S(2)}) async-start(s8[16777216]{0:T(1024)(128)(4,1)} %bitcast.4), calls=%async_computation.3 | async-start | bytes 8388608
  15.1 10.6 %slice-start.1 = ((s8[16777216]{0:T(1024)(128)(4,1)}), s8[4194304]{0:T(1024)(128)(4,1)S(1)}, s32[]{:S(2)}) async-start(s8[16777216]{0:T(1024)(128)(4,1)} %bitcast.4), calls=%async_computation.4 | async-start | bytes 8388608
  15.1 10.6 %slice-start.2 = ((s8[16777216]{0:T(1024)(128)(4,1)}), s8[4194304]{0:T(1024)(128)(4,1)S(1)}, s32[]{:S(2)}) async-start(s8[16777216]{0:T(1024)(128)(4,1)} %bitcast.4), calls=%async_computation.5 | async-start | bytes 8388608
  15.1 10.6 %slice-start.3 = ((s8[16777216]{0:T(1024)(128)(4,1)}), s8[4194304]{0:T(1024)(128)(4,1)S(1)}, s32[]{:S(2)}) async-start(s8[16777216]{0:T(1024)(128)(4,1)} %bitcast.4), calls=%async_computation.6 | async-start | bytes 8388608

commit v11 on v9

--- a/solution.py
+++ b/solution.py
@@ -179,7 +179,7 @@
     return out
 
 
-def green_spread(green, coarse, load_row, acc, tables, pot):
+def green_spread(green, coarse, load_row, acc, tables, pot, more=None):
     points = green.shape[0]
     rows = coarse.shape[0]
 
@@ -201,7 +201,9 @@
     acc[...] = green_rows(green, 0, load_row)
     for index in range(1, points // LANES):
         step(index, 0)
+    beside = more() if more else None
     settle(points // LANES - 1)
+    return beside
 
 
 def next_rows(ref, start, count):
@@ -318,8 +320,8 @@
 
 
 def rim_kernel(
-    own_east, own_west, own_lat, from_west, from_east, from_lat, sums, held_sides,
-    payload, faces, lat_lines, *, points,
+    own_east, own_west, own_lat, from_west, from_east, from_lat, sums, held_sides, green_in,
+    payload, faces, lat_lines, green_out, *, points,
 ):
     lat = lax.axis_index("lat")
     half = held_sides.shape[0] // 2
@@ -497,11 +499,9 @@
 
 def last_kernel(
     first, second, green, green_north, coarse, ocean, held, faces, lat_lines, lam_sides, lam_edge,
-    lam_out, payload, put, north_line, loads, top, done, acc, tables, pot,
+    lam_out, payload, put, north_line, loads, acc, tables, pot,
     *, points, n_lon, n_lat,
 ):
-    copy = pltpu.make_async_copy(green_north, top, done)
-    copy.start()
     rows = held.shape[0]
     blocks = points // LANES
     half = rows // LANES
@@ -540,14 +540,16 @@
     put[0:1, :LANES] = put[0:1, :LANES] + slope_ratio * from_south
     put[rows - 1 : rows, :LANES] = put[rows - 1 : rows, :LANES] - slope_ratio * from_north
     north_line[...] = from_north
-    green_spread(green, coarse, lambda k: loads[k : k + 1, :], acc, tables, pot)
+    load_row = lambda k: loads[k : k + 1, :]
+    north_sums = green_spread(
+        green, coarse, load_row, acc, tables, pot, lambda: green_rows(green_north, 0, load_row)
+    )
     for start in range(0, rows, STEP_ROWS):
         at = slice(start, start + STEP_ROWS)
         lam_out[at, :] = ocean[at, :].astype(f32) * (
             held[at, :] + put[at, :LANES] - attract_coef * pot[at, :]
         )
-    copy.wait()
-    potential = sum_lanes(green_rows(top, 0, lambda k: loads[k : k + 1, :]))[0:1]
+    potential = sum_lanes(north_sums)[0:1]
     diagonal = lambda owner: shared(owner + 1 - 2 * lat, 0, 1)
     lam_n = shared(other, 0, 1)
     lane = iota((1, LANES), 1)
@@ -613,7 +615,7 @@
         copy.wait()
 
 
-def call(kernel, shapes, scratch, args, name, far=(), far_out=(), limit=16, weight=4):
+def call(kernel, shapes, scratch, args, name, far=(), far_out=(), limit=16, weight=4, aliases=None):
     vmem = pl.BlockSpec(memory_space=pltpu.VMEM)
     away = pl.BlockSpec(memory_space=pl.ANY)
     shapes = [(shape, f32) if isinstance(shape[0], int) else shape for shape in shapes]
@@ -625,6 +627,7 @@
         scratch_shapes=scratch,
         compiler_params=pltpu.CompilerParams(vmem_limit_bytes=limit << 20),
         cost_estimate=pl.CostEstimate(flops=weight << 30, bytes_accessed=16 << 20, transcendentals=0),
+        input_output_aliases=aliases or {},
         name=name,
     )(*args)
 
@@ -657,16 +660,15 @@
         [pltpu.VMEM(grid, f32), pltpu.SemaphoreType.DMA(())], (*fields, green), "inner",
         far=(7,), limit=INNER_LIMIT,
     )
-    green_top, from_west, from_east, from_lat = lax.optimization_barrier(
-        (green_top, from_west, from_east, from_lat)
+    payload, faces, lat_lines, green_top = call(
+        functools.partial(rim_kernel, points=points),
+        [(owners, 8, LANES), (7, 2 * tall, cols), (8, cols), green_top.shape], [],
+        (
+            to_east, to_west, to_lat, from_west, from_east, from_lat, sums, held_sides, green_top,
+        ),
+        "rim", far=(8,), far_out=(3,), weight=16, aliases={8: 3},
     )
     green_north = lax.ppermute(green_top, "lat", [(0, 1), (1, 0)])
-    payload, faces, lat_lines = call(
-        functools.partial(rim_kernel, points=points),
-        [(owners, 8, LANES), (7, 2 * tall, cols), (8, cols)], [],
-        (to_east, to_west, to_lat, from_west, from_east, from_lat, sums, held_sides), "rim",
-        weight=16,
-    )
     first = lax.all_to_all(payload, ("lon", "lat"), 0, 0, tiled=True)
     deep = 4 * blocks + tall
     green_scratch = [
@@ -690,15 +692,13 @@
         [grid, (rows + n_lon, cols), (rows, 2 * cols), (1, cols)],
         [
             pltpu.VMEM((owners * blocks, LANES), f32),
-            pltpu.VMEM(green_top.shape, f32),
-            pltpu.SemaphoreType.DMA(()),
         ]
         + green_scratch,
         (
             first, second, green, green_north, coarse_of, ocean, held, faces, lat_lines,
             lam_sides, lam_edge,
         ),
-        "last", far=(3,),
+        "last",
     )
     parts = lax.all_to_all(
         payload.reshape(n_lon, span + 1, 1, LANES), "lon", 0, 0, tiled=True

time: 59.4 us -> 55.2 us (0.929)
  Pallas kernels: 18.1 us -> 12.7 us
  blocking collectives: 33.7 us -> 35.2 us
    pallas_call x6, Pallas kernels: 18.1 us -> 12.7 us  [call(): pl.pallas_call(kernel, out_shape=[jax.ShapeDtypeStruct(shape, kind) for s...]
    all_to_all x1, blocking collectives: 10.3 us -> 11.8 us  [body(): first = lax.all_to_all(payload, ('lon', 'lat'), 0, 0, tiled=True)]
  transfers between devices with their start and end apart: 4 -> 4, of which waited for: 0 -> 0; matrix products, arithmetic and copies ran while one was open for 0% -> 0% of each run, Pallas kernels for 19% -> 12%
where the time goes in v11:
time: 55.2 us; the launch traced here: 55 us
  blocking collectives  35.2 us (64%)
  Pallas kernels  12.7 us (23%)
  starting transfers between devices  6.32 us (11%)
  between operations  0.74 us (1%)
    pallas_call x6, Pallas kernels, call(): pl.pallas_call(kernel, out_shape=[jax.ShapeDtypeStruct(shape, kind) for s...  12.7 us
    all_to_all x1, blocking collectives, body(): lax.all_to_all(payload.reshape(n_lon, span + 1, 1, LANES), 'lon', 0, 0, t...  12.3 us
    all_to_all x1, blocking collectives, body(): first = lax.all_to_all(payload, ('lon', 'lat'), 0, 0, tiled=True)  11.8 us
    all_to_all x1, blocking collectives, body(): lax.all_to_all(payload.reshape(owners, deep, 1, LANES), ('lon', 'lat'), 0...  11.1 us
    ppermute x1, starting transfers between devices, body(): from_east = lax.ppermute(to_west, 'lon', backward)  3.12 us
    ppermute x1, starting transfers between devices, body(): from_west = lax.ppermute(to_east, 'lon', forward)  2.58 us
  transfers between devices with their start and end apart: 4, of which 0 were waited for; matrix products, arithmetic and copies ran while one was open for 0% of the time, Pallas kernels for 12%

profile of v11, /device:TPU:0, one launch (start us, length us, event | category | flops | bytes accessed | tf_op | source)
XLA Modules:
  0.0 55.0 jit_solution(6405370112065220104)
XLA Ops:
  0.6 2.3 %pack.1 = (f32[24,128]{1,0:T(8,128)S(1)}, f32[24,128]{1,0:T(8,128)S(1)}, f32[8,128]{1,0:T(8,128)S(1)}, f32[512,128]{1,0:T(8,128)S(1)}, f32[512,128]{1,0:T(8,128)...) custom-call(f32[512,128]{1,0:T(8,128)} %refs_0_.1, ...), custom_call_target="tpu_custom_call" | custom-call | flops 4294967296 | bytes 16777216 | tf_op jit(solution)/shard_map/pack/pallas_call | solution.py:622
  2.9 0.5 collective-permute-start.2
  3.4 2.6 %collective-permute-start = (f32[24,128]{1,0:T(8,128)S(1)}, f32[24,128]{1,0:T(8,128)S(1)}, u32[]{:S(2)}, u32[]{:S(2)}) collective-permute-start(f32[24,128]{1,0:T(8,128)S(1)} %get-tuple-element.38.own_east), channel_id=1, source_target_pairs={{0,2},{2,4},{4,6},{6,8},{8,10},{10,12},{12,14},{14,0},{1,3},{3,5},... | collective-permute-start | bytes 36872 | tf_op jit(solution)/shard_map/ppermute | solution.py:652
  6.0 3.1 %collective-permute-start.1 = (f32[24,128]{1,0:T(8,128)S(1)}, f32[24,128]{1,0:T(8,128)S(1)}, u32[]{:S(2)}, u32[]{:S(2)}) collective-permute-start(f32[24,128]{1,0:T(8,128)S(1)} %get-tuple-element.39.own_west), channel_id=1, source_target_pairs={{2,0},{4,2},{6,4},{8,6},{10,8},{12,10},{14,12},{0,14},{3,1},{5,3},... | collective-permute-start | bytes 36872 | tf_op jit(solution)/shard_map/ppermute | solution.py:653
  9.1 2.8 %inner.1 = (f32[512,128]{1,0:T(8,128)S(1)}, f32[512,128]{1,0:T(8,128)S(1)}, f32[512,128]{1,0:T(8,128)S(1)}, f32[512,128]{1,0:T(8,128)S(1)}, f32[512,128]{1,0:T(8...) custom-call(f32[512,128]{1,0:T(8,128)S(1)} %get-tuple-element.41.lam, ...), custom_call_target="tpu_custom_call" | custom-call | flops 4294967296 | bytes 16777216 | tf_op jit(solution)/shard_map/inner/pallas_call | solution.py:622
  12.0 0.0 collective-permute-done.2.from_lat
  12.0 0.0 collective-permute-done.from_west
  12.0 0.0 collective-permute-done.1.from_east
  12.0 0.0 slice-start
  12.0 0.0 slice-start.1
  12.0 0.0 slice-start.2
  12.0 0.0 slice-start.3
  12.1 0.3 rim.1
  12.3 0.1 collective-permute-start.3
  12.4 11.8 %all_to_all.15.first = f32[16,8,128]{2,1,0:T(8,128)S(1)} all-to-all(f32[16,8,128]{2,1,0:T(8,128)S(1)} %get-tuple-element.51), channel_id=1, replica_groups=mesh['groups'=2,'lon'=8,'lat'=2] {'lon','lat'}, dimensions={0} | all-to-all | bytes 131072 | tf_op jit(solution)/shard_map/all_to_all | solution.py:672
  24.3 0.0 slice-done
  24.3 0.0 slice-done.1
  24.3 0.0 slice-done.2
  24.3 3.9 %second.1 = (f32[320,128]{1,0:T(8,128)S(1)}, f32[512,128]{1,0:T(8,128)S(1)}, f32[512,128]{1,0:T(8,128)S(1)}, f32[512,128]{1,0:T(8,128)S(1)}, f32[8,128]{1,0:T(8,128)S(1)}, /*index=5*/f32[1,128]{1,0:T(1,128)S(1)}) custom-call(f32[16,8,128]{2,1,0:T(8,128)S(1)} %all_to_all.15.first, f32[512,8192]{1,0:T(8,128)S(1)} %bitcast.5, ...), custom_call_target="tpu_custom_call" | custom-call | flops 4294967296 | bytes 16777216 | tf_op jit(solution)/shard_map/second/pallas_call | solution.py:622
  28.2 11.1 %all_to_all.16 = f32[16,20,1,128]{3,2,1,0:T(1,128)S(1)} all-to-all(f32[16,20,1,128]{3,2,1,0:T(1,128)S(1)} %bitcast.9), channel_id=1, replica_groups=mesh['groups'=2,'lon'=8,'lat'=2] {'lon','lat'}, dimensions={0} | all-to-all | bytes 327680 | tf_op jit(solution)/shard_map/all_to_all | solution.py:686
  39.2 0.0 collective-permute-done.3.green_north
  39.2 2.2 %last.1 = (f32[512,128]{1,0:T(8,128)S(1)}, f32[520,128]{1,0:T(8,128)S(1)}, f32[512,256]{1,0:T(8,128)S(1)}, f32[1,128]{1,0:T(1,128)S(1)}) custom-call(f32[16,8,128]{2,1,0:T(8,128)S(1)} %all_to_all.15.first, f32[320,128]{1,0:T(8,128)S(1)} %bitcast.6, f32[512,8192]{1,0:T(8,128)S(1)} %bitcast.5, f32[128,8192]{1,0:T(8,128)S(1)} %collective-permute-done.3.green_north, ...), custom_call_target="tpu_custom_call" | custom-call | flops 4294967296 | bytes 16777216 | tf_op jit(solution)/shard_map/last/pallas_call | solution.py:622
  41.5 12.3 %all_to_all.17 = f32[8,65,1,128]{3,2,1,0:T(1,128)S(1)} all-to-all(f32[8,65,1,128]{3,2,1,0:T(1,128)S(1)} %bitcast.7), channel_id=1, replica_groups=mesh['groups'=2,'lon'=8,'lat'=2] {'lon'}, dimensions={0} | all-to-all | bytes 532480 | tf_op jit(solution)/shard_map/all_to_all | solution.py:703
  53.8 1.2 %bands.1 = (f32[512,128]{1,0:T(8,128)}, f32[512,128]{1,0:T(8,128)}, f32[512,128]{1,0:T(8,128)}, f32[3,1,64,1024]{3,2,1,0:T(8,128)}) custom-call(f32[520,128]{1,0:T(8,128)S(1)} %bitcast.8, f32[512,128]{1,0:T(8,128)S(1)} %get-tuple-element.67.lam, f32[512,128]{1,0:T(8,128)S(1)} %get-tuple-element.68.adj_u, f32[512,128]{1,0:T(8,128)S(1)} %get-tuple-element.69.adj_v, ...), custom_call_target="tpu_custom_call" | custom-call | flops 4294967296 | bytes 16777216 | tf_op jit(solution)/shard_map/bands/pallas_call | solution.py:622
  (2 shorter events, 0.0 us)
Async XLA Ops:
  2.9 9.1 %collective-permute-start.2 = (f32[8,128]{1,0:T(8,128)S(1)}, f32[8,128]{1,0:T(8,128)S(1)}, u32[]{:S(2)}, u32[]{:S(2)}) collective-permute-start(f32[8,128]{1,0:T(8,128)S(1)} %get-tuple-element.40.own_lat), channel_id=1, source_target_pairs={{0,1},{1,0},{2,3},{3,2},{4,5},{5,4},{6,7},{7,6},{8,9},{9,8},{10,11... | collective-permute-start | bytes 12296 | tf_op jit(solution)/shard_map/ppermute | solution.py:654
  3.4 8.6 %collective-permute-start = (f32[24,128]{1,0:T(8,128)S(1)}, f32[24,128]{1,0:T(8,128)S(1)}, u32[]{:S(2)}, u32[]{:S(2)}) collective-permute-start(f32[24,128]{1,0:T(8,128)S(1)} %get-tuple-element.38.own_east), channel_id=1, source_target_pairs={{0,2},{2,4},{4,6},{6,8},{8,10},{10,12},{12,14},{14,0},{1,3},{3,5},... | collective-permute-start | bytes 36872 | tf_op jit(solution)/shard_map/ppermute | solution.py:652
  6.0 6.0 %collective-permute-start.1 = (f32[24,128]{1,0:T(8,128)S(1)}, f32[24,128]{1,0:T(8,128)S(1)}, u32[]{:S(2)}, u32[]{:S(2)}) collective-permute-start(f32[24,128]{1,0:T(8,128)S(1)} %get-tuple-element.39.own_west), channel_id=1, source_target_pairs={{2,0},{4,2},{6,4},{8,6},{10,8},{12,10},{14,12},{0,14},{3,1},{5,3},... | collective-permute-start | bytes 36872 | tf_op jit(solution)/shard_map/ppermute | solution.py:653
  12.0 12.2 %slice-start = ((s8[16777216]{0:T(1024)(128)(4,1)}), s8[4194304]{0:T(1024)(128)(4,1)S(1)}, s32[]{:S(2)}) async-start(s8[16777216]{0:T(1024)(128)(4,1)} %bitcast.4), calls=%async_computation.3 | async-start | bytes 8388608
  12.0 12.2 %slice-start.1 = ((s8[16777216]{0:T(1024)(128)(4,1)}), s8[4194304]{0:T(1024)(128)(4,1)S(1)}, s32[]{:S(2)}) async-start(s8[16777216]{0:T(1024)(128)(4,1)} %bitcast.4), calls=%async_computation.4 | async-start | bytes 8388608
  12.0 12.2 %slice-start.2 = ((s8[16777216]{0:T(1024)(128)(4,1)}), s8[4194304]{0:T(1024)(128)(4,1)S(1)}, s32[]{:S(2)}) async-start(s8[16777216]{0:T(1024)(128)(4,1)} %bitcast.4), calls=%async_computation.5 | async-start | bytes 8388608
  12.0 12.2 %slice-start.3 = ((s8[16777216]{0:T(1024)(128)(4,1)}), s8[4194304]{0:T(1024)(128)(4,1)S(1)}, s32[]{:S(2)}) async-start(s8[16777216]{0:T(1024)(128)(4,1)} %bitcast.4), calls=%async_computation.6 | async-start | bytes 8388608
  12.3 26.9 %collective-permute-start.3 = (f32[128,8192]{1,0:T(8,128)S(1)}, f32[128,8192]{1,0:T(8,128)S(1)}, u32[]{:S(2)}, u32[]{:S(2)}) collective-permute-start(f32[128,8192]{1,0:T(8,128)S(1)} %get-tuple-element.62), channel_id=1, source_target_pairs={{0,1},{1,0},{2,3},{3,2},{4,5},{5,4},{6,7},{7,6},{8,9},{9,8},{10,11... | collective-permute-start | bytes 12582920 | tf_op jit(solution)/shard_map/ppermute | solution.py:671

commit v12 on v11

--- a/solution.py
+++ b/solution.py
@@ -226,8 +226,8 @@
     tall = rows // LANES
     lat = lax.axis_index("lat")
     order = (
-        (LAM, 0, lam, 3), (FLUX, 1, east, 3), (None, 2, north, 0), (DEPTH, 3, depth, 3),
-        (DRAG, 4, drag, 3), (OCEAN, 5, ocean, 1), (POINT, 6, coarse, 2),
+        (LAM, 0, lam, 2), (FLUX, 1, east, 2), (None, 2, north, 0), (DEPTH, 3, depth, 2),
+        (DRAG, 4, drag, 2), (OCEAN, 5, ocean, 1), (POINT, 6, coarse, 2),
     )
     for field, index, ref, pieces in order:
         copies[index].wait()
@@ -498,10 +498,15 @@
 
 
 def last_kernel(
-    first, second, green, green_north, coarse, ocean, held, faces, lat_lines, lam_sides, lam_edge,
-    lam_out, payload, put, north_line, loads, acc, tables, pot,
+    first, second, green, green_north, coarse, ocean, held, adj_u, adj_v, faces, lat_lines,
+    lam_sides, lam_edge, lam_out, payload, east_out, north_out,
+    put, east_buf, north_buf, done, loads, acc, tables, pot,
     *, points, n_lon, n_lat,
 ):
+    copies = [
+        pltpu.make_async_copy(east_buf, east_out, done.at[0]),
+        pltpu.make_async_copy(north_buf, north_out, done.at[1]),
+    ]
     rows = held.shape[0]
     blocks = points // LANES
     half = rows // LANES
@@ -539,7 +544,11 @@
     from_south = jnp.where(lat == 1, adj_l, 0.0)
     put[0:1, :LANES] = put[0:1, :LANES] + slope_ratio * from_south
     put[rows - 1 : rows, :LANES] = put[rows - 1 : rows, :LANES] - slope_ratio * from_north
-    north_line[...] = from_north
+    east_buf[...] = adj_u[...] + put[:, LANES:]
+    north_buf[...] = adj_v[...]
+    north_buf[rows - 1 : rows, :] = adj_v[rows - 1 : rows, :] + from_north
+    for copy in copies:
+        copy.start()
     load_row = lambda k: loads[k : k + 1, :]
     north_sums = green_spread(
         green, coarse, load_row, acc, tables, pot, lambda: green_rows(green_north, 0, load_row)
@@ -570,20 +579,14 @@
             payload[start + span : start + span + 1, :] = lam_out[stop : stop + 1, :]
         else:
             payload[start + span : start + span + 1, :] = lam_north
-
-
-def bands_kernel(
-    parts, lam, adj_u, adj_v, put, north_line,
-    lam_out, east_out, north_out, bands, east, north, planes, done, *, count,
-):
+    for copy in copies:
+        copy.wait()
+
+
+def bands_kernel(parts, lam, lam_out, bands, planes, done, *, count):
     span = parts.shape[0] // count - 1
-    rows = lam.shape[0]
-    copies = [
-        pltpu.make_async_copy(lam, lam_out, done.at[0]),
-        pltpu.make_async_copy(east, east_out, done.at[1]),
-        pltpu.make_async_copy(north, north_out, done.at[2]),
-    ] + [
-        pltpu.make_async_copy(planes.at[k], bands.at[k, 0], done.at[3 + k]) for k in range(3)
+    copies = [pltpu.make_async_copy(lam, lam_out, done.at[3])] + [
+        pltpu.make_async_copy(planes.at[k], bands.at[k, 0], done.at[k]) for k in range(3)
     ]
     copies[0].start()
     lane = iota((span, LANES), 1)
@@ -592,24 +595,19 @@
     for k in range(count):
         start = k * (span + 1)
         planes[0, :, k * LANES : (k + 1) * LANES] = parts[start : start + span, :]
-    copies[3].start()
+    copies[1].start()
     for k in range(count):
         start = k * (span + 1)
         here = parts[start : start + span, :]
         north_of = jnp.where(last, 0.0, parts[start + 1 : start + 1 + span, :])
         planes[2, :, k * LANES : (k + 1) * LANES] = north_of - here
-    copies[5].start()
+    copies[3].start()
     for k in range(count):
         at = slice(k * LANES, (k + 1) * LANES)
         here = planes[0, :, at]
         after = (k + 1) % count
         there = planes[0, :, after * LANES : (after + 1) * LANES]
         planes[1, :, at] = jnp.where(lane == LANES - 1, roll_east(there), roll_east(here)) - here
-    copies[4].start()
-    east[...] = adj_u[...] + put[:, LANES:]
-    copies[1].start()
-    north[...] = adj_v[...]
-    north[rows - 1 : rows, :] = adj_v[rows - 1 : rows, :] + north_line[...]
     copies[2].start()
     for copy in copies:
         copy.wait()
@@ -687,35 +685,33 @@
         payload.reshape(owners, deep, 1, LANES), ("lon", "lat"), 0, 0, tiled=True
     ).reshape(payload.shape)
     span = rows // n_lon
-    lam, payload, put, north_line = call(
+    lam, payload, east, north = call(
         functools.partial(last_kernel, points=points, n_lon=n_lon, n_lat=n_lat),
-        [grid, (rows + n_lon, cols), (rows, 2 * cols), (1, cols)],
+        [grid, (rows + n_lon, cols), grid, grid],
         [
+            pltpu.VMEM((rows, 2 * cols), f32),
+            pltpu.VMEM(grid, f32),
+            pltpu.VMEM(grid, f32),
+            pltpu.SemaphoreType.DMA((2,)),
             pltpu.VMEM((owners * blocks, LANES), f32),
         ]
         + green_scratch,
         (
-            first, second, green, green_north, coarse_of, ocean, held, faces, lat_lines,
-            lam_sides, lam_edge,
+            first, second, green, green_north, coarse_of, ocean, held, adj_u, adj_v, faces,
+            lat_lines, lam_sides, lam_edge,
         ),
-        "last",
+        "last", far_out=(2, 3),
     )
     parts = lax.all_to_all(
         payload.reshape(n_lon, span + 1, 1, LANES), "lon", 0, 0, tiled=True
     ).reshape(payload.shape)
-    return tuple(
-        call(
-            functools.partial(bands_kernel, count=n_lon),
-            [grid, grid, grid, (3, 1, span, n_lon * cols)],
-            [
-                pltpu.VMEM(grid, f32),
-                pltpu.VMEM(grid, f32),
-                pltpu.VMEM((3, span, n_lon * cols), f32),
-                pltpu.SemaphoreType.DMA((6,)),
-            ],
-            (parts, lam, adj_u, adj_v, put, north_line), "bands", far_out=range(4),
-        )
-    )
+    lam, bands = call(
+        functools.partial(bands_kernel, count=n_lon),
+        [grid, (3, 1, span, n_lon * cols)],
+        [pltpu.VMEM((3, span, n_lon * cols), f32), pltpu.SemaphoreType.DMA((4,))],
+        (parts, lam), "bands", far_out=(0, 1),
+    )
+    return lam, east, north, bands
 
 
 def solution(mesh):

time: 55.2 us -> 55.5 us (level)
  no operation moved by 1% of the time
where the time goes in v12:
time: 55.5 us; the launch traced here: 55.3 us
  blocking collectives  35.2 us (63%)
  Pallas kernels  13 us (23%)
  starting transfers between devices  6.33 us (11%)
  between operations  0.74 us (1%)
    pallas_call x6, Pallas kernels, call(): pl.pallas_call(kernel, out_shape=[jax.ShapeDtypeStruct(shape, kind) for s...  13 us
    all_to_all x1, blocking collectives, body(): lax.all_to_all(payload.reshape(n_lon, span + 1, 1, LANES), 'lon', 0, 0, t...  12.3 us
    all_to_all x1, blocking collectives, body(): first = lax.all_to_all(payload, ('lon', 'lat'), 0, 0, tiled=True)  11.8 us
    all_to_all x1, blocking collectives, body(): lax.all_to_all(payload.reshape(owners, deep, 1, LANES), ('lon', 'lat'), 0...  11.1 us
    ppermute x1, starting transfers between devices, body(): from_east = lax.ppermute(to_west, 'lon', backward)  3.12 us
    ppermute x1, starting transfers between devices, body(): from_west = lax.ppermute(to_east, 'lon', forward)  2.58 us
  transfers between devices with their start and end apart: 4, of which 0 were waited for; matrix products, arithmetic and copies ran while one was open for 0% of the time, Pallas kernels for 12%

profile of v12, /device:TPU:0, one launch (start us, length us, event | category | flops | bytes accessed | tf_op | source)
XLA Modules:
  0.0 55.3 jit_solution(1396905854740943741)
XLA Ops:
  0.6 2.1 %pack.1 = (f32[24,128]{1,0:T(8,128)S(1)}, f32[24,128]{1,0:T(8,128)S(1)}, f32[8,128]{1,0:T(8,128)S(1)}, f32[512,128]{1,0:T(8,128)S(1)}, f32[512,128]{1,0:T(8,128)...) custom-call(f32[512,128]{1,0:T(8,128)} %refs_0_.1, ...), custom_call_target="tpu_custom_call" | custom-call | flops 4294967296 | bytes 16777216 | tf_op jit(solution)/shard_map/pack/pallas_call | solution.py:620
  2.8 0.5 collective-permute-start.2
  3.3 2.6 %collective-permute-start = (f32[24,128]{1,0:T(8,128)S(1)}, f32[24,128]{1,0:T(8,128)S(1)}, u32[]{:S(2)}, u32[]{:S(2)}) collective-permute-start(f32[24,128]{1,0:T(8,128)S(1)} %get-tuple-element.40.own_east), channel_id=1, source_target_pairs={{0,2},{2,4},{4,6},{6,8},{8,10},{10,12},{12,14},{14,0},{1,3},{3,5},... | collective-permute-start | bytes 36872 | tf_op jit(solution)/shard_map/ppermute | solution.py:650
  5.9 3.1 %collective-permute-start.1 = (f32[24,128]{1,0:T(8,128)S(1)}, f32[24,128]{1,0:T(8,128)S(1)}, u32[]{:S(2)}, u32[]{:S(2)}) collective-permute-start(f32[24,128]{1,0:T(8,128)S(1)} %get-tuple-element.41.own_west), channel_id=1, source_target_pairs={{2,0},{4,2},{6,4},{8,6},{10,8},{12,10},{14,12},{0,14},{3,1},{5,3},... | collective-permute-start | bytes 36872 | tf_op jit(solution)/shard_map/ppermute | solution.py:651
  9.0 2.8 %inner.1 = (f32[512,128]{1,0:T(8,128)S(1)}, f32[512,128]{1,0:T(8,128)S(1)}, f32[512,128]{1,0:T(8,128)S(1)}, f32[512,128]{1,0:T(8,128)S(1)}, f32[512,128]{1,0:T(8...) custom-call(f32[512,128]{1,0:T(8,128)S(1)} %get-tuple-element.43.lam, ...), custom_call_target="tpu_custom_call" | custom-call | flops 4294967296 | bytes 16777216 | tf_op jit(solution)/shard_map/inner/pallas_call | solution.py:620
  11.8 0.0 collective-permute-done.2.from_lat
  11.8 0.0 collective-permute-done.from_west
  11.9 0.0 collective-permute-done.1.from_east
  11.9 0.0 slice-start
  11.9 0.0 slice-start.1
  11.9 0.0 slice-start.2
  11.9 0.0 slice-start.3
  11.9 0.3 rim.1
  12.2 0.1 collective-permute-start.3
  12.3 11.8 %all_to_all.15.first = f32[16,8,128]{2,1,0:T(8,128)S(1)} all-to-all(f32[16,8,128]{2,1,0:T(8,128)S(1)} %get-tuple-element.53), channel_id=1, replica_groups=mesh['groups'=2,'lon'=8,'lat'=2] {'lon','lat'}, dimensions={0} | all-to-all | bytes 131072 | tf_op jit(solution)/shard_map/all_to_all | solution.py:670
  24.1 0.0 slice-done
  24.1 0.0 slice-done.1
  24.1 0.0 slice-done.2
  24.1 3.9 %second.1 = (f32[320,128]{1,0:T(8,128)S(1)}, f32[512,128]{1,0:T(8,128)S(1)}, f32[512,128]{1,0:T(8,128)S(1)}, f32[512,128]{1,0:T(8,128)S(1)}, f32[8,128]{1,0:T(8,128)S(1)}, /*index=5*/f32[1,128]{1,0:T(1,128)S(1)}) custom-call(f32[16,8,128]{2,1,0:T(8,128)S(1)} %all_to_all.15.first, f32[512,8192]{1,0:T(8,128)S(1)} %bitcast.5, ...), custom_call_target="tpu_custom_call" | custom-call | flops 4294967296 | bytes 16777216 | tf_op jit(solution)/shard_map/second/pallas_call | solution.py:620
  28.0 11.1 %all_to_all.16 = f32[16,20,1,128]{3,2,1,0:T(1,128)S(1)} all-to-all(f32[16,20,1,128]{3,2,1,0:T(1,128)S(1)} %bitcast.9), channel_id=1, replica_groups=mesh['groups'=2,'lon'=8,'lat'=2] {'lon','lat'}, dimensions={0} | all-to-all | bytes 327680 | tf_op jit(solution)/shard_map/all_to_all | solution.py:684
  39.1 0.0 collective-permute-done.3.green_north
  39.1 2.9 %last.1 = (f32[512,128]{1,0:T(8,128)S(1)}, f32[520,128]{1,0:T(8,128)S(1)}, f32[512,128]{1,0:T(8,128)}, f32[512,128]{1,0:T(8,128)}) custom-call(f32[16,8,128]{2,1,0:T(8,128)S(1)} %all_to_all.15.first, f32[320,128]{1,0:T(8,128)S(1)} %bitcast.6, f32[512,8192]{1,0:T(8,128)S(1)} %bitcast.5, f32[128,8192]{1,0:T(8,128)S(1)} %collective-permute-done.3.green_north, ...), custom_call_target="tpu_custom_call" | custom-call | flops 4294967296 | bytes 16777216 | tf_op jit(solution)/shard_map/last/pallas_call | solution.py:620
  42.0 12.3 %all_to_all.17 = f32[8,65,1,128]{3,2,1,0:T(1,128)S(1)} all-to-all(f32[8,65,1,128]{3,2,1,0:T(1,128)S(1)} %bitcast.7), channel_id=1, replica_groups=mesh['groups'=2,'lon'=8,'lat'=2] {'lon'}, dimensions={0} | all-to-all | bytes 532480 | tf_op jit(solution)/shard_map/all_to_all | solution.py:705
  54.3 1.0 %bands.1 = (f32[512,128]{1,0:T(8,128)}, f32[3,1,64,1024]{3,2,1,0:T(8,128)}) custom-call(f32[520,128]{1,0:T(8,128)S(1)} %bitcast.8, f32[512,128]{1,0:T(8,128)S(1)} %get-tuple-element.71.lam), custom_call_target="tpu_custom_call" | custom-call | flops 4294967296 | bytes 16777216 | tf_op jit(solution)/shard_map/bands/pallas_call | solution.py:620
  (2 shorter events, 0.0 us)
Async XLA Ops:
  2.8 9.1 %collective-permute-start.2 = (f32[8,128]{1,0:T(8,128)S(1)}, f32[8,128]{1,0:T(8,128)S(1)}, u32[]{:S(2)}, u32[]{:S(2)}) collective-permute-start(f32[8,128]{1,0:T(8,128)S(1)} %get-tuple-element.42.own_lat), channel_id=1, source_target_pairs={{0,1},{1,0},{2,3},{3,2},{4,5},{5,4},{6,7},{7,6},{8,9},{9,8},{10,11... | collective-permute-start | bytes 12296 | tf_op jit(solution)/shard_map/ppermute | solution.py:652
  3.3 8.6 %collective-permute-start = (f32[24,128]{1,0:T(8,128)S(1)}, f32[24,128]{1,0:T(8,128)S(1)}, u32[]{:S(2)}, u32[]{:S(2)}) collective-permute-start(f32[24,128]{1,0:T(8,128)S(1)} %get-tuple-element.40.own_east), channel_id=1, source_target_pairs={{0,2},{2,4},{4,6},{6,8},{8,10},{10,12},{12,14},{14,0},{1,3},{3,5},... | collective-permute-start | bytes 36872 | tf_op jit(solution)/shard_map/ppermute | solution.py:650
  5.9 6.0 %collective-permute-start.1 = (f32[24,128]{1,0:T(8,128)S(1)}, f32[24,128]{1,0:T(8,128)S(1)}, u32[]{:S(2)}, u32[]{:S(2)}) collective-permute-start(f32[24,128]{1,0:T(8,128)S(1)} %get-tuple-element.41.own_west), channel_id=1, source_target_pairs={{2,0},{4,2},{6,4},{8,6},{10,8},{12,10},{14,12},{0,14},{3,1},{5,3},... | collective-permute-start | bytes 36872 | tf_op jit(solution)/shard_map/ppermute | solution.py:651
  11.9 12.2 %slice-start = ((s8[16777216]{0:T(1024)(128)(4,1)}), s8[4194304]{0:T(1024)(128)(4,1)S(1)}, s32[]{:S(2)}) async-start(s8[16777216]{0:T(1024)(128)(4,1)} %bitcast.4), calls=%async_computation.3 | async-start | bytes 8388608
  11.9 12.2 %slice-start.1 = ((s8[16777216]{0:T(1024)(128)(4,1)}), s8[4194304]{0:T(1024)(128)(4,1)S(1)}, s32[]{:S(2)}) async-start(s8[16777216]{0:T(1024)(128)(4,1)} %bitcast.4), calls=%async_computation.4 | async-start | bytes 8388608
  11.9 12.2 %slice-start.2 = ((s8[16777216]{0:T(1024)(128)(4,1)}), s8[4194304]{0:T(1024)(128)(4,1)S(1)}, s32[]{:S(2)}) async-start(s8[16777216]{0:T(1024)(128)(4,1)} %bitcast.4), calls=%async_computation.5 | async-start | bytes 8388608
  11.9 12.2 %slice-start.3 = ((s8[16777216]{0:T(1024)(128)(4,1)}), s8[4194304]{0:T(1024)(128)(4,1)S(1)}, s32[]{:S(2)}) async-start(s8[16777216]{0:T(1024)(128)(4,1)} %bitcast.4), calls=%async_computation.6 | async-start | bytes 8388608
  12.2 26.9 %collective-permute-start.3 = (f32[128,8192]{1,0:T(8,128)S(1)}, f32[128,8192]{1,0:T(8,128)S(1)}, u32[]{:S(2)}, u32[]{:S(2)}) collective-permute-start(f32[128,8192]{1,0:T(8,128)S(1)} %get-tuple-element.64), channel_id=1, source_target_pairs={{0,1},{1,0},{2,3},{3,2},{4,5},{5,4},{6,7},{7,6},{8,9},{9,8},{10,11... | collective-permute-start | bytes 12582920 | tf_op jit(solution)/shard_map/ppermute | solution.py:669

commit v13 on v11

--- a/solution.py
+++ b/solution.py
@@ -226,8 +226,8 @@
     tall = rows // LANES
     lat = lax.axis_index("lat")
     order = (
-        (LAM, 0, lam, 3), (FLUX, 1, east, 3), (None, 2, north, 0), (DEPTH, 3, depth, 3),
-        (DRAG, 4, drag, 3), (OCEAN, 5, ocean, 1), (POINT, 6, coarse, 2),
+        (LAM, 0, lam, 2), (FLUX, 1, east, 2), (None, 2, north, 0), (DEPTH, 3, depth, 2),
+        (DRAG, 4, drag, 2), (OCEAN, 5, ocean, 1), (POINT, 6, coarse, 2),
     )
     for field, index, ref, pieces in order:
         copies[index].wait()
@@ -649,8 +649,8 @@
     ocean, coarse_of = fields[5:]
     forward = [(k, (k + 1) % n_lon) for k in range(n_lon)]
     backward = [(target, source) for source, target in forward]
+    from_east = lax.ppermute(to_west, "lon", backward)
     from_west = lax.ppermute(to_east, "lon", forward)
-    from_east = lax.ppermute(to_west, "lon", backward)
     from_lat = lax.ppermute(to_lat, "lat", [(0, 1), (1, 0)])
     held, gu, cu, gv, cv, sums, left, right, held_sides, green_top = call(
         functools.partial(inner_kernel, points=points),

time: 55.2 us -> 55.1 us (level)
  no operation moved by 1% of the time
where the time goes in v13:
time: 55.1 us; the launch traced here: 54.8 us
  blocking collectives  35.2 us (64%)
  Pallas kernels  12.5 us (23%)
  starting transfers between devices  6.33 us (11%)
  between operations  0.74 us (1%)
    pallas_call x6, Pallas kernels, call(): pl.pallas_call(kernel, out_shape=[jax.ShapeDtypeStruct(shape, kind) for s...  12.5 us
    all_to_all x1, blocking collectives, body(): lax.all_to_all(payload.reshape(n_lon, span + 1, 1, LANES), 'lon', 0, 0, t...  12.3 us
    all_to_all x1, blocking collectives, body(): first = lax.all_to_all(payload, ('lon', 'lat'), 0, 0, tiled=True)  11.8 us
    all_to_all x1, blocking collectives, body(): lax.all_to_all(payload.reshape(owners, deep, 1, LANES), ('lon', 'lat'), 0...  11.1 us
    ppermute x1, starting transfers between devices, body(): from_east = lax.ppermute(to_west, 'lon', backward)  3.12 us
    ppermute x1, starting transfers between devices, body(): from_west = lax.ppermute(to_east, 'lon', forward)  2.58 us
  transfers between devices with their start and end apart: 4, of which 0 were waited for; matrix products, arithmetic and copies ran while one was open for 0% of the time, Pallas kernels for 12%

profile of v13, /device:TPU:0, one launch (start us, length us, event | category | flops | bytes accessed | tf_op | source)
XLA Modules:
  0.0 54.8 jit_solution(1608945735458303455)
XLA Ops:
  0.6 2.1 %pack.1 = (f32[24,128]{1,0:T(8,128)S(1)}, f32[24,128]{1,0:T(8,128)S(1)}, f32[8,128]{1,0:T(8,128)S(1)}, f32[512,128]{1,0:T(8,128)S(1)}, f32[512,128]{1,0:T(8,128)...) custom-call(f32[512,128]{1,0:T(8,128)} %refs_0_.1, ...), custom_call_target="tpu_custom_call" | custom-call | flops 4294967296 | bytes 16777216 | tf_op jit(solution)/shard_map/pack/pallas_call | solution.py:622
  2.8 0.5 collective-permute-start.2
  3.3 2.6 %collective-permute-start = (f32[24,128]{1,0:T(8,128)S(1)}, f32[24,128]{1,0:T(8,128)S(1)}, u32[]{:S(2)}, u32[]{:S(2)}) collective-permute-start(f32[24,128]{1,0:T(8,128)S(1)} %get-tuple-element.38.own_east), channel_id=1, source_target_pairs={{0,2},{2,4},{4,6},{6,8},{8,10},{10,12},{12,14},{14,0},{1,3},{3,5},... | collective-permute-start | bytes 36872 | tf_op jit(solution)/shard_map/ppermute | solution.py:653
  5.9 3.1 %collective-permute-start.1 = (f32[24,128]{1,0:T(8,128)S(1)}, f32[24,128]{1,0:T(8,128)S(1)}, u32[]{:S(2)}, u32[]{:S(2)}) collective-permute-start(f32[24,128]{1,0:T(8,128)S(1)} %get-tuple-element.39.own_west), channel_id=1, source_target_pairs={{2,0},{4,2},{6,4},{8,6},{10,8},{12,10},{14,12},{0,14},{3,1},{5,3},... | collective-permute-start | bytes 36872 | tf_op jit(solution)/shard_map/ppermute | solution.py:652
  9.0 2.8 %inner.1 = (f32[512,128]{1,0:T(8,128)S(1)}, f32[512,128]{1,0:T(8,128)S(1)}, f32[512,128]{1,0:T(8,128)S(1)}, f32[512,128]{1,0:T(8,128)S(1)}, f32[512,128]{1,0:T(8...) custom-call(f32[512,128]{1,0:T(8,128)S(1)} %get-tuple-element.41.lam, ...), custom_call_target="tpu_custom_call" | custom-call | flops 4294967296 | bytes 16777216 | tf_op jit(solution)/shard_map/inner/pallas_call | solution.py:622
  11.8 0.0 collective-permute-done.2.from_lat
  11.8 0.0 collective-permute-done.from_west
  11.9 0.0 collective-permute-done.1.from_east
  11.9 0.0 slice-start
  11.9 0.0 slice-start.1
  11.9 0.0 slice-start.2
  11.9 0.0 slice-start.3
  11.9 0.3 rim.1
  12.2 0.1 collective-permute-start.3
  12.3 11.8 %all_to_all.15.first = f32[16,8,128]{2,1,0:T(8,128)S(1)} all-to-all(f32[16,8,128]{2,1,0:T(8,128)S(1)} %get-tuple-element.51), channel_id=1, replica_groups=mesh['groups'=2,'lon'=8,'lat'=2] {'lon','lat'}, dimensions={0} | all-to-all | bytes 131072 | tf_op jit(solution)/shard_map/all_to_all | solution.py:672
  24.1 0.0 slice-done
  24.1 0.0 slice-done.1
  24.1 0.0 slice-done.2
  24.1 3.9 %second.1 = (f32[320,128]{1,0:T(8,128)S(1)}, f32[512,128]{1,0:T(8,128)S(1)}, f32[512,128]{1,0:T(8,128)S(1)}, f32[512,128]{1,0:T(8,128)S(1)}, f32[8,128]{1,0:T(8,128)S(1)}, /*index=5*/f32[1,128]{1,0:T(1,128)S(1)}) custom-call(f32[16,8,128]{2,1,0:T(8,128)S(1)} %all_to_all.15.first, f32[512,8192]{1,0:T(8,128)S(1)} %bitcast.5, ...), custom_call_target="tpu_custom_call" | custom-call | flops 4294967296 | bytes 16777216 | tf_op jit(solution)/shard_map/second/pallas_call | solution.py:622
  28.0 11.1 %all_to_all.16 = f32[16,20,1,128]{3,2,1,0:T(1,128)S(1)} all-to-all(f32[16,20,1,128]{3,2,1,0:T(1,128)S(1)} %bitcast.9), channel_id=1, replica_groups=mesh['groups'=2,'lon'=8,'lat'=2] {'lon','lat'}, dimensions={0} | all-to-all | bytes 327680 | tf_op jit(solution)/shard_map/all_to_all | solution.py:686
  39.1 0.0 collective-permute-done.3.green_north
  39.1 2.2 %last.1 = (f32[512,128]{1,0:T(8,128)S(1)}, f32[520,128]{1,0:T(8,128)S(1)}, f32[512,256]{1,0:T(8,128)S(1)}, f32[1,128]{1,0:T(1,128)S(1)}) custom-call(f32[16,8,128]{2,1,0:T(8,128)S(1)} %all_to_all.15.first, f32[320,128]{1,0:T(8,128)S(1)} %bitcast.6, f32[512,8192]{1,0:T(8,128)S(1)} %bitcast.5, f32[128,8192]{1,0:T(8,128)S(1)} %collective-permute-done.3.green_north, ...), custom_call_target="tpu_custom_call" | custom-call | flops 4294967296 | bytes 16777216 | tf_op jit(solution)/shard_map/last/pallas_call | solution.py:622
  41.3 12.3 %all_to_all.17 = f32[8,65,1,128]{3,2,1,0:T(1,128)S(1)} all-to-all(f32[8,65,1,128]{3,2,1,0:T(1,128)S(1)} %bitcast.7), channel_id=1, replica_groups=mesh['groups'=2,'lon'=8,'lat'=2] {'lon'}, dimensions={0} | all-to-all | bytes 532480 | tf_op jit(solution)/shard_map/all_to_all | solution.py:703
  53.6 1.2 %bands.1 = (f32[512,128]{1,0:T(8,128)}, f32[512,128]{1,0:T(8,128)}, f32[512,128]{1,0:T(8,128)}, f32[3,1,64,1024]{3,2,1,0:T(8,128)}) custom-call(f32[520,128]{1,0:T(8,128)S(1)} %bitcast.8, f32[512,128]{1,0:T(8,128)S(1)} %get-tuple-element.67.lam, f32[512,128]{1,0:T(8,128)S(1)} %get-tuple-element.68.adj_u, f32[512,128]{1,0:T(8,128)S(1)} %get-tuple-element.69.adj_v, ...), custom_call_target="tpu_custom_call" | custom-call | flops 4294967296 | bytes 16777216 | tf_op jit(solution)/shard_map/bands/pallas_call | solution.py:622
  (2 shorter events, 0.0 us)
Async XLA Ops:
  2.8 9.1 %collective-permute-start.2 = (f32[8,128]{1,0:T(8,128)S(1)}, f32[8,128]{1,0:T(8,128)S(1)}, u32[]{:S(2)}, u32[]{:S(2)}) collective-permute-start(f32[8,128]{1,0:T(8,128)S(1)} %get-tuple-element.40.own_lat), channel_id=1, source_target_pairs={{0,1},{1,0},{2,3},{3,2},{4,5},{5,4},{6,7},{7,6},{8,9},{9,8},{10,11... | collective-permute-start | bytes 12296 | tf_op jit(solution)/shard_map/ppermute | solution.py:654
  3.3 8.6 %collective-permute-start = (f32[24,128]{1,0:T(8,128)S(1)}, f32[24,128]{1,0:T(8,128)S(1)}, u32[]{:S(2)}, u32[]{:S(2)}) collective-permute-start(f32[24,128]{1,0:T(8,128)S(1)} %get-tuple-element.38.own_east), channel_id=1, source_target_pairs={{0,2},{2,4},{4,6},{6,8},{8,10},{10,12},{12,14},{14,0},{1,3},{3,5},... | collective-permute-start | bytes 36872 | tf_op jit(solution)/shard_map/ppermute | solution.py:653
  5.9 6.0 %collective-permute-start.1 = (f32[24,128]{1,0:T(8,128)S(1)}, f32[24,128]{1,0:T(8,128)S(1)}, u32[]{:S(2)}, u32[]{:S(2)}) collective-permute-start(f32[24,128]{1,0:T(8,128)S(1)} %get-tuple-element.39.own_west), channel_id=1, source_target_pairs={{2,0},{4,2},{6,4},{8,6},{10,8},{12,10},{14,12},{0,14},{3,1},{5,3},... | collective-permute-start | bytes 36872 | tf_op jit(solution)/shard_map/ppermute | solution.py:652
  11.9 12.2 %slice-start = ((s8[16777216]{0:T(1024)(128)(4,1)}), s8[4194304]{0:T(1024)(128)(4,1)S(1)}, s32[]{:S(2)}) async-start(s8[16777216]{0:T(1024)(128)(4,1)} %bitcast.4), calls=%async_computation.3 | async-start | bytes 8388608
  11.9 12.2 %slice-start.1 = ((s8[16777216]{0:T(1024)(128)(4,1)}), s8[4194304]{0:T(1024)(128)(4,1)S(1)}, s32[]{:S(2)}) async-start(s8[16777216]{0:T(1024)(128)(4,1)} %bitcast.4), calls=%async_computation.4 | async-start | bytes 8388608
  11.9 12.2 %slice-start.2 = ((s8[16777216]{0:T(1024)(128)(4,1)}), s8[4194304]{0:T(1024)(128)(4,1)S(1)}, s32[]{:S(2)}) async-start(s8[16777216]{0:T(1024)(128)(4,1)} %bitcast.4), calls=%async_computation.5 | async-start | bytes 8388608
  11.9 12.2 %slice-start.3 = ((s8[16777216]{0:T(1024)(128)(4,1)}), s8[4194304]{0:T(1024)(128)(4,1)S(1)}, s32[]{:S(2)}) async-start(s8[16777216]{0:T(1024)(128)(4,1)} %bitcast.4), calls=%async_computation.6 | async-start | bytes 8388608
  12.2 26.9 %collective-permute-start.3 = (f32[128,8192]{1,0:T(8,128)S(1)}, f32[128,8192]{1,0:T(8,128)S(1)}, u32[]{:S(2)}, u32[]{:S(2)}) collective-permute-start(f32[128,8192]{1,0:T(8,128)S(1)} %get-tuple-element.62), channel_id=1, source_target_pairs={{0,1},{1,0},{2,3},{3,2},{4,5},{5,4},{6,7},{7,6},{8,9},{9,8},{10,11... | collective-permute-start | bytes 12582920 | tf_op jit(solution)/shard_map/ppermute | solution.py:671

commit v14 on v13

--- a/solution.py
+++ b/solution.py
@@ -649,9 +649,10 @@
     ocean, coarse_of = fields[5:]
     forward = [(k, (k + 1) % n_lon) for k in range(n_lon)]
     backward = [(target, source) for source, target in forward]
+    from_lat = lax.ppermute(to_lat, "lat", [(0, 1), (1, 0)])
     from_east = lax.ppermute(to_west, "lon", backward)
+    to_east, from_lat = lax.optimization_barrier((to_east, from_lat))
     from_west = lax.ppermute(to_east, "lon", forward)
-    from_lat = lax.ppermute(to_lat, "lat", [(0, 1), (1, 0)])
     held, gu, cu, gv, cv, sums, left, right, held_sides, green_top = call(
         functools.partial(inner_kernel, points=points),
         [grid] * 5

time: 55.1 us -> 56.6 us (1.027)
  waiting for transfers between devices: 0.01 us -> 3.53 us
  blocking collectives: 35.2 us -> 33.4 us
    ppermute x1, waiting for transfers between devices: 0.01 us -> 3.52 us  [body(): from_west = lax.ppermute(to_east, 'lon', forward)]
    ppermute x1, starting transfers between devices: 2.58 us -> 0.01 us  [body(): from_west = lax.ppermute(to_east, 'lon', forward)]
    ppermute x1, starting transfers between devices: 3.12 us -> 5.62 us  [body(): from_east = lax.ppermute(to_west, 'lon', backward)]
    all_to_all x1, blocking collectives: 11.8 us -> 10 us  [body(): first = lax.all_to_all(payload, ('lon', 'lat'), 0, 0, tiled=True)]
  transfers between devices with their start and end apart: 4 -> 4, of which waited for: 0 -> 1; matrix products, arithmetic and copies ran while one was open for 0% -> 0% of each run, Pallas kernels for 12% -> 12%
where the time goes in v14:
time: 56.6 us; the launch traced here: 56.3 us
  blocking collectives  33.4 us (59%)
  Pallas kernels  12.5 us (22%)
  starting transfers between devices  6.17 us (11%)
  waiting for transfers between devices  3.53 us (6%)
  between operations  0.71 us (1%)
    pallas_call x6, Pallas kernels, call(): pl.pallas_call(kernel, out_shape=[jax.ShapeDtypeStruct(shape, kind) for s...  12.5 us
    all_to_all x1, blocking collectives, body(): lax.all_to_all(payload.reshape(n_lon, span + 1, 1, LANES), 'lon', 0, 0, t...  12.3 us
    all_to_all x1, blocking collectives, body(): lax.all_to_all(payload.reshape(owners, deep, 1, LANES), ('lon', 'lat'), 0...  11.1 us
    all_to_all x1, blocking collectives, body(): first = lax.all_to_all(payload, ('lon', 'lat'), 0, 0, tiled=True)  10 us
    ppermute x1, starting transfers between devices, body(): from_east = lax.ppermute(to_west, 'lon', backward)  5.62 us
    ppermute x1, waiting for transfers between devices, body(): from_west = lax.ppermute(to_east, 'lon', forward)  3.52 us
  transfers between devices with their start and end apart: 4, of which 1 were waited for; matrix products, arithmetic and copies ran while one was open for 0% of the time, Pallas kernels for 12%

profile of v14, /device:TPU:0, one launch (start us, length us, event | category | flops | bytes accessed | tf_op | source)
XLA Modules:
  0.0 56.3 jit_solution(10429295223746612150)
XLA Ops:
  0.6 2.1 %pack.1 = (f32[24,128]{1,0:T(8,128)S(1)}, f32[24,128]{1,0:T(8,128)S(1)}, f32[8,128]{1,0:T(8,128)S(1)}, f32[512,128]{1,0:T(8,128)S(1)}, f32[512,128]{1,0:T(8,128)...) custom-call(f32[512,128]{1,0:T(8,128)} %refs_0_.1, ...), custom_call_target="tpu_custom_call" | custom-call | flops 4294967296 | bytes 16777216 | tf_op jit(solution)/shard_map/pack/pallas_call | solution.py:622
  2.8 0.5 collective-permute-start
  3.3 5.6 %collective-permute-start.2 = (f32[24,128]{1,0:T(8,128)S(1)}, f32[24,128]{1,0:T(8,128)S(1)}, u32[]{:S(2)}, u32[]{:S(2)}) collective-permute-start(f32[24,128]{1,0:T(8,128)S(1)} %get-tuple-element.43.own_west), channel_id=1, source_target_pairs={{2,0},{4,2},{6,4},{8,6},{10,8},{12,10},{14,12},{0,14},{3,1},{5,3},... | collective-permute-start | bytes 36872 | tf_op jit(solution)/shard_map/ppermute | solution.py:653
  8.9 0.0 collective-permute-done.from_lat
  8.9 0.0 collective-permute-start.1
  8.9 2.8 %inner.1 = (f32[512,128]{1,0:T(8,128)S(1)}, f32[512,128]{1,0:T(8,128)S(1)}, f32[512,128]{1,0:T(8,128)S(1)}, f32[512,128]{1,0:T(8,128)S(1)}, f32[512,128]{1,0:T(8...) custom-call(f32[512,128]{1,0:T(8,128)S(1)} %get-tuple-element.45.lam, ...), custom_call_target="tpu_custom_call" | custom-call | flops 4294967296 | bytes 16777216 | tf_op jit(solution)/shard_map/inner/pallas_call | solution.py:622
  11.8 0.0 collective-permute-done.2.from_east
  11.8 3.5 %collective-permute-done.1.from_west = f32[24,128]{1,0:T(8,128)S(1)} collective-permute-done((f32[24,128]{1,0:T(8,128)S(1)}, f32[24,128]{1,0:T(8,128)S(1)}, u32[]{:S(2)}, u32[]{:S(2)}) %collective-permute-start.1) | collective-permute-done | bytes 12320 | tf_op jit(solution)/shard_map/ppermute | solution.py:655
  15.3 0.0 slice-start
  15.3 0.0 slice-start.2
  15.3 0.0 slice-start.3
  15.3 0.3 rim.1
  15.6 0.0 collective-permute-start.3
  15.6 10.0 %all_to_all.15.first = f32[16,8,128]{2,1,0:T(8,128)S(1)} all-to-all(f32[16,8,128]{2,1,0:T(8,128)S(1)} %get-tuple-element.55), channel_id=1, replica_groups=mesh['groups'=2,'lon'=8,'lat'=2] {'lon','lat'}, dimensions={0} | all-to-all | bytes 131072 | tf_op jit(solution)/shard_map/all_to_all | solution.py:673
  25.6 0.0 slice-done
  25.6 0.0 slice-done.1
  25.6 0.0 slice-done.2
  25.6 0.0 slice-done.3
  25.6 3.9 %second.1 = (f32[320,128]{1,0:T(8,128)S(1)}, f32[512,128]{1,0:T(8,128)S(1)}, f32[512,128]{1,0:T(8,128)S(1)}, f32[512,128]{1,0:T(8,128)S(1)}, f32[8,128]{1,0:T(8,128)S(1)}, /*index=5*/f32[1,128]{1,0:T(1,128)S(1)}) custom-call(f32[16,8,128]{2,1,0:T(8,128)S(1)} %all_to_all.15.first, f32[512,8192]{1,0:T(8,128)S(1)} %bitcast.5, ...), custom_call_target="tpu_custom_call" | custom-call | flops 4294967296 | bytes 16777216 | tf_op jit(solution)/shard_map/second/pallas_call | solution.py:622
  29.5 11.1 %all_to_all.16 = f32[16,20,1,128]{3,2,1,0:T(1,128)S(1)} all-to-all(f32[16,20,1,128]{3,2,1,0:T(1,128)S(1)} %bitcast.9), channel_id=1, replica_groups=mesh['groups'=2,'lon'=8,'lat'=2] {'lon','lat'}, dimensions={0} | all-to-all | bytes 327680 | tf_op jit(solution)/shard_map/all_to_all | solution.py:687
  40.6 0.0 collective-permute-done.3.green_north
  40.6 2.2 %last.1 = (f32[512,128]{1,0:T(8,128)S(1)}, f32[520,128]{1,0:T(8,128)S(1)}, f32[512,256]{1,0:T(8,128)S(1)}, f32[1,128]{1,0:T(1,128)S(1)}) custom-call(f32[16,8,128]{2,1,0:T(8,128)S(1)} %all_to_all.15.first, f32[320,128]{1,0:T(8,128)S(1)} %bitcast.6, f32[512,8192]{1,0:T(8,128)S(1)} %bitcast.5, f32[128,8192]{1,0:T(8,128)S(1)} %collective-permute-done.3.green_north, ...), custom_call_target="tpu_custom_call" | custom-call | flops 4294967296 | bytes 16777216 | tf_op jit(solution)/shard_map/last/pallas_call | solution.py:622
  42.8 12.3 %all_to_all.17 = f32[8,65,1,128]{3,2,1,0:T(1,128)S(1)} all-to-all(f32[8,65,1,128]{3,2,1,0:T(1,128)S(1)} %bitcast.7), channel_id=1, replica_groups=mesh['groups'=2,'lon'=8,'lat'=2] {'lon'}, dimensions={0} | all-to-all | bytes 532480 | tf_op jit(solution)/shard_map/all_to_all | solution.py:704
  55.1 1.2 %bands.1 = (f32[512,128]{1,0:T(8,128)}, f32[512,128]{1,0:T(8,128)}, f32[512,128]{1,0:T(8,128)}, f32[3,1,64,1024]{3,2,1,0:T(8,128)}) custom-call(f32[520,128]{1,0:T(8,128)S(1)} %bitcast.8, f32[512,128]{1,0:T(8,128)S(1)} %get-tuple-element.71.lam, f32[512,128]{1,0:T(8,128)S(1)} %get-tuple-element.72.adj_u, f32[512,128]{1,0:T(8,128)S(1)} %get-tuple-element.73.adj_v, ...), custom_call_target="tpu_custom_call" | custom-call | flops 4294967296 | bytes 16777216 | tf_op jit(solution)/shard_map/bands/pallas_call | solution.py:622
  (2 shorter events, 0.0 us)
Async XLA Ops:
  2.8 6.1 %collective-permute-start = (f32[8,128]{1,0:T(8,128)S(1)}, f32[8,128]{1,0:T(8,128)S(1)}, u32[]{:S(2)}, u32[]{:S(2)}) collective-permute-start(f32[8,128]{1,0:T(8,128)S(1)} %get-tuple-element.41.own_lat), channel_id=1, source_target_pairs={{0,1},{1,0},{2,3},{3,2},{4,5},{5,4},{6,7},{7,6},{8,9},{9,8},{10,11... | collective-permute-start | bytes 12296 | tf_op jit(solution)/shard_map/ppermute | solution.py:652
  3.3 8.5 %collective-permute-start.2 = (f32[24,128]{1,0:T(8,128)S(1)}, f32[24,128]{1,0:T(8,128)S(1)}, u32[]{:S(2)}, u32[]{:S(2)}) collective-permute-start(f32[24,128]{1,0:T(8,128)S(1)} %get-tuple-element.43.own_west), channel_id=1, source_target_pairs={{2,0},{4,2},{6,4},{8,6},{10,8},{12,10},{14,12},{0,14},{3,1},{5,3},... | collective-permute-start | bytes 36872 | tf_op jit(solution)/shard_map/ppermute | solution.py:653
  8.9 6.4 %collective-permute-start.1 = (f32[24,128]{1,0:T(8,128)S(1)}, f32[24,128]{1,0:T(8,128)S(1)}, u32[]{:S(2)}, u32[]{:S(2)}) collective-permute-start(f32[24,128]{1,0:T(8,128)S(1)} %get-tuple-element.42.own_east), channel_id=1, source_target_pairs={{0,2},{2,4},{4,6},{6,8},{8,10},{10,12},{12,14},{14,0},{1,3},{3,5},... | collective-permute-start | bytes 36872 | tf_op jit(solution)/shard_map/ppermute | solution.py:655
  15.3 10.3 %slice-start = ((s8[16777216]{0:T(1024)(128)(4,1)}), s8[4194304]{0:T(1024)(128)(4,1)S(1)}, s32[]{:S(2)}) async-start(s8[16777216]{0:T(1024)(128)(4,1)} %bitcast.4), calls=%async_computation.3 | async-start | bytes 8388608
  15.3 10.3 %slice-start.1 = ((s8[16777216]{0:T(1024)(128)(4,1)}), s8[4194304]{0:T(1024)(128)(4,1)S(1)}, s32[]{:S(2)}) async-start(s8[16777216]{0:T(1024)(128)(4,1)} %bitcast.4), calls=%async_computation.4 | async-start | bytes 8388608
  15.3 10.3 %slice-start.2 = ((s8[16777216]{0:T(1024)(128)(4,1)}), s8[4194304]{0:T(1024)(128)(4,1)S(1)}, s32[]{:S(2)}) async-start(s8[16777216]{0:T(1024)(128)(4,1)} %bitcast.4), calls=%async_computation.5 | async-start | bytes 8388608
  15.3 10.3 %slice-start.3 = ((s8[16777216]{0:T(1024)(128)(4,1)}), s8[4194304]{0:T(1024)(128)(4,1)S(1)}, s32[]{:S(2)}) async-start(s8[16777216]{0:T(1024)(128)(4,1)} %bitcast.4), calls=%async_computation.6 | async-start | bytes 8388608
  15.6 25.0 %collective-permute-start.3 = (f32[128,8192]{1,0:T(8,128)S(1)}, f32[128,8192]{1,0:T(8,128)S(1)}, u32[]{:S(2)}, u32[]{:S(2)}) collective-permute-start(f32[128,8192]{1,0:T(8,128)S(1)} %get-tuple-element.66), channel_id=1, source_target_pairs={{0,1},{1,0},{2,3},{3,2},{4,5},{5,4},{6,7},{7,6},{8,9},{9,8},{10,11... | collective-permute-start | bytes 12582920 | tf_op jit(solution)/shard_map/ppermute | solution.py:672

commit v15 on v13

--- a/solution.py
+++ b/solution.py
@@ -190,7 +190,9 @@
             at = slice(start, start + STEP_ROWS)
             ids = local_ids(coarse[at, :], points)
             value = look_up(table, lax.bitwise_and(ids, LANES - 1))
-            pot[at, :] = jnp.where(lax.shift_right_logical(ids, 7) == index, value, pot[at, :])
+            if index > 0:
+                value = jnp.where(lax.shift_right_logical(ids, 7) == index, value, pot[at, :])
+            pot[at, :] = value
 
     def step(index, carry):
         block = green_rows(green, index * LANES, load_row)

time: 55.1 us -> 55 us (level)
  no operation moved by 1% of the time
where the time goes in v15:
time: 55 us; the launch traced here: 54.8 us
  blocking collectives  35.2 us (64%)
  Pallas kernels  12.5 us (23%)
  starting transfers between devices  6.33 us (12%)
  between operations  0.74 us (1%)
    pallas_call x6, Pallas kernels, call(): pl.pallas_call(kernel, out_shape=[jax.ShapeDtypeStruct(shape, kind) for s...  12.5 us
    all_to_all x1, blocking collectives, body(): lax.all_to_all(payload.reshape(n_lon, span + 1, 1, LANES), 'lon', 0, 0, t...  12.3 us
    all_to_all x1, blocking collectives, body(): first = lax.all_to_all(payload, ('lon', 'lat'), 0, 0, tiled=True)  11.8 us
    all_to_all x1, blocking collectives, body(): lax.all_to_all(payload.reshape(owners, deep, 1, LANES), ('lon', 'lat'), 0...  11.1 us
    ppermute x1, starting transfers between devices, body(): from_east = lax.ppermute(to_west, 'lon', backward)  3.12 us
    ppermute x1, starting transfers between devices, body(): from_west = lax.ppermute(to_east, 'lon', forward)  2.58 us
  transfers between devices with their start and end apart: 4, of which 0 were waited for; matrix products, arithmetic and copies ran while one was open for 0% of the time, Pallas kernels for 12%

profile of v15, /device:TPU:0, one launch (start us, length us, event | category | flops | bytes accessed | tf_op | source)
XLA Modules:
  0.0 54.8 jit_solution(12579137361411735987)
XLA Ops:
  0.6 2.1 %pack.1 = (f32[24,128]{1,0:T(8,128)S(1)}, f32[24,128]{1,0:T(8,128)S(1)}, f32[8,128]{1,0:T(8,128)S(1)}, f32[512,128]{1,0:T(8,128)S(1)}, f32[512,128]{1,0:T(8,128)...) custom-call(f32[512,128]{1,0:T(8,128)} %refs_0_.1, ...), custom_call_target="tpu_custom_call" | custom-call | flops 4294967296 | bytes 16777216 | tf_op jit(solution)/shard_map/pack/pallas_call | solution.py:624
  2.8 0.5 collective-permute-start.2
  3.3 2.6 %collective-permute-start = (f32[24,128]{1,0:T(8,128)S(1)}, f32[24,128]{1,0:T(8,128)S(1)}, u32[]{:S(2)}, u32[]{:S(2)}) collective-permute-start(f32[24,128]{1,0:T(8,128)S(1)} %get-tuple-element.38.own_east), channel_id=1, source_target_pairs={{0,2},{2,4},{4,6},{6,8},{8,10},{10,12},{12,14},{14,0},{1,3},{3,5},... | collective-permute-start | bytes 36872 | tf_op jit(solution)/shard_map/ppermute | solution.py:655
  5.9 3.1 %collective-permute-start.1 = (f32[24,128]{1,0:T(8,128)S(1)}, f32[24,128]{1,0:T(8,128)S(1)}, u32[]{:S(2)}, u32[]{:S(2)}) collective-permute-start(f32[24,128]{1,0:T(8,128)S(1)} %get-tuple-element.39.own_west), channel_id=1, source_target_pairs={{2,0},{4,2},{6,4},{8,6},{10,8},{12,10},{14,12},{0,14},{3,1},{5,3},... | collective-permute-start | bytes 36872 | tf_op jit(solution)/shard_map/ppermute | solution.py:654
  9.0 2.8 %inner.1 = (f32[512,128]{1,0:T(8,128)S(1)}, f32[512,128]{1,0:T(8,128)S(1)}, f32[512,128]{1,0:T(8,128)S(1)}, f32[512,128]{1,0:T(8,128)S(1)}, f32[512,128]{1,0:T(8...) custom-call(f32[512,128]{1,0:T(8,128)S(1)} %get-tuple-element.41.lam, ...), custom_call_target="tpu_custom_call" | custom-call | flops 4294967296 | bytes 16777216 | tf_op jit(solution)/shard_map/inner/pallas_call | solution.py:624
  11.8 0.0 collective-permute-done.2.from_lat
  11.8 0.0 collective-permute-done.from_west
  11.9 0.0 collective-permute-done.1.from_east
  11.9 0.0 slice-start
  11.9 0.0 slice-start.1
  11.9 0.0 slice-start.2
  11.9 0.0 slice-start.3
  11.9 0.3 rim.1
  12.2 0.1 collective-permute-start.3
  12.3 11.8 %all_to_all.15.first = f32[16,8,128]{2,1,0:T(8,128)S(1)} all-to-all(f32[16,8,128]{2,1,0:T(8,128)S(1)} %get-tuple-element.51), channel_id=1, replica_groups=mesh['groups'=2,'lon'=8,'lat'=2] {'lon','lat'}, dimensions={0} | all-to-all | bytes 131072 | tf_op jit(solution)/shard_map/all_to_all | solution.py:674
  24.1 0.0 slice-done
  24.1 0.0 slice-done.1
  24.1 0.0 slice-done.2
  24.1 3.8 %second.1 = (f32[320,128]{1,0:T(8,128)S(1)}, f32[512,128]{1,0:T(8,128)S(1)}, f32[512,128]{1,0:T(8,128)S(1)}, f32[512,128]{1,0:T(8,128)S(1)}, f32[8,128]{1,0:T(8,128)S(1)}, /*index=5*/f32[1,128]{1,0:T(1,128)S(1)}) custom-call(f32[16,8,128]{2,1,0:T(8,128)S(1)} %all_to_all.15.first, f32[512,8192]{1,0:T(8,128)S(1)} %bitcast.5, ...), custom_call_target="tpu_custom_call" | custom-call | flops 4294967296 | bytes 16777216 | tf_op jit(solution)/shard_map/second/pallas_call | solution.py:624
  28.0 11.1 %all_to_all.16 = f32[16,20,1,128]{3,2,1,0:T(1,128)S(1)} all-to-all(f32[16,20,1,128]{3,2,1,0:T(1,128)S(1)} %bitcast.9), channel_id=1, replica_groups=mesh['groups'=2,'lon'=8,'lat'=2] {'lon','lat'}, dimensions={0} | all-to-all | bytes 327680 | tf_op jit(solution)/shard_map/all_to_all | solution.py:688
  39.0 0.0 collective-permute-done.3.green_north
  39.0 2.3 %last.1 = (f32[512,128]{1,0:T(8,128)S(1)}, f32[520,128]{1,0:T(8,128)S(1)}, f32[512,256]{1,0:T(8,128)S(1)}, f32[1,128]{1,0:T(1,128)S(1)}) custom-call(f32[16,8,128]{2,1,0:T(8,128)S(1)} %all_to_all.15.first, f32[320,128]{1,0:T(8,128)S(1)} %bitcast.6, f32[512,8192]{1,0:T(8,128)S(1)} %bitcast.5, f32[128,8192]{1,0:T(8,128)S(1)} %collective-permute-done.3.green_north, ...), custom_call_target="tpu_custom_call" | custom-call | flops 4294967296 | bytes 16777216 | tf_op jit(solution)/shard_map/last/pallas_call | solution.py:624
  41.3 12.3 %all_to_all.17 = f32[8,65,1,128]{3,2,1,0:T(1,128)S(1)} all-to-all(f32[8,65,1,128]{3,2,1,0:T(1,128)S(1)} %bitcast.7), channel_id=1, replica_groups=mesh['groups'=2,'lon'=8,'lat'=2] {'lon'}, dimensions={0} | all-to-all | bytes 532480 | tf_op jit(solution)/shard_map/all_to_all | solution.py:705
  53.6 1.2 %bands.1 = (f32[512,128]{1,0:T(8,128)}, f32[512,128]{1,0:T(8,128)}, f32[512,128]{1,0:T(8,128)}, f32[3,1,64,1024]{3,2,1,0:T(8,128)}) custom-call(f32[520,128]{1,0:T(8,128)S(1)} %bitcast.8, f32[512,128]{1,0:T(8,128)S(1)} %get-tuple-element.67.lam, f32[512,128]{1,0:T(8,128)S(1)} %get-tuple-element.68.adj_u, f32[512,128]{1,0:T(8,128)S(1)} %get-tuple-element.69.adj_v, ...), custom_call_target="tpu_custom_call" | custom-call | flops 4294967296 | bytes 16777216 | tf_op jit(solution)/shard_map/bands/pallas_call | solution.py:624
  (2 shorter events, 0.0 us)
Async XLA Ops:
  2.8 9.1 %collective-permute-start.2 = (f32[8,128]{1,0:T(8,128)S(1)}, f32[8,128]{1,0:T(8,128)S(1)}, u32[]{:S(2)}, u32[]{:S(2)}) collective-permute-start(f32[8,128]{1,0:T(8,128)S(1)} %get-tuple-element.40.own_lat), channel_id=1, source_target_pairs={{0,1},{1,0},{2,3},{3,2},{4,5},{5,4},{6,7},{7,6},{8,9},{9,8},{10,11... | collective-permute-start | bytes 12296 | tf_op jit(solution)/shard_map/ppermute | solution.py:656
  3.3 8.6 %collective-permute-start = (f32[24,128]{1,0:T(8,128)S(1)}, f32[24,128]{1,0:T(8,128)S(1)}, u32[]{:S(2)}, u32[]{:S(2)}) collective-permute-start(f32[24,128]{1,0:T(8,128)S(1)} %get-tuple-element.38.own_east), channel_id=1, source_target_pairs={{0,2},{2,4},{4,6},{6,8},{8,10},{10,12},{12,14},{14,0},{1,3},{3,5},... | collective-permute-start | bytes 36872 | tf_op jit(solution)/shard_map/ppermute | solution.py:655
  5.9 6.0 %collective-permute-start.1 = (f32[24,128]{1,0:T(8,128)S(1)}, f32[24,128]{1,0:T(8,128)S(1)}, u32[]{:S(2)}, u32[]{:S(2)}) collective-permute-start(f32[24,128]{1,0:T(8,128)S(1)} %get-tuple-element.39.own_west), channel_id=1, source_target_pairs={{2,0},{4,2},{6,4},{8,6},{10,8},{12,10},{14,12},{0,14},{3,1},{5,3},... | collective-permute-start | bytes 36872 | tf_op jit(solution)/shard_map/ppermute | solution.py:654
  11.9 12.2 %slice-start = ((s8[16777216]{0:T(1024)(128)(4,1)}), s8[4194304]{0:T(1024)(128)(4,1)S(1)}, s32[]{:S(2)}) async-start(s8[16777216]{0:T(1024)(128)(4,1)} %bitcast.4), calls=%async_computation.3 | async-start | bytes 8388608
  11.9 12.2 %slice-start.1 = ((s8[16777216]{0:T(1024)(128)(4,1)}), s8[4194304]{0:T(1024)(128)(4,1)S(1)}, s32[]{:S(2)}) async-start(s8[16777216]{0:T(1024)(128)(4,1)} %bitcast.4), calls=%async_computation.4 | async-start | bytes 8388608
  11.9 12.2 %slice-start.2 = ((s8[16777216]{0:T(1024)(128)(4,1)}), s8[4194304]{0:T(1024)(128)(4,1)S(1)}, s32[]{:S(2)}) async-start(s8[16777216]{0:T(1024)(128)(4,1)} %bitcast.4), calls=%async_computation.5 | async-start | bytes 8388608
  11.9 12.2 %slice-start.3 = ((s8[16777216]{0:T(1024)(128)(4,1)}), s8[4194304]{0:T(1024)(128)(4,1)S(1)}, s32[]{:S(2)}) async-start(s8[16777216]{0:T(1024)(128)(4,1)} %bitcast.4), calls=%async_computation.6 | async-start | bytes 8388608
  12.2 26.8 %collective-permute-start.3 = (f32[128,8192]{1,0:T(8,128)S(1)}, f32[128,8192]{1,0:T(8,128)S(1)}, u32[]{:S(2)}, u32[]{:S(2)}) collective-permute-start(f32[128,8192]{1,0:T(8,128)S(1)} %get-tuple-element.62), channel_id=1, source_target_pairs={{0,1},{1,0},{2,3},{3,2},{4,5},{5,4},{6,7},{7,6},{8,9},{9,8},{10,11... | collective-permute-start | bytes 12582920 | tf_op jit(solution)/shard_map/ppermute | solution.py:673
